TPU v7x, 32 devices: a whole 2x2x4 slice. The times are simulated.
32 devices in a mesh: tile: 4 (over x, core), gz: 8 (over z, y).
Axes of the slice: x: 2, y: 2, z: 4, core: 2. Of those that a mesh axis runs over, the one named last changes fastest.
Arguments:
- planes: bfloat16 [32, 3, 512, 1024], P('gz', None, 'tile'), may hold values from -8 to 8
- level_gain: float32 [4], replicated, may hold values from 3 to 12
Outputs:
- joined: bfloat16 [3, 512, 1024], P(None, ('tile', 'gz'))
All inputs are finite; a program needn't handle non-finite values.
Results may differ from a plain program's by a relative error of at most 0.0068.
The roundings to bfloat16 on the way count: a program that leaves them out, or rounds other values in their place, can miss the bound.
Values may be sent and summed in bfloat16 or wider, within the bound.
No kernel may reach another device: no remote copies, remote signals or barrier semaphores. Data moves between devices by JAX's collectives and lax.ppermute only.
A program may use at most 192 MiB of HBM per device.

v0:
```python
import jax
import jax.numpy as jnp
from jax import lax
from jax.sharding import PartitionSpec as P

LEVELS = 4


TAPS = (0.0625, 0.25, 0.375, 0.25, 0.0625)


def extended_2(cells, sides, width):
    for axis, dim in sides:
        count = lax.axis_size(axis)
        ends = count - 1
        head = lax.slice_in_dim(cells, 0, width, axis=dim)
        tail = lax.slice_in_dim(cells, cells.shape[dim] - width, cells.shape[dim], axis=dim)
        cells = jnp.concatenate(
            [
                lax.ppermute(tail, axis, [(i, (i + 1) % count) for i in range(ends)]),
                cells,
                lax.ppermute(head, axis, [((i + 1) % count, i) for i in range(ends)]),
            ],
            axis=dim,
        )
    return cells


def combined_all(value, axis, join):
    pieces = jax.tree.map(lambda part: lax.all_gather(part, axis), value)
    head = jax.tree.map(lambda part: part[0], pieces)
    tail = jax.tree.map(lambda part: part[1:], pieces)
    total, _ = lax.scan(lambda total, share: (join(total, share), None), head, tail)
    return total


def taps_rows(field, stride):
    count = field.shape[1] - 4 * stride
    result = jnp.zeros((field.shape[0], count, field.shape[2]), jnp.float32)
    for place, factor in enumerate(TAPS):
        result = result + factor * field[:, place * stride : place * stride + count]
    return result


def smooth_cols(field, stride):
    count = field.shape[2]
    padded = jnp.pad(field, ((0, 0), (0, 0), (2 * stride, 2 * stride)))
    result = jnp.zeros_like(field)
    for place, factor in enumerate(TAPS):
        result = result + factor * padded[:, :, place * stride : place * stride + count]
    return result


def combine_states(first, second):
    top = jnp.maximum(first[0], second[0])
    scale_one = jnp.exp(first[0] - top)
    scale_two = jnp.exp(second[0] - top)
    rest = tuple(
        (left * scale_one + right * scale_two for left, right in zip(first[1:], second[1:]))
    )
    return (top,) + rest


def per_device(planes, level_gain):
    rows = planes.shape[2]
    luminance = (
        0.299 * planes[:, 0].astype(jnp.float32)
        + 0.587 * planes[:, 1].astype(jnp.float32)
        + 0.114 * planes[:, 2].astype(jnp.float32)
    ).astype(jnp.bfloat16)
    reach = 2 * (2**LEVELS - 1)
    extended = extended_2(luminance, (("tile", 1),), reach)
    approx = extended.astype(jnp.float32)
    first_row = lax.axis_index("tile") * rows - reach
    image_rows = rows * lax.axis_size("tile")
    energy = jnp.zeros(approx.shape, jnp.float32)
    offset = 0
    for level in range(LEVELS):
        stride = 2**level
        smoother = smooth_cols(taps_rows(approx, stride), stride)
        offset = offset + 2 * stride
        global_row = first_row + offset + jnp.arange(smoother.shape[1], dtype=jnp.int32)
        inside = (global_row >= 0) & (global_row < image_rows)
        smoother = jnp.where(inside[None, :, None], smoother, 0.0)
        detail = approx[:, 2 * stride : -2 * stride] - smoother
        energy = energy[:, 2 * stride : -2 * stride] + level_gain[level] * detail * detail
        approx = smoother
    local_peak = jnp.max(energy, axis=0)
    weight = jnp.exp(energy - local_peak[None])
    total = jnp.sum(weight, axis=0)
    colours = tuple(
        (jnp.sum(weight * planes[:, channel].astype(jnp.float32), axis=0) for channel in range(3))
    )
    share = rows // lax.axis_size("gz")
    merged = combined_all((local_peak, total) + colours, "gz", combine_states)
    start = lax.axis_index("gz") * share
    band_total = lax.dynamic_slice_in_dim(merged[1], start, share, 0)
    band_colour = jnp.stack(
        [lax.dynamic_slice_in_dim(merged[channel + 2], start, share, 0) for channel in range(3)]
    )
    joined = (band_colour / band_total[None]).astype(jnp.bfloat16)
    return joined


def solution(mesh):
    return jax.shard_map(
        per_device,
        mesh=mesh,
        in_specs=(P("gz", None, "tile", None), P()),
        out_specs=P(None, ("tile", "gz"), None),
        check_vma=False,
    )
```

profile of v0, /device:TPU:1, one launch (start us, length us, event | category | flops | bytes accessed | tf_op | source)
XLA Modules:
  0.0 447.8 jit_solution(13045559367690591403)
XLA Ops:
  6.5 2.6 fusion.56
  9.3 4.5 %collective-permute-start = (bf16[4,30,1024]{2,1,0:T(8,128)(2,1)S(1)}, bf16[4,30,1024]{2,1,0:T(8,128)(2,1)S(1)}, u32[]{:S(2)}, u32[]{:S(2)}) collective-permute-start(bf16[4,30,1024]{2,1,0:T(8,128)(2,1)S(1)} %get-tuple-element.106), channel_id=1, source_target_pairs={{0,8},{8,16},{16,24},{1,9},{9,17},{17,25},{2,10},{10,18},{18,26},{... | collective-permute-start | bytes 737288 | tf_op jit(solution)/shard_map/ppermute | solution.py:20
  13.8 1.9 collective-permute-start.1
  15.8 0.7 fusion.74
  16.4 0.6 collective-permute-done
  17.1 4.4 collective-permute-done.1
  21.5 0.4 maximum_convert_fusion
  21.9 0.3 slice.267
  22.2 1.7 fusion.14
  23.9 3.4 fusion.10
  27.3 0.3 slice.268
  27.6 1.3 fusion.27
  28.9 3.2 fusion.23
  32.1 1.0 fusion.72
  33.1 2.8 fusion.36
  35.9 0.5 fusion.63
  36.4 7.2 %fusion.70 = (f32[128,1024]{1,0:T(8,128)}, f32[4,128,1024]{2,1,0:T(8,128)}) fusion(f32[4,128,1024]{2,1,0:T(8,128)S(1)} %fusion.63, pred[128]{0:T(512)(128)(4,1)S(1)} %compare_and_fusion, f32[]{:T(128)} %bitcast.11, f32[4,160,1024]{2,1,0:T(8,128)S(1)} %fusion.36, f32[]{:T(128)} %bitcast.10, f32[4,160,1024]{2,1,0:T(8,128)S(1)} %get-tuple-element.104, ...), kind=kLoop, calls=%fused_computation.130 | loop fusion | flops 13500416 | bytes 13107344 | tf_op jit(solution)/shard_map/reduce_max | solution.py:88
  43.7 0.2 all-gather.13.cloned.1.call-start
  43.9 4.3 fusion.59
  48.3 0.7 all-gather.17.cloned.1.call-update
  49.0 0.5 all-gather.15.cloned.1.call-update
  49.6 0.5 all-gather.19.cloned.1.call-update
  50.1 65.7 %all-gather.11.cloned.1.call-done = f32[1024,1024]{1,0:T(8,128)} async-done(((f32[128,1024]{1,0:T(8,128)}), f32[1024,1024]{1,0:T(8,128)}) %all-gather.11.cloned.1.call-update) | async-done | bytes 4194320 | tf_op jit(solution)/shard_map/all_gather | solution.py:30
  115.8 4.3 slice.292
  120.2 69.5 %all-gather.13.cloned.1.call-done = f32[1024,1024]{1,0:T(8,128)} async-done(((f32[128,1024]{1,0:T(8,128)}), f32[1024,1024]{1,0:T(8,128)}) %all-gather.13.cloned.1.call-update) | async-done | bytes 4194320 | tf_op jit(solution)/shard_map/all_gather | solution.py:30
  189.7 4.4 slice.293
  194.1 69.4 %all-gather.17.cloned.1.call-done = f32[1024,1024]{1,0:T(8,128)} async-done(((f32[128,1024]{1,0:T(8,128)}), f32[1024,1024]{1,0:T(8,128)}) %all-gather.17.cloned.1.call-update) | async-done | bytes 4194320 | tf_op jit(solution)/shard_map/all_gather | solution.py:30
  263.5 4.4 slice.295
  267.9 69.3 %all-gather.15.cloned.1.call-done = f32[1024,1024]{1,0:T(8,128)} async-done(((f32[128,1024]{1,0:T(8,128)}), f32[1024,1024]{1,0:T(8,128)}) %all-gather.15.cloned.1.call-update) | async-done | bytes 4194320 | tf_op jit(solution)/shard_map/all_gather | solution.py:30
  337.2 4.3 slice.294
  341.5 69.4 %all-gather.19.cloned.1.call-done = f32[1024,1024]{1,0:T(8,128)} async-done(((f32[128,1024]{1,0:T(8,128)}), f32[1024,1024]{1,0:T(8,128)}) %all-gather.19.cloned.1.call-update) | async-done | bytes 4194320 | tf_op jit(solution)/shard_map/all_gather | solution.py:30
  410.9 4.5 %slice.296 = f32[896,1024]{1,0:T(8,128)} slice(f32[1024,1024]{1,0:T(8,128)} %all-gather.19.cloned.1.call-done), slice={[128:1024], [0:1024]} | slice | bytes 7340032 | tf_op jit(solution)/shard_map/slice | solution.py:32
  415.4 25.2 %while.18 = (s32[]{:T(128)}, f32[128,1024]{1,0:T(8,128)S(1)}, f32[128,1024]{1,0:T(8,128)S(1)}, f32[128,1024]{1,0:T(8,128)S(1)}, f32[128,1024]{1,0:T(8,128)S(1)},...) while((s32[]{:T(128)}, f32[128,1024]{1,0:T(8,128)S(1)}, ...), condition=%wide.region_6.7_spmd, body=%wide.region_5.6_spmd.sunk | while | flops 1966082 | bytes 9961605 | solution.py:33
  415.4 1.7 fusion.77
  417.0 1.9 fusion.78
  419.0 1.7 fusion.77
  420.6 1.9 fusion.78
  422.6 1.7 fusion.77
  424.2 1.9 fusion.78
  426.2 1.7 fusion.77
  427.8 1.9 fusion.78
  429.7 1.7 fusion.77
  431.4 1.9 fusion.78
  433.3 1.7 fusion.77
  435.0 1.9 fusion.78
  436.9 1.7 fusion.77
  438.6 1.9 fusion.78
  440.6 0.7 fusion.68
  (28 shorter events, 0.3 us)
Async XLA Ops:
  6.5 9.2 %copy-start.1 = (f32[4]{0:T(128)S(1)}, f32[4]{0:T(128)}, u32[]{:S(2)}) copy-start(f32[4]{0:T(128)} %param.5) | copy-start | bytes 52
  6.5 109.3 %all-gather.11.cloned.1.call-start = ((), (), s32[]{:S(2)}) async-start(), calls=%async_computation | async-start | bytes 4718592 | tf_op jit(solution)/shard_map/all_gather | solution.py:30
  9.3 7.8 %collective-permute-start = (bf16[4,30,1024]{2,1,0:T(8,128)(2,1)S(1)}, bf16[4,30,1024]{2,1,0:T(8,128)(2,1)S(1)}, u32[]{:S(2)}, u32[]{:S(2)}) collective-permute-start(bf16[4,30,1024]{2,1,0:T(8,128)(2,1)S(1)} %get-tuple-element.106), channel_id=1, source_target_pairs={{0,8},{8,16},{16,24},{1,9},{9,17},{17,25},{2,10},{10,18},{18,26},{... | collective-permute-start | bytes 737288 | tf_op jit(solution)/shard_map/ppermute | solution.py:20
  13.8 7.7 %collective-permute-start.1 = (bf16[4,30,1024]{2,1,0:T(8,128)(2,1)S(1)}, bf16[4,30,1024]{2,1,0:T(8,128)(2,1)S(1)}, u32[]{:S(2)}, u32[]{:S(2)}) collective-permute-start(bf16[4,30,1024]{2,1,0:T(8,128)(2,1)S(1)} %get-tuple-element.107), channel_id=1, source_target_pairs={{8,0},{16,8},{24,16},{9,1},{17,9},{25,17},{10,2},{18,10},{26,18},{... | collective-permute-start | bytes 737288 | tf_op jit(solution)/shard_map/ppermute | solution.py:22
  36.4 7.5 %copy-start = (bf16[4,3,128,1024]{3,2,1,0:T(8,128)(2,1)S(1)}, bf16[4,3,128,1024]{3,2,1,0:T(8,128)(2,1)}, u32[]{:S(2)}) copy-start(bf16[4,3,128,1024]{3,2,1,0:T(8,128)(2,1)} %param.4) | copy-start | bytes 9437188
  43.7 146.0 %all-gather.13.cloned.1.call-start = ((), (), s32[]{:S(2)}) async-start(), calls=%async_computation.1 | async-start | bytes 4718592 | tf_op jit(solution)/shard_map/all_gather | solution.py:30
  48.2 215.3 %all-gather.17.cloned.1.call-start = ((), (), s32[]{:S(2)}) async-start(), calls=%async_computation.3 | async-start | bytes 4718592 | tf_op jit(solution)/shard_map/all_gather | solution.py:30
  48.9 288.2 %all-gather.15.cloned.1.call-start = ((), (), s32[]{:S(2)}) async-start(), calls=%async_computation.2 | async-start | bytes 4718592 | tf_op jit(solution)/shard_map/all_gather | solution.py:30
  49.5 361.3 %all-gather.19.cloned.1.call-start = ((), (), s32[]{:S(2)}) async-start(), calls=%async_computation.4 | async-start | bytes 4718592 | tf_op jit(solution)/shard_map/all_gather | solution.py:30
  410.8 4.5 %slice-start = ((f32[1024,1024]{1,0:T(8,128)}), f32[128,1024]{1,0:T(8,128)S(1)}, s32[]{:S(2)}) async-start(f32[1024,1024]{1,0:T(8,128)} %all-gather.13.cloned.1.call-done), calls=%async_computation.5 | async-start | bytes 1048576 | tf_op jit(solution)/shard_map/slice | solution.py:31
  410.8 4.5 %slice-start.1 = ((f32[1024,1024]{1,0:T(8,128)}), f32[128,1024]{1,0:T(8,128)S(1)}, s32[]{:S(2)}) async-start(f32[1024,1024]{1,0:T(8,128)} %all-gather.17.cloned.1.call-done), calls=%async_computation.6 | async-start | bytes 1048576 | tf_op jit(solution)/shard_map/slice | solution.py:31
  410.8 4.5 %slice-start.2 = ((f32[1024,1024]{1,0:T(8,128)}), f32[128,1024]{1,0:T(8,128)S(1)}, s32[]{:S(2)}) async-start(f32[1024,1024]{1,0:T(8,128)} %all-gather.15.cloned.1.call-done), calls=%async_computation.7 | async-start | bytes 1048576 | tf_op jit(solution)/shard_map/slice | solution.py:31
  410.8 4.5 %slice-start.3 = ((f32[1024,1024]{1,0:T(8,128)}), f32[128,1024]{1,0:T(8,128)S(1)}, s32[]{:S(2)}) async-start(f32[1024,1024]{1,0:T(8,128)} %all-gather.19.cloned.1.call-done), calls=%async_computation.8 | async-start | bytes 1048576 | tf_op jit(solution)/shard_map/slice | solution.py:31
  410.8 4.5 %slice-start.4 = ((f32[1024,1024]{1,0:T(8,128)}), f32[128,1024]{1,0:T(8,128)S(1)}, s32[]{:S(2)}) async-start(f32[1024,1024]{1,0:T(8,128)} %all-gather.11.cloned.1.call-done), calls=%async_computation.9 | async-start | bytes 1048576 | tf_op jit(solution)/shard_map/slice | solution.py:31
Sparse Core Ops, SparseCore 0:
  43.8 72.0 all-gather.10
  118.0 71.6 all-gather.12
  191.8 71.6 all-gather.16
  265.5 71.6 all-gather.14
  339.1 71.6 all-gather.18
where the time goes:
time: 450 us; the launch traced here: 448 us
  waiting for transfers between devices  350 us (78%)
  other arithmetic  54.1 us (12%)
  local copies, waits for them, and re-layouts  23.4 us (5%)
  between operations  13.4 us (3%)
  starting transfers between devices  6.77 us (2%)
    all_gather x5, waiting for transfers between devices, combined_all(): pieces = jax.tree.map(lambda part: lax.all_gather(part, axis), value)  343 us
    add x14, other arithmetic, combine_states(): left * scale_one + right * scale_two  25 us
    slice x5, local copies, waits for them, and re-layouts, combined_all(): tail = jax.tree.map(lambda part: part[1:], pieces)  22 us
    select_n x3, other arithmetic, per_device(): smoother = jnp.where(inside[None, :, None], smoother, 0.0)  9.37 us
  transfers between devices with their start and end apart: 7, of which 7 were waited for; matrix products, arithmetic and copies ran while one was open for 5% of the time, Pallas kernels for 0%

commit v1 on v0

v1 whole, which is shorter than its diff:
```python
import functools

import jax
import jax.numpy as jnp
import numpy as np
from jax import lax
from jax.experimental import pallas as pl
from jax.experimental.pallas import tpu as pltpu
from jax.sharding import PartitionSpec as P

LEVELS = 4
TAPS = (1, 4, 6, 4, 1)
HALO = 32
SIDE = 64
LANES = 128


def band_products(count):
    made = []
    whole = np.eye(count, dtype=np.int64)
    for level in range(LEVELS):
        step = np.zeros((count, count), np.int64)
        for place, tap in enumerate(TAPS):
            step += tap * np.eye(count, k=(place - 2) * 2**level, dtype=np.int64)
        whole = step @ whole
        made.append(whole)
    return made


def split_exact(matrix):
    high = matrix.astype(jnp.bfloat16).astype(np.int64)
    return high, matrix - high


def row_matrices(image_rows, rows):
    bands = band_products(image_rows)
    tiles = []
    for tile in range(image_rows // rows):
        parts = []
        for level, band in enumerate(bands):
            window = np.pad(band, ((0, 0), (HALO, HALO)))
            window = window[tile * rows : (tile + 1) * rows, tile * rows : (tile + 1) * rows + 2 * HALO]
            high, low = split_exact(window)
            scale = 1.0 / 16 ** (level + 1)
            parts.append(high * scale)
            if level >= 2:
                parts.append(low * scale)
        tiles.append(np.concatenate(parts, axis=0))
    return np.stack(tiles).astype(jnp.bfloat16)


def column_matrices(columns):
    bands = band_products(columns)
    blocks = columns // LANES
    cases = []
    for block in (0, 1, blocks - 1):
        parts = []
        for level, band in enumerate(bands):
            window = np.pad(band.T, ((SIDE, SIDE), (0, 0)))
            window = window[block * LANES : block * LANES + LANES + 2 * SIDE, block * LANES : (block + 1) * LANES]
            high, low = split_exact(window)
            scale = 1.0 / 16 ** (level + 1)
            parts.append(high * scale)
            if level >= 2:
                parts.append(low * scale)
        cases.append(np.concatenate(parts, axis=1))
    return np.stack(cases).astype(jnp.bfloat16)


def dot(left, right):
    return jnp.dot(left, right, preferred_element_type=jnp.float32)


def luminance_of(colours):
    red, green, blue = (colours[channel].astype(jnp.float32) for channel in range(3))
    return (0.299 * red + 0.587 * green + 0.114 * blue).astype(jnp.bfloat16)


def state_kernel(tile_ref, gain_ref, planes_ref, above_ref, below_ref, row_ref, col_ref, out_ref, lum, wide, high, low):
    depth, _, rows, columns = planes_ref.shape
    blocks = columns // LANES
    padding = jnp.zeros((rows + 2 * HALO, LANES), jnp.float32)
    for plane in range(depth):
        own = luminance_of([planes_ref[plane, channel] for channel in range(3)])
        lum[plane] = own
        field = jnp.concatenate([above_ref[plane], own, below_ref[plane]], axis=0).astype(jnp.float32)
        field = jnp.concatenate([field, padding], axis=1)
        wide[plane] = pltpu.roll(field, SIDE, 1).astype(jnp.bfloat16)

    def rows_step(block, _):
        at = pl.ds(pl.multiple_of(block * LANES, LANES), LANES)
        for plane in range(depth):
            window = wide[plane, :, at]
            smooth = dot(row_ref[0], window)
            part = [smooth[k * rows : (k + 1) * rows] for k in range(6)]
            for level, value in enumerate((part[0], part[1], part[2] + part[3], part[4] + part[5])):
                top = value.astype(jnp.bfloat16)
                here = pl.ds(plane * rows, rows)
                high[level, here, at] = top
                low[level, here, at] = (value - top.astype(jnp.float32)).astype(jnp.bfloat16)
        return 0

    lax.fori_loop(0, blocks + 1, rows_step, 0)

    def columns_step(block, _):
        at = pl.ds(pl.multiple_of(block * LANES, LANES), LANES)
        window = pl.ds(pl.multiple_of(block * LANES, LANES), 2 * LANES)
        case = jnp.where(block == 0, 0, jnp.where(block == blocks - 1, 2, 1))
        approx = [lum[:, :, at].astype(jnp.float32).reshape(depth * rows, LANES)]
        for level in range(LEVELS):
            top, rest = high[level, :, window], low[level, :, window]
            if level < 2:
                taps = col_ref[case, :, level * LANES : (level + 1) * LANES]
                approx.append(dot(top, taps) + dot(rest, taps))
            else:
                first = (2 * level - 2) * LANES
                both = dot(top, col_ref[case, :, first : first + 2 * LANES])
                extra = dot(rest, col_ref[case, :, first : first + LANES])
                approx.append(both[:, :LANES] + both[:, LANES:] + extra)
        score = jnp.zeros((depth * rows, LANES), jnp.float32)
        for level in range(LEVELS):
            detail = approx[level] - approx[level + 1]
            score = score + gain_ref[level] * detail * detail
        score = score.reshape(depth, rows, LANES)
        peak = jnp.max(score, axis=0).astype(jnp.bfloat16)
        weight = jnp.exp(score - peak.astype(jnp.float32)[None])
        total = jnp.sum(weight, axis=0)
        inverse = 1.0 / total
        out_ref[0, :, at] = peak
        out_ref[1, :, at] = total.astype(jnp.bfloat16)
        for channel in range(3):
            colour = jnp.sum(weight * planes_ref[:, channel, :, at].astype(jnp.float32), axis=0)
            out_ref[2 + channel, :, at] = (colour * inverse).astype(jnp.bfloat16)
        return 0

    lax.fori_loop(0, blocks, columns_step, 0)


def local_state(planes, above, below, level_gain, tile_count):
    depth, _, rows, columns = planes.shape
    row_bands = jnp.asarray(row_matrices(rows * tile_count, rows))
    col_bands = jnp.asarray(column_matrices(columns))
    tile = lax.axis_index("tile").astype(jnp.int32).reshape(1)
    vmem = pl.BlockSpec(memory_space=pltpu.VMEM)
    wide = columns + LANES

    def whole(shape):
        return pl.BlockSpec(shape, lambda i, t: (0,) * len(shape))

    return pl.pallas_call(
        state_kernel,
        out_shape=jax.ShapeDtypeStruct((5, rows, columns), jnp.bfloat16),
        grid_spec=pltpu.PrefetchScalarGridSpec(
            num_scalar_prefetch=1,
            grid=(1,),
            in_specs=[
                pl.BlockSpec(memory_space=pltpu.SMEM),
                whole(planes.shape),
                whole(above.shape),
                whole(below.shape),
                pl.BlockSpec((1,) + row_bands.shape[1:], lambda i, t: (t[0], 0, 0)),
                whole(col_bands.shape),
            ],
            out_specs=whole((5, rows, columns)),
            scratch_shapes=[
                pltpu.VMEM((depth, rows, columns), jnp.bfloat16),
                pltpu.VMEM((depth, rows + 2 * HALO, wide), jnp.bfloat16),
                pltpu.VMEM((LEVELS, depth * rows, wide), jnp.bfloat16),
                pltpu.VMEM((LEVELS, depth * rows, wide), jnp.bfloat16),
            ],
        ),
        compiler_params=pltpu.CompilerParams(vmem_limit_bytes=56 * 2**20),
        name="local_state",
    )(tile, level_gain, planes, above, below, row_bands, col_bands)


def merge_kernel(*refs):
    *states, out_ref = refs
    peak = functools.reduce(jnp.maximum, [state[0].astype(jnp.float32) for state in states])
    total = jnp.zeros(peak.shape, jnp.float32)
    colour = [jnp.zeros(peak.shape, jnp.float32) for _ in range(3)]
    for state in states:
        weight = state[1].astype(jnp.float32) * jnp.exp(state[0].astype(jnp.float32) - peak)
        total = total + weight
        for channel in range(3):
            colour[channel] = colour[channel] + weight * state[2 + channel].astype(jnp.float32)
    for channel in range(3):
        out_ref[channel] = (colour[channel] / total).astype(jnp.bfloat16)


def merge(states):
    _, share, columns = states[0].shape
    return pl.pallas_call(
        merge_kernel,
        out_shape=jax.ShapeDtypeStruct((3, share, columns), jnp.bfloat16),
        compiler_params=pltpu.CompilerParams(vmem_limit_bytes=32 * 2**20),
        name="merge",
    )(*states)


def per_device(planes, level_gain):
    rows = planes.shape[2]
    tiles = lax.axis_size("tile")
    groups = lax.axis_size("gz")
    share = rows // groups
    head = luminance_of([planes[:, channel, :HALO] for channel in range(3)])
    tail = luminance_of([planes[:, channel, rows - HALO :] for channel in range(3)])
    above = lax.ppermute(tail, "tile", [(i, i + 1) for i in range(tiles - 1)])
    below = lax.ppermute(head, "tile", [(i + 1, i) for i in range(tiles - 1)])
    state = local_state(planes, above, below, level_gain, tiles)
    me = lax.axis_index("gz")
    states = [lax.dynamic_slice_in_dim(state, me * share, share, 1)]
    for other in range(1, groups):
        band = lax.dynamic_slice_in_dim(state, (me ^ other) * share, share, 1)
        states.append(lax.ppermute(band, "gz", [(i, i ^ other) for i in range(groups)]))
    return merge(states)


def solution(mesh):
    return jax.shard_map(
        per_device,
        mesh=mesh,
        in_specs=(P("gz", None, "tile", None), P()),
        out_specs=P(None, ("tile", "gz"), None),
        check_vma=False,
    )
```

time: 450 us -> 62.9 us (0.14)
  waiting for transfers between devices: 350 us -> 12.1 us
  other arithmetic: 54.1 us -> 1.66 us
  starting transfers between devices: 6.77 us -> 28.9 us
  local copies, waits for them, and re-layouts: 23.4 us -> 2.21 us
  Pallas kernels: 0 us -> 17.8 us
  between operations: 13.4 us -> 0.09 us
    all_gather x5 -> x0, waiting for transfers between devices: 343 us -> none  [combined_all(): pieces = jax.tree.map(lambda part: lax.all_gather(part, axis), value)]
    add x17 -> x1, other arithmetic: 28.6 us -> 1.66 us  [luminance_of(): return (0.299 * red + 0.587 * green + 0.114 * blue).astype(jnp.bfloat16)]
    slice x19 -> x0, local copies, waits for them, and re-layouts: 23.3 us -> none  [the longest x5 22 us: combined_all(): tail = jax.tree.map(lambda part: part[1:], pieces)]
    ppermute x2 -> x9, starting transfers between devices: 6.43 us -> 28.9 us  [the longest x7 22.4 us: per_device(): lax.ppermute(band, 'gz', [(i, i ^ other) for i in range(groups)])]
    pallas_call x0 -> x2, Pallas kernels: none -> 17.8 us  [the longest x1 16.8 us: local_state(): pl.pallas_call(state_kernel, out_shape=jax.ShapeDtypeStruct((5, rows, col...]
    select_n x3 -> x0, other arithmetic: 9.37 us -> none  [per_device(): smoother = jnp.where(inside[None, :, None], smoother, 0.0)]
    reduce_max x1 -> x0, other arithmetic: 7.24 us -> none  [per_device(): local_peak = jnp.max(energy, axis=0)]
    ppermute x2 -> x9, waiting for transfers between devices: 5.01 us -> 12.1 us  [the longest x7 8.81 us: per_device(): lax.ppermute(band, 'gz', [(i, i ^ other) for i in range(groups)])]
  transfers between devices with their start and end apart: 7 -> 9, of which waited for: 7 -> 5; matrix products, arithmetic and copies ran while one was open for 5% -> 0% of each run, Pallas kernels for 0% -> 0%
where the time goes in v1:
time: 62.9 us; the launch traced here: 62.7 us
  starting transfers between devices  28.9 us (46%)
  Pallas kernels  17.8 us (28%)
  waiting for transfers between devices  12.1 us (19%)
  local copies, waits for them, and re-layouts  2.21 us (4%)
  other arithmetic  1.66 us (3%)
    ppermute x7, starting transfers between devices, per_device(): lax.ppermute(band, 'gz', [(i, i ^ other) for i in range(groups)])  22.4 us
    pallas_call x1, Pallas kernels, local_state(): pl.pallas_call(state_kernel, out_shape=jax.ShapeDtypeStruct((5, rows, col...  16.8 us
    ppermute x7, waiting for transfers between devices, per_device(): lax.ppermute(band, 'gz', [(i, i ^ other) for i in range(groups)])  8.81 us
    ppermute x1, starting transfers between devices, per_device(): above = lax.ppermute(tail, 'tile', [(i, i + 1) for i in range(tiles - 1)])  4.46 us
    ppermute x1, waiting for transfers between devices, per_device(): below = lax.ppermute(head, 'tile', [(i + 1, i) for i in range(tiles - 1)])  2.07 us
    ppermute x1, starting transfers between devices, per_device(): below = lax.ppermute(head, 'tile', [(i + 1, i) for i in range(tiles - 1)])  1.97 us
    add x1, other arithmetic, luminance_of(): return (0.299 * red + 0.587 * green + 0.114 * blue).astype(jnp.bfloat16)  1.66 us
    dynamic_slice x1, local copies, waits for them, and re-layouts, per_device(): band = lax.dynamic_slice_in_dim(state, (me ^ other) * share, share, 1)  1.51 us
  transfers between devices with their start and end apart: 9, of which 5 were waited for; matrix products, arithmetic and copies ran while one was open for 0% of the time, Pallas kernels for 0%

profile of v1, /device:TPU:1, one launch (start us, length us, event | category | flops | bytes accessed | tf_op | source)
XLA Modules:
  0.0 62.7 jit_solution(11094140024985225688)
XLA Ops:
  0.0 1.7 %fusion.1 = (bf16[4,32,1024]{2,1,0:T(8,128)(2,1)S(1)}, bf16[4,32,1024]{2,1,0:T(8,128)(2,1)S(1)}) fusion(bf16[4,3,128,1024]{3,2,1,0:T(8,128)(2,1)} %planes_ref.1), kind=kLoop, calls=%fused_computation.3 | loop fusion | flops 2359296 | bytes 2097152 | tf_op jit(solution)/shard_map/add | solution.py:76
  1.7 2.0 %collective-permute-start.1 = (bf16[4,32,1024]{2,1,0:T(8,128)(2,1)S(1)}, bf16[4,32,1024]{2,1,0:T(8,128)(2,1)S(1)}, u32[]{:S(2)}, u32[]{:S(2)}) collective-permute-start(bf16[4,32,1024]{2,1,0:T(8,128)(2,1)S(1)} %get-tuple-element.5), channel_id=1, source_target_pairs={{8,0},{16,8},{24,16},{9,1},{17,9},{25,17},{10,2},{18,10},{26,18},{... | collective-permute-start | bytes 786440 | tf_op jit(solution)/shard_map/ppermute | solution.py:209
  3.6 4.5 %collective-permute-start = (bf16[4,32,1024]{2,1,0:T(8,128)(2,1)S(1)}, bf16[4,32,1024]{2,1,0:T(8,128)(2,1)S(1)}, u32[]{:S(2)}, u32[]{:S(2)}) collective-permute-start(bf16[4,32,1024]{2,1,0:T(8,128)(2,1)S(1)} %get-tuple-element.6), channel_id=1, source_target_pairs={{0,8},{8,16},{16,24},{1,9},{9,17},{17,25},{2,10},{10,18},{18,26},{... | collective-permute-start | bytes 786440 | tf_op jit(solution)/shard_map/ppermute | solution.py:208
  8.2 2.1 %collective-permute-done.1.below_ref = bf16[4,32,1024]{2,1,0:T(8,128)(2,1)S(1)} collective-permute-done((bf16[4,32,1024]{2,1,0:T(8,128)(2,1)S(1)}, bf16[4,32,1024]{2,1,0:T(8,128)(2,1)S(1)}, u32[]{:S(2)}, u32[]{:S(2)}) %collective-permute-start.1) | collective-permute-done | bytes 262176 | tf_op jit(solution)/shard_map/ppermute | solution.py:209
  10.2 0.0 copy-start
  10.2 1.2 %collective-permute-done.above_ref = bf16[4,32,1024]{2,1,0:T(8,128)(2,1)S(1)} collective-permute-done((bf16[4,32,1024]{2,1,0:T(8,128)(2,1)S(1)}, bf16[4,32,1024]{2,1,0:T(8,128)(2,1)S(1)}, u32[]{:S(2)}, u32[]{:S(2)}) %collective-permute-start) | collective-permute-done | bytes 262176 | tf_op jit(solution)/shard_map/ppermute | solution.py:208
  11.4 0.0 copy-start.1
  11.4 0.0 copy-done
  11.4 0.7 %copy-done.1 = bf16[4,32,1024]{2,1,0:T(8,128)(2,1)} copy-done((bf16[4,32,1024]{2,1,0:T(8,128)(2,1)}, bf16[4,32,1024]{2,1,0:T(8,128)(2,1)S(1)}, u32[]{:S(2)}) %copy-start.1) | copy-done | bytes 262168
  12.1 16.8 %local_state.1 = bf16[5,128,1024]{2,1,0:T(8,128)(2,1)} custom-call(s32[1]{0:T(128)} %bitcast.tile_ref, f32[4]{0:T(128)} %gain_ref.1, bf16[4,3,128,1024]{3,2,1,0:T(8,128)(2,1)} %planes_ref.1, bf16[4,32,1024]{2,1,0:T(8,128)(2,1)} %copy-done.1, bf16[4,32,1024]{2,1,0:T(8,128)(2,1)} %copy-done, bf16[4,768,192]{2,1,0:T(8,128)(2,1)} %constant.38.clone.row_ref, ...), custom_call_target="tpu_custom_call" | custom-call | tf_op jit(solution)/shard_map/local_state/pallas_call | solution.py:150
  28.9 1.5 %constant_dynamic-slice_fusion = (bf16[5,16,1024]{2,1,0:T(8,128)(2,1)S(1)}, bf16[5,16,1024]{2,1,0:T(8,128)(2,1)S(1)}, bf16[5,16,1024]{2,1,0:T(8,128)(2,1)S(1)}, ...) fusion(bf16[5,128,1024]{2,1,0:T(8,128)(2,1)} %local_state.1, ...), kind=kLoop, calls=%fused_computation.4 | loop fusion | bytes 2621472 | tf_op jit(solution)/shard_map/dynamic_slice | solution.py:214
  30.4 4.3 %collective-permute-start.8 = (bf16[5,16,1024]{2,1,0:T(8,128)(2,1)S(1)}, bf16[5,16,1024]{2,1,0:T(8,128)(2,1)S(1)}, u32[]{:S(2)}, u32[]{:S(2)}) collective-permute-start(bf16[5,16,1024]{2,1,0:T(8,128)(2,1)S(1)} %get-tuple-element.7), channel_id=1, source_target_pairs={{0,7},{1,6},{2,5},{3,4},{4,3},{5,2},{6,1},{7,0},{8,15},{9,14},{10,... | collective-permute-start | bytes 491528 | tf_op jit(solution)/shard_map/ppermute | solution.py:215
  34.8 0.0 collective-permute-start.7
  34.8 0.4 collective-permute-start.6
  35.2 2.0 %collective-permute-start.5 = (bf16[5,16,1024]{2,1,0:T(8,128)(2,1)S(1)}, bf16[5,16,1024]{2,1,0:T(8,128)(2,1)S(1)}, u32[]{:S(2)}, u32[]{:S(2)}) collective-permute-start(bf16[5,16,1024]{2,1,0:T(8,128)(2,1)S(1)} %get-tuple-element.10), channel_id=1, source_target_pairs={{0,4},{1,5},{2,6},{3,7},{4,0},{5,1},{6,2},{7,3},{8,12},{9,13},{10,... | collective-permute-start | bytes 491528 | tf_op jit(solution)/shard_map/ppermute | solution.py:215
  37.2 2.0 %collective-permute-start.4 = (bf16[5,16,1024]{2,1,0:T(8,128)(2,1)S(1)}, bf16[5,16,1024]{2,1,0:T(8,128)(2,1)S(1)}, u32[]{:S(2)}, u32[]{:S(2)}) collective-permute-start(bf16[5,16,1024]{2,1,0:T(8,128)(2,1)S(1)} %get-tuple-element.11), channel_id=1, source_target_pairs={{0,3},{1,2},{2,1},{3,0},{4,7},{5,6},{6,5},{7,4},{8,11},{9,10},{10,... | collective-permute-start | bytes 491528 | tf_op jit(solution)/shard_map/ppermute | solution.py:215
  39.2 0.0 collective-permute-done.8.refs_7_
  39.2 12.7 %collective-permute-start.3 = (bf16[5,16,1024]{2,1,0:T(8,128)(2,1)S(1)}, bf16[5,16,1024]{2,1,0:T(8,128)(2,1)S(1)}, u32[]{:S(2)}, u32[]{:S(2)}) collective-permute-start(bf16[5,16,1024]{2,1,0:T(8,128)(2,1)S(1)} %get-tuple-element.12), channel_id=1, source_target_pairs={{0,2},{1,3},{2,0},{3,1},{4,6},{5,7},{6,4},{7,5},{8,10},{9,11},{10,... | collective-permute-start | bytes 491528 | tf_op jit(solution)/shard_map/ppermute | solution.py:215
  51.9 0.0 collective-permute-done.7.refs_6_
  51.9 1.0 %collective-permute-start.2 = (bf16[5,16,1024]{2,1,0:T(8,128)(2,1)S(1)}, bf16[5,16,1024]{2,1,0:T(8,128)(2,1)S(1)}, u32[]{:S(2)}, u32[]{:S(2)}) collective-permute-start(bf16[5,16,1024]{2,1,0:T(8,128)(2,1)S(1)} %get-tuple-element.13), channel_id=1, source_target_pairs={{0,1},{1,0},{2,3},{3,2},{4,5},{5,4},{6,7},{7,6},{8,9},{9,8},{10,11... | collective-permute-start | bytes 491528 | tf_op jit(solution)/shard_map/ppermute | solution.py:215
  52.9 5.1 %collective-permute-done.6.refs_5_ = bf16[5,16,1024]{2,1,0:T(8,128)(2,1)S(1)} collective-permute-done((bf16[5,16,1024]{2,1,0:T(8,128)(2,1)S(1)}, bf16[5,16,1024]{2,1,0:T(8,128)(2,1)S(1)}, u32[]{:S(2)}, u32[]{:S(2)}) %collective-permute-start.6) | collective-permute-done | bytes 163872 | tf_op jit(solution)/shard_map/ppermute | solution.py:215
  58.0 2.8 %collective-permute-done.5.refs_4_ = bf16[5,16,1024]{2,1,0:T(8,128)(2,1)S(1)} collective-permute-done((bf16[5,16,1024]{2,1,0:T(8,128)(2,1)S(1)}, bf16[5,16,1024]{2,1,0:T(8,128)(2,1)S(1)}, u32[]{:S(2)}, u32[]{:S(2)}) %collective-permute-start.5) | collective-permute-done | bytes 163872 | tf_op jit(solution)/shard_map/ppermute | solution.py:215
  60.8 0.0 collective-permute-done.4.refs_3_
  60.8 0.9 %collective-permute-done.3.refs_2_ = bf16[5,16,1024]{2,1,0:T(8,128)(2,1)S(1)} collective-permute-done((bf16[5,16,1024]{2,1,0:T(8,128)(2,1)S(1)}, bf16[5,16,1024]{2,1,0:T(8,128)(2,1)S(1)}, u32[]{:S(2)}, u32[]{:S(2)}) %collective-permute-start.3) | collective-permute-done | bytes 163872 | tf_op jit(solution)/shard_map/ppermute | solution.py:215
  61.7 0.0 collective-permute-done.2.refs_1_
  61.7 1.0 %merge.1 = bf16[3,16,1024]{2,1,0:T(8,128)(2,1)} custom-call(bf16[5,16,1024]{2,1,0:T(8,128)(2,1)S(1)} %get-tuple-element.14.refs_0_, bf16[5,16,1024]{2,1,0:T(8,128)(2,1)S(1)} %collective-permute-done.2.refs_1_, bf16[5,16,1024]{2,1,0:T(8,128)(2,1)S(1)} %collective-permute-done.3.refs_2_, bf16[5,16,1024]{2,1,0:T(8,128)(2,1)S(1)} %collective-permute-done.4.refs_3_, ...), custom_call_target="tpu_custom_call" | custom-call | tf_op jit(solution)/shard_map/merge/pallas_call | solution.py:193
Async XLA Ops:
  1.7 8.6 %collective-permute-start.1 = (bf16[4,32,1024]{2,1,0:T(8,128)(2,1)S(1)}, bf16[4,32,1024]{2,1,0:T(8,128)(2,1)S(1)}, u32[]{:S(2)}, u32[]{:S(2)}) collective-permute-start(bf16[4,32,1024]{2,1,0:T(8,128)(2,1)S(1)} %get-tuple-element.5), channel_id=1, source_target_pairs={{8,0},{16,8},{24,16},{9,1},{17,9},{25,17},{10,2},{18,10},{26,18},{... | collective-permute-start | bytes 786440 | tf_op jit(solution)/shard_map/ppermute | solution.py:209
  3.6 7.8 %collective-permute-start = (bf16[4,32,1024]{2,1,0:T(8,128)(2,1)S(1)}, bf16[4,32,1024]{2,1,0:T(8,128)(2,1)S(1)}, u32[]{:S(2)}, u32[]{:S(2)}) collective-permute-start(bf16[4,32,1024]{2,1,0:T(8,128)(2,1)S(1)} %get-tuple-element.6), channel_id=1, source_target_pairs={{0,8},{8,16},{16,24},{1,9},{9,17},{17,25},{2,10},{10,18},{18,26},{... | collective-permute-start | bytes 786440 | tf_op jit(solution)/shard_map/ppermute | solution.py:208
  10.2 1.2 %copy-start = (bf16[4,32,1024]{2,1,0:T(8,128)(2,1)}, bf16[4,32,1024]{2,1,0:T(8,128)(2,1)S(1)}, u32[]{:S(2)}) copy-start(bf16[4,32,1024]{2,1,0:T(8,128)(2,1)S(1)} %collective-permute-done.1.below_ref) | copy-start | bytes 786436
  11.4 0.7 %copy-start.1 = (bf16[4,32,1024]{2,1,0:T(8,128)(2,1)}, bf16[4,32,1024]{2,1,0:T(8,128)(2,1)S(1)}, u32[]{:S(2)}) copy-start(bf16[4,32,1024]{2,1,0:T(8,128)(2,1)S(1)} %collective-permute-done.above_ref) | copy-start | bytes 786436
  30.4 8.8 %collective-permute-start.8 = (bf16[5,16,1024]{2,1,0:T(8,128)(2,1)S(1)}, bf16[5,16,1024]{2,1,0:T(8,128)(2,1)S(1)}, u32[]{:S(2)}, u32[]{:S(2)}) collective-permute-start(bf16[5,16,1024]{2,1,0:T(8,128)(2,1)S(1)} %get-tuple-element.7), channel_id=1, source_target_pairs={{0,7},{1,6},{2,5},{3,4},{4,3},{5,2},{6,1},{7,0},{8,15},{9,14},{10,... | collective-permute-start | bytes 491528 | tf_op jit(solution)/shard_map/ppermute | solution.py:215
  34.8 17.1 %collective-permute-start.7 = (bf16[5,16,1024]{2,1,0:T(8,128)(2,1)S(1)}, bf16[5,16,1024]{2,1,0:T(8,128)(2,1)S(1)}, u32[]{:S(2)}, u32[]{:S(2)}) collective-permute-start(bf16[5,16,1024]{2,1,0:T(8,128)(2,1)S(1)} %get-tuple-element.8), channel_id=1, source_target_pairs={{0,6},{1,7},{2,4},{3,5},{4,2},{5,3},{6,0},{7,1},{8,14},{9,15},{10,... | collective-permute-start | bytes 491528 | tf_op jit(solution)/shard_map/ppermute | solution.py:215
  34.8 23.2 %collective-permute-start.6 = (bf16[5,16,1024]{2,1,0:T(8,128)(2,1)S(1)}, bf16[5,16,1024]{2,1,0:T(8,128)(2,1)S(1)}, u32[]{:S(2)}, u32[]{:S(2)}) collective-permute-start(bf16[5,16,1024]{2,1,0:T(8,128)(2,1)S(1)} %get-tuple-element.9), channel_id=1, source_target_pairs={{0,5},{1,4},{2,7},{3,6},{4,1},{5,0},{6,3},{7,2},{8,13},{9,12},{10,... | collective-permute-start | bytes 491528 | tf_op jit(solution)/shard_map/ppermute | solution.py:215
  35.2 25.6 %collective-permute-start.5 = (bf16[5,16,1024]{2,1,0:T(8,128)(2,1)S(1)}, bf16[5,16,1024]{2,1,0:T(8,128)(2,1)S(1)}, u32[]{:S(2)}, u32[]{:S(2)}) collective-permute-start(bf16[5,16,1024]{2,1,0:T(8,128)(2,1)S(1)} %get-tuple-element.10), channel_id=1, source_target_pairs={{0,4},{1,5},{2,6},{3,7},{4,0},{5,1},{6,2},{7,3},{8,12},{9,13},{10,... | collective-permute-start | bytes 491528 | tf_op jit(solution)/shard_map/ppermute | solution.py:215
  37.2 23.6 %collective-permute-start.4 = (bf16[5,16,1024]{2,1,0:T(8,128)(2,1)S(1)}, bf16[5,16,1024]{2,1,0:T(8,128)(2,1)S(1)}, u32[]{:S(2)}, u32[]{:S(2)}) collective-permute-start(bf16[5,16,1024]{2,1,0:T(8,128)(2,1)S(1)} %get-tuple-element.11), channel_id=1, source_target_pairs={{0,3},{1,2},{2,1},{3,0},{4,7},{5,6},{6,5},{7,4},{8,11},{9,10},{10,... | collective-permute-start | bytes 491528 | tf_op jit(solution)/shard_map/ppermute | solution.py:215
  39.2 22.5 %collective-permute-start.3 = (bf16[5,16,1024]{2,1,0:T(8,128)(2,1)S(1)}, bf16[5,16,1024]{2,1,0:T(8,128)(2,1)S(1)}, u32[]{:S(2)}, u32[]{:S(2)}) collective-permute-start(bf16[5,16,1024]{2,1,0:T(8,128)(2,1)S(1)} %get-tuple-element.12), channel_id=1, source_target_pairs={{0,2},{1,3},{2,0},{3,1},{4,6},{5,7},{6,4},{7,5},{8,10},{9,11},{10,... | collective-permute-start | bytes 491528 | tf_op jit(solution)/shard_map/ppermute | solution.py:215
  51.9 9.8 %collective-permute-start.2 = (bf16[5,16,1024]{2,1,0:T(8,128)(2,1)S(1)}, bf16[5,16,1024]{2,1,0:T(8,128)(2,1)S(1)}, u32[]{:S(2)}, u32[]{:S(2)}) collective-permute-start(bf16[5,16,1024]{2,1,0:T(8,128)(2,1)S(1)} %get-tuple-element.13), channel_id=1, source_target_pairs={{0,1},{1,0},{2,3},{3,2},{4,5},{5,4},{6,7},{7,6},{8,9},{9,8},{10,11... | collective-permute-start | bytes 491528 | tf_op jit(solution)/shard_map/ppermute | solution.py:215

commit v2 on v1

v2 whole, which is shorter than its diff:
```python
import functools

import jax
import jax.numpy as jnp
import numpy as np
from jax import lax
from jax.experimental import pallas as pl
from jax.experimental.pallas import tpu as pltpu
from jax.sharding import PartitionSpec as P

LEVELS = 4
TAPS = (1, 4, 6, 4, 1)
HALO = 32
SIDE = 64
LANES = 128


def band_products(count):
    made = []
    whole = np.eye(count)
    for level in range(LEVELS):
        step = sum(tap * np.eye(count, k=(place - 2) * 2**level) for place, tap in enumerate(TAPS))
        whole = step @ whole
        made.append(whole)
    return made


def split_exact(matrix):
    high = matrix.astype(jnp.bfloat16).astype(matrix.dtype)
    return high, matrix - high


def row_matrices(image_rows, rows):
    bands = band_products(image_rows)
    tiles = []
    for tile in (0, 1, image_rows // rows - 1):
        parts = []
        for level, band in enumerate(bands):
            window = np.pad(band, ((0, 0), (HALO, HALO)))
            window = window[tile * rows : (tile + 1) * rows, tile * rows : (tile + 1) * rows + 2 * HALO]
            high, low = split_exact(window)
            scale = 1.0 / 16 ** (level + 1)
            parts.append(high * scale)
            if level >= 2:
                parts.append(low * scale)
        tiles.append(np.concatenate(parts, axis=0))
    return np.stack(tiles).astype(jnp.bfloat16)


def column_matrices(columns):
    bands = band_products(columns)
    blocks = columns // LANES
    cases = []
    for block in (0, 1, blocks - 1):
        parts = []
        for level, band in enumerate(bands):
            window = np.pad(band.T, ((SIDE, SIDE), (0, 0)))
            window = window[block * LANES : block * LANES + LANES + 2 * SIDE, block * LANES : (block + 1) * LANES]
            high, low = split_exact(window)
            scale = 1.0 / 16 ** (level + 1)
            parts.append(high * scale)
            if level >= 2:
                parts.append(low * scale)
        cases.append(np.concatenate(parts, axis=1))
    return np.stack(cases).astype(jnp.bfloat16)


def dot(left, right):
    return jnp.dot(left, right, preferred_element_type=jnp.float32)


def luminance_of(colours):
    red, green, blue = (colours[channel].astype(jnp.float32) for channel in range(3))
    return (0.299 * red + 0.587 * green + 0.114 * blue).astype(jnp.bfloat16)


def combine(states):
    states = [[part.astype(jnp.float32) for part in state] for state in states]
    peak = functools.reduce(jnp.maximum, [state[0] for state in states])
    weights = [state[1] * jnp.exp(state[0] - peak) for state in states]
    total = sum(weights[1:], weights[0])
    inverse = 1.0 / total
    colours = []
    for channel in range(2, 5):
        terms = [weight * state[channel] for weight, state in zip(weights, states)]
        colours.append(sum(terms[1:], terms[0]) * inverse)
    return [peak, total] + colours


def state_kernel(slow, gain_ref, planes_ref, above_ref, below_ref, row_ref, col_ref, *refs):
    *outs, lum, wide, high, low, held = refs
    depth, _, rows, columns = planes_ref.shape
    groups, _, share, _ = held.shape
    fast = groups // slow
    split = outs[0].shape[-1]
    blocks = columns // LANES
    tile, tiles = lax.axis_index("tile"), lax.axis_size("tile")
    tile_case = jnp.where(tile == 0, 0, jnp.where(tile == tiles - 1, 2, 1))
    padding = jnp.zeros((rows + 2 * HALO, LANES), jnp.float32)
    for plane in range(depth):
        own = luminance_of([planes_ref[plane, channel] for channel in range(3)])
        lum[plane] = own
        field = jnp.concatenate([above_ref[plane], own, below_ref[plane]], axis=0).astype(jnp.float32)
        field = jnp.concatenate([field, padding], axis=1)
        wide[plane] = pltpu.roll(field, SIDE, 1).astype(jnp.bfloat16)

    for start in range(0, columns + LANES, 2 * LANES):
        at = pl.ds(start, min(2 * LANES, columns + LANES - start))
        for plane in range(depth):
            here = pl.ds(plane * rows, rows)
            smooth = dot(row_ref[tile_case], wide[plane, :, at])
            part = [smooth[k * rows : (k + 1) * rows] for k in range(6)]
            for level, value in enumerate((part[0], part[1], part[2] + part[3], part[4] + part[5])):
                top = value.astype(jnp.bfloat16)
                high[level, here, at] = top
                low[level, here, at] = (value - top.astype(jnp.float32)).astype(jnp.bfloat16)

    for block in range(blocks):
        at = pl.ds(block * LANES, LANES)
        window = pl.ds(block * LANES, 2 * LANES)
        case = 0 if block == 0 else 2 if block == blocks - 1 else 1
        approx = [lum[:, :, at].astype(jnp.float32).reshape(depth * rows, LANES)]
        for level in range(LEVELS):
            top, rest = high[level, :, window], low[level, :, window]
            if level < 2:
                taps = col_ref[case, :, level * LANES : (level + 1) * LANES]
                approx.append(dot(top, taps) + dot(rest, taps))
            else:
                first = (2 * level - 2) * LANES
                both = dot(top, col_ref[case, :, first : first + 2 * LANES])
                extra = dot(rest, col_ref[case, :, first : first + LANES])
                approx.append(both[:, :LANES] + both[:, LANES:] + extra)
        score = jnp.zeros((depth * rows, LANES), jnp.float32)
        for level in range(LEVELS):
            detail = approx[level] - approx[level + 1]
            score = score + gain_ref[level] * detail * detail
        score = score.reshape(depth, rows, LANES)
        peak = jnp.max(score, axis=0).astype(jnp.bfloat16)
        weight = jnp.exp(score - peak.astype(jnp.float32)[None])
        total = jnp.sum(weight, axis=0)
        inverse = 1.0 / total
        state = [peak, total.astype(jnp.bfloat16)]
        for channel in range(3):
            colour = jnp.sum(weight * planes_ref[:, channel, :, at].astype(jnp.float32), axis=0)
            state.append((colour * inverse).astype(jnp.bfloat16))
        for k, part in enumerate(state):
            held[:, k, :, at] = part.reshape(groups, share, LANES)

    group = lax.axis_index("gz")
    mine_slow, mine_fast = group // fast, group % fast
    for other in range(fast):
        for place in range(slow):
            outs[other][place] = held[place * fast + (mine_fast ^ other), :, :, :split]
    for other in range(slow):
        for place in range(fast):
            outs[fast + other][place] = held[(mine_slow ^ other) * fast + place, :, :, split:]


def local_state(planes, above, below, level_gain, slow, groups, tiles, split):
    depth, _, rows, columns = planes.shape
    fast, share = groups // slow, rows // groups
    row_bands = jnp.asarray(row_matrices(rows * tiles, rows))
    col_bands = jnp.asarray(column_matrices(columns))
    vmem = pl.BlockSpec(memory_space=pltpu.VMEM)
    wide = columns + LANES
    shapes = [(slow, 5, share, split)] * fast + [(fast, 5, share, columns - split)] * slow
    return pl.pallas_call(
        functools.partial(state_kernel, slow),
        out_shape=[jax.ShapeDtypeStruct(shape, jnp.bfloat16) for shape in shapes],
        in_specs=[pl.BlockSpec(memory_space=pltpu.SMEM)] + [vmem] * 5,
        out_specs=[vmem] * len(shapes),
        scratch_shapes=[
            pltpu.VMEM((depth, rows, columns), jnp.bfloat16),
            pltpu.VMEM((depth, rows + 2 * HALO, wide), jnp.bfloat16),
            pltpu.VMEM((LEVELS, depth * rows, wide), jnp.bfloat16),
            pltpu.VMEM((LEVELS, depth * rows, wide), jnp.bfloat16),
            pltpu.VMEM((groups, 5, share, columns), jnp.bfloat16),
        ],
        compiler_params=pltpu.CompilerParams(vmem_limit_bytes=40 * 2**20),
        name="local_state",
    )(level_gain, planes, above, below, row_bands, col_bands)


def merge_kernel(count, pick, *refs):
    states, outs, held = refs[:count], refs[count:-1], refs[-1]
    for place in range(held.shape[0]):
        for k, part in enumerate(combine([[state[place, k] for k in range(5)] for state in states])):
            held[place, k] = part.astype(jnp.bfloat16)
    place = pick(lax.axis_index("gz"))
    for other, out in enumerate(outs):
        out[...] = held[place ^ other]


def merge(states, pick):
    bands, _, share, columns = states[0].shape
    return pl.pallas_call(
        functools.partial(merge_kernel, len(states), pick),
        out_shape=[jax.ShapeDtypeStruct((5, share, columns), jnp.bfloat16)] * bands,
        scratch_shapes=[pltpu.VMEM(states[0].shape, jnp.bfloat16)],
        compiler_params=pltpu.CompilerParams(vmem_limit_bytes=16 * 2**20),
        name="merge",
    )(*states)


def join_kernel(counts, *refs):
    *refs, out_ref = refs
    start = 0
    for count in counts:
        states, refs = refs[:count], refs[count:]
        width = states[0].shape[-1]
        merged = combine([[state[k] for k in range(5)] for state in states])
        for channel in range(3):
            out_ref[channel, :, start : start + width] = merged[2 + channel].astype(jnp.bfloat16)
        start += width


def join(*parts):
    share = parts[0][0].shape[1]
    columns = sum(part[0].shape[2] for part in parts)
    return pl.pallas_call(
        functools.partial(join_kernel, [len(part) for part in parts]),
        out_shape=jax.ShapeDtypeStruct((3, share, columns), jnp.bfloat16),
        compiler_params=pltpu.CompilerParams(vmem_limit_bytes=16 * 2**20),
        name="join",
    )(*[state for part in parts for state in part])


def swap(states, groups, step):
    moved = [
        lax.ppermute(state, "gz", [(i, i ^ (k * step)) for i in range(groups)]) for k, state in enumerate(states) if k
    ]
    return [states[0]] + moved


def per_device(planes, level_gain):
    rows, columns = planes.shape[2:]
    tiles = lax.axis_size("tile")
    groups = lax.axis_size("gz")
    slow = min(4, groups)
    fast = groups // slow
    split = 5 * columns // 8
    head = luminance_of([planes[:, channel, :HALO] for channel in range(3)])
    tail = luminance_of([planes[:, channel, rows - HALO :] for channel in range(3)])
    above = lax.ppermute(tail, "tile", [(i, i + 1) for i in range(tiles - 1)])
    below = lax.ppermute(head, "tile", [(i + 1, i) for i in range(tiles - 1)])
    states = local_state(planes, above, below, level_gain, slow, groups, tiles, split)
    first = swap(states[:fast], groups, 1)
    second = swap(states[fast:], groups, fast)
    first = swap(merge(first, lambda group: group // fast), groups, fast)
    second = swap(merge(second, lambda group: group % fast), groups, 1)
    return join(first, second)


def solution(mesh):
    return jax.shard_map(
        per_device,
        mesh=mesh,
        in_specs=(P("gz", None, "tile", None), P()),
        out_specs=P(None, ("tile", "gz"), None),
        check_vma=False,
    )
```

time: 62.9 us -> 48.9 us (0.78)
  starting transfers between devices: 28.9 us -> 16.8 us
  Pallas kernels: 17.8 us -> 9.76 us
  local copies, waits for them, and re-layouts: 2.21 us -> 5.08 us
  waiting for transfers between devices: 12.1 us -> 14.9 us
    ppermute x7 -> x8, starting transfers between devices: 22.4 us -> 10.3 us  [swap(): lax.ppermute(state, 'gz', [(i, i ^ k * step) for i in range(groups)])]
    pallas_call x2 -> x4, Pallas kernels: 17.8 us -> 9.76 us  [the longest x1 8.57 us: local_state(): pl.pallas_call(functools.partial(state_kernel, slow), out_shape=[jax.Shap...]
    unnamed x4 -> x8, local copies, waits for them, and re-layouts: 0.7 us -> 5.08 us
    ppermute x7 -> x8, waiting for transfers between devices: 8.81 us -> 11.6 us  [swap(): lax.ppermute(state, 'gz', [(i, i ^ k * step) for i in range(groups)])]
    dynamic_slice x1 -> x0, local copies, waits for them, and re-layouts: 1.51 us -> none  [per_device(): band = lax.dynamic_slice_in_dim(state, (me ^ other) * share, share, 1)]
  transfers between devices with their start and end apart: 9 -> 10, of which waited for: 5 -> 5; matrix products, arithmetic and copies ran while one was open for 0% -> 0% of each run, Pallas kernels for 0% -> 1%
where the time goes in v2:
time: 48.9 us; the launch traced here: 48.2 us
  starting transfers between devices  16.8 us (34%)
  waiting for transfers between devices  14.9 us (30%)
  Pallas kernels  9.76 us (20%)
  local copies, waits for them, and re-layouts  5.08 us (10%)
  other arithmetic  1.66 us (3%)
    ppermute x8, waiting for transfers between devices, swap(): lax.ppermute(state, 'gz', [(i, i ^ k * step) for i in range(groups)])  11.6 us
    ppermute x8, starting transfers between devices, swap(): lax.ppermute(state, 'gz', [(i, i ^ k * step) for i in range(groups)])  10.3 us
    pallas_call x1, Pallas kernels, local_state(): pl.pallas_call(functools.partial(state_kernel, slow), out_shape=[jax.Shap...  8.57 us
    unnamed x8, local copies, waits for them, and re-layouts  5.08 us
    ppermute x1, starting transfers between devices, per_device(): above = lax.ppermute(tail, 'tile', [(i, i + 1) for i in range(tiles - 1)])  4.46 us
    ppermute x1, waiting for transfers between devices, per_device(): below = lax.ppermute(head, 'tile', [(i + 1, i) for i in range(tiles - 1)])  2.11 us
    ppermute x1, starting transfers between devices, per_device(): below = lax.ppermute(head, 'tile', [(i + 1, i) for i in range(tiles - 1)])  1.97 us
    add x1, other arithmetic, luminance_of(): return (0.299 * red + 0.587 * green + 0.114 * blue).astype(jnp.bfloat16)  1.66 us
  transfers between devices with their start and end apart: 10, of which 5 were waited for; matrix products, arithmetic and copies ran while one was open for 0% of the time, Pallas kernels for 1%

profile of v2, /device:TPU:1, one launch (start us, length us, event | category | flops | bytes accessed | tf_op | source)
XLA Modules:
  0.0 48.2 jit_solution(3061592599708317918)
XLA Ops:
  0.0 1.7 %fusion.1 = (bf16[4,32,1024]{2,1,0:T(8,128)(2,1)S(1)}, bf16[4,32,1024]{2,1,0:T(8,128)(2,1)S(1)}) fusion(bf16[4,3,128,1024]{3,2,1,0:T(8,128)(2,1)} %planes_ref.1), kind=kLoop, calls=%fused_computation.3 | loop fusion | flops 2359296 | bytes 2097152 | tf_op jit(solution)/shard_map/add | solution.py:74
  1.7 2.0 %collective-permute-start.1 = (bf16[4,32,1024]{2,1,0:T(8,128)(2,1)S(1)}, bf16[4,32,1024]{2,1,0:T(8,128)(2,1)S(1)}, u32[]{:S(2)}, u32[]{:S(2)}) collective-permute-start(bf16[4,32,1024]{2,1,0:T(8,128)(2,1)S(1)} %get-tuple-element.29), channel_id=1, source_target_pairs={{8,0},{16,8},{24,16},{9,1},{17,9},{25,17},{10,2},{18,10},{26,18},{... | collective-permute-start | bytes 786440 | tf_op jit(solution)/shard_map/ppermute | solution.py:245
  3.6 4.5 %collective-permute-start = (bf16[4,32,1024]{2,1,0:T(8,128)(2,1)S(1)}, bf16[4,32,1024]{2,1,0:T(8,128)(2,1)S(1)}, u32[]{:S(2)}, u32[]{:S(2)}) collective-permute-start(bf16[4,32,1024]{2,1,0:T(8,128)(2,1)S(1)} %get-tuple-element.30), channel_id=1, source_target_pairs={{0,8},{8,16},{16,24},{1,9},{9,17},{17,25},{2,10},{10,18},{18,26},{... | collective-permute-start | bytes 786440 | tf_op jit(solution)/shard_map/ppermute | solution.py:244
  8.1 2.1 %collective-permute-done.1.below_ref = bf16[4,32,1024]{2,1,0:T(8,128)(2,1)S(1)} collective-permute-done((bf16[4,32,1024]{2,1,0:T(8,128)(2,1)S(1)}, bf16[4,32,1024]{2,1,0:T(8,128)(2,1)S(1)}, u32[]{:S(2)}, u32[]{:S(2)}) %collective-permute-start.1) | collective-permute-done | bytes 262176 | tf_op jit(solution)/shard_map/ppermute | solution.py:245
  10.2 1.2 %collective-permute-done.above_ref = bf16[4,32,1024]{2,1,0:T(8,128)(2,1)S(1)} collective-permute-done((bf16[4,32,1024]{2,1,0:T(8,128)(2,1)S(1)}, bf16[4,32,1024]{2,1,0:T(8,128)(2,1)S(1)}, u32[]{:S(2)}, u32[]{:S(2)}) %collective-permute-start) | collective-permute-done | bytes 262176 | tf_op jit(solution)/shard_map/ppermute | solution.py:244
  11.4 0.0 copy-start
  11.4 1.9 %copy-done = bf16[4,3,128,1024]{3,2,1,0:T(8,128)(2,1)S(1)} copy-done((bf16[4,3,128,1024]{3,2,1,0:T(8,128)(2,1)S(1)}, bf16[4,3,128,1024]{3,2,1,0:T(8,128)(2,1)}, u32[]{:S(2)}) %copy-start) | copy-done | bytes 3145752
  13.3 0.0 copy-start.1
  13.3 1.3 %copy-done.1 = bf16[3,256,768]{2,1,0:T(8,128)(2,1)S(1)} copy-done((bf16[3,256,768]{2,1,0:T(8,128)(2,1)S(1)}, bf16[3,256,768]{2,1,0:T(8,128)(2,1)}, u32[]{:S(2)}) %copy-start.1) | copy-done | bytes 1179672
  14.6 0.0 copy-start.2
  14.6 1.3 %copy-done.2 = bf16[3,768,192]{2,1,0:T(8,128)(2,1)S(1)} copy-done((bf16[3,768,192]{2,1,0:T(8,128)(2,1)S(1)}, bf16[3,768,192]{2,1,0:T(8,128)(2,1)}, u32[]{:S(2)}) %copy-start.2) | copy-done | bytes 884760
  15.8 0.0 copy-start.3
  15.8 0.7 %copy-done.3 = f32[4]{0:T(128)S(1)} copy-done((f32[4]{0:T(128)S(1)}, f32[4]{0:T(128)}, u32[]{:S(2)}) %copy-start.3) | copy-done | bytes 40
  16.5 8.6 %local_state.1 = (bf16[4,5,16,640]{3,2,1,0:T(8,128)(2,1)S(1)}, bf16[4,5,16,640]{3,2,1,0:T(8,128)(2,1)S(1)}, bf16[2,5,16,384]{3,2,1,0:T(8,128)(2,1)S(1)}, bf16[2,...) custom-call(f32[4]{0:T(128)S(1)} %copy-done.3, ...), custom_call_target="tpu_custom_call" | custom-call | tf_op jit(solution)/shard_map/local_state/pallas_call | solution.py:167
  25.1 1.3 %collective-permute-start.2 = (bf16[4,5,16,640]{3,2,1,0:T(8,128)(2,1)S(1)}, bf16[4,5,16,640]{3,2,1,0:T(8,128)(2,1)S(1)}, u32[]{:S(2)}, u32[]{:S(2)}) collective-permute-start(bf16[4,5,16,640]{3,2,1,0:T(8,128)(2,1)S(1)} %get-tuple-element.18), channel_id=1, source_target_pairs={{0,1},{1,0},{2,3},{3,2},{4,5},{5,4},{6,7},{7,6},{8,9},{9,8},{10,11... | collective-permute-start | bytes 1228808 | tf_op jit(solution)/shard_map/ppermute | solution.py:230
  26.4 1.3 %collective-permute-start.6 = (bf16[2,5,16,384]{3,2,1,0:T(8,128)(2,1)S(1)}, bf16[2,5,16,384]{3,2,1,0:T(8,128)(2,1)S(1)}, u32[]{:S(2)}, u32[]{:S(2)}) collective-permute-start(bf16[2,5,16,384]{3,2,1,0:T(8,128)(2,1)S(1)} %get-tuple-element.24), channel_id=1, source_target_pairs={{0,2},{1,3},{2,0},{3,1},{4,6},{5,7},{6,4},{7,5},{8,10},{9,11},{10,... | collective-permute-start | bytes 368648 | tf_op jit(solution)/shard_map/ppermute | solution.py:230
  27.7 2.3 %collective-permute-start.7 = (bf16[2,5,16,384]{3,2,1,0:T(8,128)(2,1)S(1)}, bf16[2,5,16,384]{3,2,1,0:T(8,128)(2,1)S(1)}, u32[]{:S(2)}, u32[]{:S(2)}) collective-permute-start(bf16[2,5,16,384]{3,2,1,0:T(8,128)(2,1)S(1)} %get-tuple-element.25), channel_id=1, source_target_pairs={{0,4},{1,5},{2,6},{3,7},{4,0},{5,1},{6,2},{7,3},{8,12},{9,13},{10,... | collective-permute-start | bytes 368648 | tf_op jit(solution)/shard_map/ppermute | solution.py:230
  30.0 0.0 collective-permute-start.8
  30.0 3.8 %collective-permute-done.2.refs_1_ = bf16[4,5,16,640]{3,2,1,0:T(8,128)(2,1)S(1)} collective-permute-done((bf16[4,5,16,640]{3,2,1,0:T(8,128)(2,1)S(1)}, bf16[4,5,16,640]{3,2,1,0:T(8,128)(2,1)S(1)}, u32[]{:S(2)}, u32[]{:S(2)}) %collective-permute-start.2) | collective-permute-done | bytes 409632 | tf_op jit(solution)/shard_map/ppermute | solution.py:230
  33.8 0.3 merge.2
  34.1 1.9 %collective-permute-start.3 = (bf16[5,16,640]{2,1,0:T(8,128)(2,1)S(1)}, bf16[5,16,640]{2,1,0:T(8,128)(2,1)S(1)}, u32[]{:S(2)}, u32[]{:S(2)}) collective-permute-start(bf16[5,16,640]{2,1,0:T(8,128)(2,1)S(1)} %get-tuple-element.20), channel_id=1, source_target_pairs={{0,2},{1,3},{2,0},{3,1},{4,6},{5,7},{6,4},{7,5},{8,10},{9,11},{10,... | collective-permute-start | bytes 307208 | tf_op jit(solution)/shard_map/ppermute | solution.py:230
  36.0 2.3 %collective-permute-start.4 = (bf16[5,16,640]{2,1,0:T(8,128)(2,1)S(1)}, bf16[5,16,640]{2,1,0:T(8,128)(2,1)S(1)}, u32[]{:S(2)}, u32[]{:S(2)}) collective-permute-start(bf16[5,16,640]{2,1,0:T(8,128)(2,1)S(1)} %get-tuple-element.21), channel_id=1, source_target_pairs={{0,4},{1,5},{2,6},{3,7},{4,0},{5,1},{6,2},{7,3},{8,12},{9,13},{10,... | collective-permute-start | bytes 307208 | tf_op jit(solution)/shard_map/ppermute | solution.py:230
  38.3 0.0 collective-permute-done.6.refs_1_
  38.3 0.0 collective-permute-start.5
  38.3 0.0 collective-permute-done.7.refs_2_
  38.3 0.0 collective-permute-done.8.refs_3_
  38.3 0.2 merge.3
  38.4 1.2 %collective-permute-start.9 = (bf16[5,16,384]{2,1,0:T(8,128)(2,1)S(1)}, bf16[5,16,384]{2,1,0:T(8,128)(2,1)S(1)}, u32[]{:S(2)}, u32[]{:S(2)}) collective-permute-start(bf16[5,16,384]{2,1,0:T(8,128)(2,1)S(1)} %get-tuple-element.28), channel_id=1, source_target_pairs={{0,1},{1,0},{2,3},{3,2},{4,5},{5,4},{6,7},{7,6},{8,9},{9,8},{10,11... | collective-permute-start | bytes 184328 | tf_op jit(solution)/shard_map/ppermute | solution.py:230
  39.7 2.2 %collective-permute-done.9.refs_5_ = bf16[5,16,384]{2,1,0:T(8,128)(2,1)S(1)} collective-permute-done((bf16[5,16,384]{2,1,0:T(8,128)(2,1)S(1)}, bf16[5,16,384]{2,1,0:T(8,128)(2,1)S(1)}, u32[]{:S(2)}, u32[]{:S(2)}) %collective-permute-start.9) | collective-permute-done | bytes 61472 | tf_op jit(solution)/shard_map/ppermute | solution.py:230
  41.9 0.0 collective-permute-done.3.refs_1_
  41.9 5.6 %collective-permute-done.4.refs_2_ = bf16[5,16,640]{2,1,0:T(8,128)(2,1)S(1)} collective-permute-done((bf16[5,16,640]{2,1,0:T(8,128)(2,1)S(1)}, bf16[5,16,640]{2,1,0:T(8,128)(2,1)S(1)}, u32[]{:S(2)}, u32[]{:S(2)}) %collective-permute-start.4) | collective-permute-done | bytes 102432 | tf_op jit(solution)/shard_map/ppermute | solution.py:230
  47.4 0.0 collective-permute-done.5.refs_3_
  47.4 0.8 %join.1 = bf16[3,16,1024]{2,1,0:T(8,128)(2,1)} custom-call(bf16[5,16,640]{2,1,0:T(8,128)(2,1)S(1)} %get-tuple-element.19.refs_0_, bf16[5,16,640]{2,1,0:T(8,128)(2,1)S(1)} %collective-permute-done.3.refs_1_, bf16[5,16,640]{2,1,0:T(8,128)(2,1)S(1)} %collective-permute-done.4.refs_2_, bf16[5,16,640]{2,1,0:T(8,128)(2,1)S(1)} %collective-permute-done.5.refs_3_, ...), custom_call_target="tpu_custom_call" | custom-call | tf_op jit(solution)/shard_map/join/pallas_call | solution.py:220
Async XLA Ops:
  1.7 8.6 %collective-permute-start.1 = (bf16[4,32,1024]{2,1,0:T(8,128)(2,1)S(1)}, bf16[4,32,1024]{2,1,0:T(8,128)(2,1)S(1)}, u32[]{:S(2)}, u32[]{:S(2)}) collective-permute-start(bf16[4,32,1024]{2,1,0:T(8,128)(2,1)S(1)} %get-tuple-element.29), channel_id=1, source_target_pairs={{8,0},{16,8},{24,16},{9,1},{17,9},{25,17},{10,2},{18,10},{26,18},{... | collective-permute-start | bytes 786440 | tf_op jit(solution)/shard_map/ppermute | solution.py:245
  3.6 7.8 %collective-permute-start = (bf16[4,32,1024]{2,1,0:T(8,128)(2,1)S(1)}, bf16[4,32,1024]{2,1,0:T(8,128)(2,1)S(1)}, u32[]{:S(2)}, u32[]{:S(2)}) collective-permute-start(bf16[4,32,1024]{2,1,0:T(8,128)(2,1)S(1)} %get-tuple-element.30), channel_id=1, source_target_pairs={{0,8},{8,16},{16,24},{1,9},{9,17},{17,25},{2,10},{10,18},{18,26},{... | collective-permute-start | bytes 786440 | tf_op jit(solution)/shard_map/ppermute | solution.py:244
  11.4 1.9 %copy-start = (bf16[4,3,128,1024]{3,2,1,0:T(8,128)(2,1)S(1)}, bf16[4,3,128,1024]{3,2,1,0:T(8,128)(2,1)}, u32[]{:S(2)}) copy-start(bf16[4,3,128,1024]{3,2,1,0:T(8,128)(2,1)} %planes_ref.1) | copy-start | bytes 9437188
  13.3 1.3 %copy-start.1 = (bf16[3,256,768]{2,1,0:T(8,128)(2,1)S(1)}, bf16[3,256,768]{2,1,0:T(8,128)(2,1)}, u32[]{:S(2)}) copy-start(bf16[3,256,768]{2,1,0:T(8,128)(2,1)} %constant.11.clone.col_ref) | copy-start | bytes 3538948
  14.6 1.3 %copy-start.2 = (bf16[3,768,192]{2,1,0:T(8,128)(2,1)S(1)}, bf16[3,768,192]{2,1,0:T(8,128)(2,1)}, u32[]{:S(2)}) copy-start(bf16[3,768,192]{2,1,0:T(8,128)(2,1)} %constant.10.clone.row_ref) | copy-start | bytes 2654212
  15.8 0.7 %copy-start.3 = (f32[4]{0:T(128)S(1)}, f32[4]{0:T(128)}, u32[]{:S(2)}) copy-start(f32[4]{0:T(128)} %gain_ref.1) | copy-start | bytes 52
  25.1 8.8 %collective-permute-start.2 = (bf16[4,5,16,640]{3,2,1,0:T(8,128)(2,1)S(1)}, bf16[4,5,16,640]{3,2,1,0:T(8,128)(2,1)S(1)}, u32[]{:S(2)}, u32[]{:S(2)}) collective-permute-start(bf16[4,5,16,640]{3,2,1,0:T(8,128)(2,1)S(1)} %get-tuple-element.18), channel_id=1, source_target_pairs={{0,1},{1,0},{2,3},{3,2},{4,5},{5,4},{6,7},{7,6},{8,9},{9,8},{10,11... | collective-permute-start | bytes 1228808 | tf_op jit(solution)/shard_map/ppermute | solution.py:230
  26.4 11.9 %collective-permute-start.6 = (bf16[2,5,16,384]{3,2,1,0:T(8,128)(2,1)S(1)}, bf16[2,5,16,384]{3,2,1,0:T(8,128)(2,1)S(1)}, u32[]{:S(2)}, u32[]{:S(2)}) collective-permute-start(bf16[2,5,16,384]{3,2,1,0:T(8,128)(2,1)S(1)} %get-tuple-element.24), channel_id=1, source_target_pairs={{0,2},{1,3},{2,0},{3,1},{4,6},{5,7},{6,4},{7,5},{8,10},{9,11},{10,... | collective-permute-start | bytes 368648 | tf_op jit(solution)/shard_map/ppermute | solution.py:230
  27.7 10.6 %collective-permute-start.7 = (bf16[2,5,16,384]{3,2,1,0:T(8,128)(2,1)S(1)}, bf16[2,5,16,384]{3,2,1,0:T(8,128)(2,1)S(1)}, u32[]{:S(2)}, u32[]{:S(2)}) collective-permute-start(bf16[2,5,16,384]{3,2,1,0:T(8,128)(2,1)S(1)} %get-tuple-element.25), channel_id=1, source_target_pairs={{0,4},{1,5},{2,6},{3,7},{4,0},{5,1},{6,2},{7,3},{8,12},{9,13},{10,... | collective-permute-start | bytes 368648 | tf_op jit(solution)/shard_map/ppermute | solution.py:230
  30.0 8.3 %collective-permute-start.8 = (bf16[2,5,16,384]{3,2,1,0:T(8,128)(2,1)S(1)}, bf16[2,5,16,384]{3,2,1,0:T(8,128)(2,1)S(1)}, u32[]{:S(2)}, u32[]{:S(2)}) collective-permute-start(bf16[2,5,16,384]{3,2,1,0:T(8,128)(2,1)S(1)} %get-tuple-element.26), channel_id=1, source_target_pairs={{0,6},{1,7},{2,4},{3,5},{4,2},{5,3},{6,0},{7,1},{8,14},{9,15},{10,... | collective-permute-start | bytes 368648 | tf_op jit(solution)/shard_map/ppermute | solution.py:230
  34.1 7.8 %collective-permute-start.3 = (bf16[5,16,640]{2,1,0:T(8,128)(2,1)S(1)}, bf16[5,16,640]{2,1,0:T(8,128)(2,1)S(1)}, u32[]{:S(2)}, u32[]{:S(2)}) collective-permute-start(bf16[5,16,640]{2,1,0:T(8,128)(2,1)S(1)} %get-tuple-element.20), channel_id=1, source_target_pairs={{0,2},{1,3},{2,0},{3,1},{4,6},{5,7},{6,4},{7,5},{8,10},{9,11},{10,... | collective-permute-start | bytes 307208 | tf_op jit(solution)/shard_map/ppermute | solution.py:230
  36.0 11.5 %collective-permute-start.4 = (bf16[5,16,640]{2,1,0:T(8,128)(2,1)S(1)}, bf16[5,16,640]{2,1,0:T(8,128)(2,1)S(1)}, u32[]{:S(2)}, u32[]{:S(2)}) collective-permute-start(bf16[5,16,640]{2,1,0:T(8,128)(2,1)S(1)} %get-tuple-element.21), channel_id=1, source_target_pairs={{0,4},{1,5},{2,6},{3,7},{4,0},{5,1},{6,2},{7,3},{8,12},{9,13},{10,... | collective-permute-start | bytes 307208 | tf_op jit(solution)/shard_map/ppermute | solution.py:230
  38.3 9.2 %collective-permute-start.5 = (bf16[5,16,640]{2,1,0:T(8,128)(2,1)S(1)}, bf16[5,16,640]{2,1,0:T(8,128)(2,1)S(1)}, u32[]{:S(2)}, u32[]{:S(2)}) collective-permute-start(bf16[5,16,640]{2,1,0:T(8,128)(2,1)S(1)} %get-tuple-element.22), channel_id=1, source_target_pairs={{0,6},{1,7},{2,4},{3,5},{4,2},{5,3},{6,0},{7,1},{8,14},{9,15},{10,... | collective-permute-start | bytes 307208 | tf_op jit(solution)/shard_map/ppermute | solution.py:230
  38.4 3.4 %collective-permute-start.9 = (bf16[5,16,384]{2,1,0:T(8,128)(2,1)S(1)}, bf16[5,16,384]{2,1,0:T(8,128)(2,1)S(1)}, u32[]{:S(2)}, u32[]{:S(2)}) collective-permute-start(bf16[5,16,384]{2,1,0:T(8,128)(2,1)S(1)} %get-tuple-element.28), channel_id=1, source_target_pairs={{0,1},{1,0},{2,3},{3,2},{4,5},{5,4},{6,7},{7,6},{8,9},{9,8},{10,11... | collective-permute-start | bytes 184328 | tf_op jit(solution)/shard_map/ppermute | solution.py:230

commit v3 on v2

--- a/solution.py
+++ b/solution.py
@@ -87,28 +87,101 @@
     return [peak, total] + colours
 
 
-def state_kernel(slow, gain_ref, planes_ref, above_ref, below_ref, row_ref, col_ref, *refs):
-    *outs, lum, wide, high, low, held = refs
+def edge_kernel(planes_ref, core_ref, far_ref, edges, arrived):
+    rows = planes_ref.shape[2]
+    odd = lax.axis_index("tile") % 2
+    tail, head = rows - HALO, 0
+    copies = []
+    for side, start in enumerate((jnp.where(odd == 0, tail, head), jnp.where(odd == 0, head, tail))):
+        at = pl.ds(pl.multiple_of(start, HALO), HALO)
+        copies.append(pltpu.make_async_copy(planes_ref.at[:, :, at], edges.at[side], arrived.at[side]))
+        copies[-1].start()
+    for side, out in enumerate((core_ref, far_ref)):
+        copies[side].wait()
+        for plane in range(planes_ref.shape[0]):
+            out[plane] = luminance_of([edges[side, plane, channel] for channel in range(3)])
+
+
+def edge_luminance(planes):
+    depth, channels, rows, columns = planes.shape
+    vmem = pl.BlockSpec(memory_space=pltpu.VMEM)
+    return pl.pallas_call(
+        edge_kernel,
+        out_shape=[jax.ShapeDtypeStruct((depth, HALO, columns), jnp.bfloat16)] * 2,
+        in_specs=[pl.BlockSpec(memory_space=pl.ANY)],
+        out_specs=[vmem] * 2,
+        scratch_shapes=[
+            pltpu.VMEM((2, depth, channels, HALO, columns), jnp.bfloat16),
+            pltpu.SemaphoreType.DMA((2,)),
+        ],
+        compiler_params=pltpu.CompilerParams(vmem_limit_bytes=52 * 2**20),
+        name="edge_luminance",
+    )(planes)
+
+
+def own_kernel(planes_ref, rows_ref, cols_ref, stack_ref, lum_ref, wide_ref, row_ref, col_ref, arrived):
+    depth, _, rows, columns = planes_ref.shape
+    tile, tiles = lax.axis_index("tile"), lax.axis_size("tile")
+    tile_case = jnp.where(tile == 0, 0, jnp.where(tile == tiles - 1, 2, 1))
+    copies = [pltpu.make_async_copy(planes_ref.at[p], stack_ref.at[p], arrived.at[p]) for p in range(depth)]
+    copies.append(pltpu.make_async_copy(rows_ref.at[tile_case], row_ref, arrived.at[depth]))
+    copies.append(pltpu.make_async_copy(cols_ref, col_ref, arrived.at[depth + 1]))
+    for copy in copies:
+        copy.start()
+    padding = jnp.zeros((rows, LANES), jnp.float32)
+    for plane in range(depth):
+        copies[plane].wait()
+        own = luminance_of([stack_ref[plane, channel] for channel in range(3)])
+        lum_ref[plane] = own
+        field = jnp.concatenate([own.astype(jnp.float32), padding], axis=1)
+        wide_ref[plane] = pltpu.roll(field, SIDE, 1).astype(jnp.bfloat16)
+    for copy in copies[depth:]:
+        copy.wait()
+
+
+def own_rows(planes, tiles):
+    depth, channels, rows, columns = planes.shape
+    row_bands = jnp.asarray(row_matrices(rows * tiles, rows))
+    col_bands = jnp.asarray(column_matrices(columns))
+    vmem = pl.BlockSpec(memory_space=pltpu.VMEM)
+    shapes = [planes.shape, (depth, rows, columns), (depth, rows, columns + LANES), row_bands.shape[1:], col_bands.shape]
+    return pl.pallas_call(
+        own_kernel,
+        out_shape=[jax.ShapeDtypeStruct(shape, jnp.bfloat16) for shape in shapes],
+        in_specs=[pl.BlockSpec(memory_space=pl.ANY)] * 3,
+        out_specs=[vmem] * len(shapes),
+        scratch_shapes=[pltpu.SemaphoreType.DMA((depth + 2,))],
+        compiler_params=pltpu.CompilerParams(vmem_limit_bytes=44 * 2**20),
+        cost_estimate=pl.CostEstimate(flops=2**24, bytes_accessed=10 * 2**20, transcendentals=0),
+        name="own_rows",
+    )(planes, row_bands, col_bands)
+
+
+def state_kernel(slow, gain_ref, planes_ref, lum_ref, wide_ref, core_ref, far_ref, row_ref, col_ref, *refs):
+    *outs, halo, high, low, held = refs
     depth, _, rows, columns = planes_ref.shape
     groups, _, share, _ = held.shape
     fast = groups // slow
     split = outs[0].shape[-1]
     blocks = columns // LANES
-    tile, tiles = lax.axis_index("tile"), lax.axis_size("tile")
-    tile_case = jnp.where(tile == 0, 0, jnp.where(tile == tiles - 1, 2, 1))
-    padding = jnp.zeros((rows + 2 * HALO, LANES), jnp.float32)
-    for plane in range(depth):
-        own = luminance_of([planes_ref[plane, channel] for channel in range(3)])
-        lum[plane] = own
-        field = jnp.concatenate([above_ref[plane], own, below_ref[plane]], axis=0).astype(jnp.float32)
-        field = jnp.concatenate([field, padding], axis=1)
-        wide[plane] = pltpu.roll(field, SIDE, 1).astype(jnp.bfloat16)
+    odd = lax.axis_index("tile") % 2
+    padding = jnp.zeros((HALO, LANES), jnp.float32)
+
+    def place_halo(above_ref, below_ref):
+        for side, ref in enumerate((above_ref, below_ref)):
+            for plane in range(depth):
+                field = jnp.concatenate([ref[plane].astype(jnp.float32), padding], axis=1)
+                halo[side, plane] = pltpu.roll(field, SIDE, 1).astype(jnp.bfloat16)
+
+    pl.when(odd == 0)(lambda: place_halo(far_ref, core_ref))
+    pl.when(odd == 1)(lambda: place_halo(core_ref, far_ref))
 
     for start in range(0, columns + LANES, 2 * LANES):
         at = pl.ds(start, min(2 * LANES, columns + LANES - start))
         for plane in range(depth):
             here = pl.ds(plane * rows, rows)
-            smooth = dot(row_ref[tile_case], wide[plane, :, at])
+            window = jnp.concatenate([halo[0, plane, :, at], wide_ref[plane, :, at], halo[1, plane, :, at]], axis=0)
+            smooth = dot(row_ref[...], window)
             part = [smooth[k * rows : (k + 1) * rows] for k in range(6)]
             for level, value in enumerate((part[0], part[1], part[2] + part[3], part[4] + part[5])):
                 top = value.astype(jnp.bfloat16)
@@ -119,7 +192,7 @@
         at = pl.ds(block * LANES, LANES)
         window = pl.ds(block * LANES, 2 * LANES)
         case = 0 if block == 0 else 2 if block == blocks - 1 else 1
-        approx = [lum[:, :, at].astype(jnp.float32).reshape(depth * rows, LANES)]
+        approx = [lum_ref[:, :, at].astype(jnp.float32).reshape(depth * rows, LANES)]
         for level in range(LEVELS):
             top, rest = high[level, :, window], low[level, :, window]
             if level < 2:
@@ -156,29 +229,26 @@
             outs[fast + other][place] = held[(mine_slow ^ other) * fast + place, :, :, split:]
 
 
-def local_state(planes, above, below, level_gain, slow, groups, tiles, split):
-    depth, _, rows, columns = planes.shape
+def local_state(own, core, far, level_gain, slow, groups, split):
+    depth, _, rows, columns = own[0].shape
     fast, share = groups // slow, rows // groups
-    row_bands = jnp.asarray(row_matrices(rows * tiles, rows))
-    col_bands = jnp.asarray(column_matrices(columns))
     vmem = pl.BlockSpec(memory_space=pltpu.VMEM)
     wide = columns + LANES
     shapes = [(slow, 5, share, split)] * fast + [(fast, 5, share, columns - split)] * slow
     return pl.pallas_call(
         functools.partial(state_kernel, slow),
         out_shape=[jax.ShapeDtypeStruct(shape, jnp.bfloat16) for shape in shapes],
-        in_specs=[pl.BlockSpec(memory_space=pltpu.SMEM)] + [vmem] * 5,
+        in_specs=[pl.BlockSpec(memory_space=pltpu.SMEM)] + [vmem] * 7,
         out_specs=[vmem] * len(shapes),
         scratch_shapes=[
-            pltpu.VMEM((depth, rows, columns), jnp.bfloat16),
-            pltpu.VMEM((depth, rows + 2 * HALO, wide), jnp.bfloat16),
+            pltpu.VMEM((2, depth, HALO, wide), jnp.bfloat16),
             pltpu.VMEM((LEVELS, depth * rows, wide), jnp.bfloat16),
             pltpu.VMEM((LEVELS, depth * rows, wide), jnp.bfloat16),
             pltpu.VMEM((groups, 5, share, columns), jnp.bfloat16),
         ],
         compiler_params=pltpu.CompilerParams(vmem_limit_bytes=40 * 2**20),
         name="local_state",
-    )(level_gain, planes, above, below, row_bands, col_bands)
+    )(level_gain, *own[:3], core, far, *own[3:])
 
 
 def merge_kernel(count, pick, *refs):
@@ -233,17 +303,18 @@
 
 
 def per_device(planes, level_gain):
-    rows, columns = planes.shape[2:]
+    columns = planes.shape[3]
     tiles = lax.axis_size("tile")
     groups = lax.axis_size("gz")
     slow = min(4, groups)
     fast = groups // slow
     split = 5 * columns // 8
-    head = luminance_of([planes[:, channel, :HALO] for channel in range(3)])
-    tail = luminance_of([planes[:, channel, rows - HALO :] for channel in range(3)])
-    above = lax.ppermute(tail, "tile", [(i, i + 1) for i in range(tiles - 1)])
-    below = lax.ppermute(head, "tile", [(i + 1, i) for i in range(tiles - 1)])
-    states = local_state(planes, above, below, level_gain, slow, groups, tiles, split)
+    to_core, to_far = edge_luminance(planes)
+    core = lax.ppermute(to_core, "tile", [(i, i ^ 1) for i in range(tiles)])
+    between = range(1, tiles - 1, 2)
+    far = lax.ppermute(to_far, "tile", [(i, i + 1) for i in between] + [(i + 1, i) for i in between])
+    own = own_rows(planes, tiles)
+    states = local_state(own, core, far, level_gain, slow, groups, split)
     first = swap(states[:fast], groups, 1)
     second = swap(states[fast:], groups, fast)
     first = swap(merge(first, lambda group: group // fast), groups, fast)

time: 48.9 us -> 41.4 us (0.85)
  the two profiles are of different devices: /device:TPU:1 before, /device:TPU:10 now
where the time goes in v3:
time: 41.4 us; the launch traced here: 41.2 us
  waiting for transfers between devices  16.7 us (40%)
  Pallas kernels  13 us (31%)
  starting transfers between devices  11.4 us (28%)
    ppermute x8, waiting for transfers between devices, swap(): lax.ppermute(state, 'gz', [(i, i ^ k * step) for i in range(groups)])  13.9 us
    ppermute x8, starting transfers between devices, swap(): lax.ppermute(state, 'gz', [(i, i ^ k * step) for i in range(groups)])  8.7 us
    pallas_call x1, Pallas kernels, local_state(): pl.pallas_call(functools.partial(state_kernel, slow), out_shape=[jax.Shap...  7.95 us
    ppermute x1, waiting for transfers between devices, per_device(): lax.ppermute(to_far, 'tile', [(i, i + 1) for i in between] + [(i + 1, i)...  2.81 us
    ppermute x1, starting transfers between devices, per_device(): lax.ppermute(to_far, 'tile', [(i, i + 1) for i in between] + [(i + 1, i)...  2.65 us
    pallas_call x1, Pallas kernels, own_rows(): pl.pallas_call(own_kernel, out_shape=[jax.ShapeDtypeStruct(shape, jnp.bfl...  2.18 us
    pallas_call x1, Pallas kernels, edge_luminance(): pl.pallas_call(edge_kernel, out_shape=[jax.ShapeDtypeStruct((depth, HALO,...  1.68 us
  transfers between devices with their start and end apart: 10, of which 5 were waited for; matrix products, arithmetic and copies ran while one was open for 0% of the time, Pallas kernels for 6%

profile of v3, /device:TPU:10, one launch (start us, length us, event | category | flops | bytes accessed | tf_op | source)
XLA Modules:
  0.0 41.2 jit_solution(6381402205749773607)
XLA Ops:
  0.0 0.0 copy-start
  0.0 0.0 copy-start.1
  0.0 1.7 %edge_luminance.1 = (bf16[4,32,1024]{2,1,0:T(8,128)(2,1)S(1)}, bf16[4,32,1024]{2,1,0:T(8,128)(2,1)S(1)}) custom-call(bf16[4,3,128,1024]{3,2,1,0:T(8,128)(2,1)} %planes_ref.3), custom_call_target="tpu_custom_call" | custom-call | tf_op jit(solution)/shard_map/edge_luminance/pallas_call | solution.py:108
  1.7 0.1 collective-permute-start
  1.8 0.0 copy-start.2
  1.8 2.7 %collective-permute-start.1 = (bf16[4,32,1024]{2,1,0:T(8,128)(2,1)S(1)}, bf16[4,32,1024]{2,1,0:T(8,128)(2,1)S(1)}, u32[]{:S(2)}, u32[]{:S(2)}) collective-permute-start(bf16[4,32,1024]{2,1,0:T(8,128)(2,1)S(1)} %get-tuple-element.28), channel_id=1, source_target_pairs={{8,16},{16,8},{9,17},{17,9},{10,18},{18,10},{11,19},{19,11},{12,20... | collective-permute-start | bytes 786440 | tf_op jit(solution)/shard_map/ppermute | solution.py:315
  4.4 0.0 copy-done
  4.5 0.0 copy-done.1
  4.5 2.2 %own_rows.1 = (bf16[4,3,128,1024]{3,2,1,0:T(8,128)(2,1)S(1)}, bf16[4,128,1024]{2,1,0:T(8,128)(2,1)S(1)}, bf16[4,128,1152]{2,1,0:T(8,128)(2,1)S(1)}, bf16[768,192]{1,0:T(8,128)(2,1)S(1)}, bf16[3,256,768]{2,1,0:T(8,128)(2,1)S(1)}) custom-call(bf16[4,3,128,1024]{3,2,1,0:T(8,128)(2,1)} %planes_ref.3, bf16[3,768,192]{2,1,0:T(8,128)(2,1)S(1)} %copy-done.1, ...), custom_call_target="tpu_custom_call" | custom-call | flops 16777216 | bytes 10485760 | tf_op jit(solution)/shard_map/own_rows/pallas_call | solution.py:148
  6.7 0.0 collective-permute-done.core_ref
  6.7 2.8 %collective-permute-done.1.far_ref = bf16[4,32,1024]{2,1,0:T(8,128)(2,1)S(1)} collective-permute-done((bf16[4,32,1024]{2,1,0:T(8,128)(2,1)S(1)}, bf16[4,32,1024]{2,1,0:T(8,128)(2,1)S(1)}, u32[]{:S(2)}, u32[]{:S(2)}) %collective-permute-start.1) | collective-permute-done | bytes 262176 | tf_op jit(solution)/shard_map/ppermute | solution.py:315
  9.5 0.0 copy-done.2
  9.5 8.0 %local_state.1 = (bf16[4,5,16,640]{3,2,1,0:T(8,128)(2,1)S(1)}, bf16[4,5,16,640]{3,2,1,0:T(8,128)(2,1)S(1)}, bf16[2,5,16,384]{3,2,1,0:T(8,128)(2,1)S(1)}, bf16[2,...) custom-call(f32[4]{0:T(128)S(1)} %copy-done.2, ...), custom_call_target="tpu_custom_call" | custom-call | tf_op jit(solution)/shard_map/local_state/pallas_call | solution.py:238
  17.4 1.6 %collective-permute-start.2 = (bf16[4,5,16,640]{3,2,1,0:T(8,128)(2,1)S(1)}, bf16[4,5,16,640]{3,2,1,0:T(8,128)(2,1)S(1)}, u32[]{:S(2)}, u32[]{:S(2)}) collective-permute-start(bf16[4,5,16,640]{3,2,1,0:T(8,128)(2,1)S(1)} %get-tuple-element.32), channel_id=1, source_target_pairs={{0,1},{1,0},{2,3},{3,2},{4,5},{5,4},{6,7},{7,6},{8,9},{9,8},{10,11... | collective-permute-start | bytes 1228808 | tf_op jit(solution)/shard_map/ppermute | solution.py:300
  19.0 0.5 %collective-permute-start.6 = (bf16[2,5,16,384]{3,2,1,0:T(8,128)(2,1)S(1)}, bf16[2,5,16,384]{3,2,1,0:T(8,128)(2,1)S(1)}, u32[]{:S(2)}, u32[]{:S(2)}) collective-permute-start(bf16[2,5,16,384]{3,2,1,0:T(8,128)(2,1)S(1)} %get-tuple-element.38), channel_id=1, source_target_pairs={{0,2},{1,3},{2,0},{3,1},{4,6},{5,7},{6,4},{7,5},{8,10},{9,11},{10,... | collective-permute-start | bytes 368648 | tf_op jit(solution)/shard_map/ppermute | solution.py:300
  19.5 2.6 %collective-permute-start.7 = (bf16[2,5,16,384]{3,2,1,0:T(8,128)(2,1)S(1)}, bf16[2,5,16,384]{3,2,1,0:T(8,128)(2,1)S(1)}, u32[]{:S(2)}, u32[]{:S(2)}) collective-permute-start(bf16[2,5,16,384]{3,2,1,0:T(8,128)(2,1)S(1)} %get-tuple-element.39), channel_id=1, source_target_pairs={{0,4},{1,5},{2,6},{3,7},{4,0},{5,1},{6,2},{7,3},{8,12},{9,13},{10,... | collective-permute-start | bytes 368648 | tf_op jit(solution)/shard_map/ppermute | solution.py:300
  22.1 0.4 %collective-permute-start.8 = (bf16[2,5,16,384]{3,2,1,0:T(8,128)(2,1)S(1)}, bf16[2,5,16,384]{3,2,1,0:T(8,128)(2,1)S(1)}, u32[]{:S(2)}, u32[]{:S(2)}) collective-permute-start(bf16[2,5,16,384]{3,2,1,0:T(8,128)(2,1)S(1)} %get-tuple-element.40), channel_id=1, source_target_pairs={{0,6},{1,7},{2,4},{3,5},{4,2},{5,3},{6,0},{7,1},{8,14},{9,15},{10,... | collective-permute-start | bytes 368648 | tf_op jit(solution)/shard_map/ppermute | solution.py:300
  22.5 2.9 %collective-permute-done.2.refs_1_ = bf16[4,5,16,640]{3,2,1,0:T(8,128)(2,1)S(1)} collective-permute-done((bf16[4,5,16,640]{3,2,1,0:T(8,128)(2,1)S(1)}, bf16[4,5,16,640]{3,2,1,0:T(8,128)(2,1)S(1)}, u32[]{:S(2)}, u32[]{:S(2)}) %collective-permute-start.2) | collective-permute-done | bytes 409632 | tf_op jit(solution)/shard_map/ppermute | solution.py:300
  25.5 0.3 merge.2
  25.7 0.5 %collective-permute-start.3 = (bf16[5,16,640]{2,1,0:T(8,128)(2,1)S(1)}, bf16[5,16,640]{2,1,0:T(8,128)(2,1)S(1)}, u32[]{:S(2)}, u32[]{:S(2)}) collective-permute-start(bf16[5,16,640]{2,1,0:T(8,128)(2,1)S(1)} %get-tuple-element.34), channel_id=1, source_target_pairs={{0,2},{1,3},{2,0},{3,1},{4,6},{5,7},{6,4},{7,5},{8,10},{9,11},{10,... | collective-permute-start | bytes 307208 | tf_op jit(solution)/shard_map/ppermute | solution.py:300
  26.2 2.6 %collective-permute-start.4 = (bf16[5,16,640]{2,1,0:T(8,128)(2,1)S(1)}, bf16[5,16,640]{2,1,0:T(8,128)(2,1)S(1)}, u32[]{:S(2)}, u32[]{:S(2)}) collective-permute-start(bf16[5,16,640]{2,1,0:T(8,128)(2,1)S(1)} %get-tuple-element.35), channel_id=1, source_target_pairs={{0,4},{1,5},{2,6},{3,7},{4,0},{5,1},{6,2},{7,3},{8,12},{9,13},{10,... | collective-permute-start | bytes 307208 | tf_op jit(solution)/shard_map/ppermute | solution.py:300
  28.8 0.0 collective-permute-done.6.refs_1_
  28.8 0.5 %collective-permute-start.5 = (bf16[5,16,640]{2,1,0:T(8,128)(2,1)S(1)}, bf16[5,16,640]{2,1,0:T(8,128)(2,1)S(1)}, u32[]{:S(2)}, u32[]{:S(2)}) collective-permute-start(bf16[5,16,640]{2,1,0:T(8,128)(2,1)S(1)} %get-tuple-element.36), channel_id=1, source_target_pairs={{0,6},{1,7},{2,4},{3,5},{4,2},{5,3},{6,0},{7,1},{8,14},{9,15},{10,... | collective-permute-start | bytes 307208 | tf_op jit(solution)/shard_map/ppermute | solution.py:300
  29.3 1.2 %collective-permute-done.7.refs_2_ = bf16[2,5,16,384]{3,2,1,0:T(8,128)(2,1)S(1)} collective-permute-done((bf16[2,5,16,384]{3,2,1,0:T(8,128)(2,1)S(1)}, bf16[2,5,16,384]{3,2,1,0:T(8,128)(2,1)S(1)}, u32[]{:S(2)}, u32[]{:S(2)}) %collective-permute-start.7) | collective-permute-done | bytes 122912 | tf_op jit(solution)/shard_map/ppermute | solution.py:300
  30.5 5.5 %collective-permute-done.8.refs_3_ = bf16[2,5,16,384]{3,2,1,0:T(8,128)(2,1)S(1)} collective-permute-done((bf16[2,5,16,384]{3,2,1,0:T(8,128)(2,1)S(1)}, bf16[2,5,16,384]{3,2,1,0:T(8,128)(2,1)S(1)}, u32[]{:S(2)}, u32[]{:S(2)}) %collective-permute-start.8) | collective-permute-done | bytes 122912 | tf_op jit(solution)/shard_map/ppermute | solution.py:300
  36.0 0.2 merge.3
  36.2 0.1 collective-permute-start.9
  36.2 4.2 %collective-permute-done.9.refs_5_ = bf16[5,16,384]{2,1,0:T(8,128)(2,1)S(1)} collective-permute-done((bf16[5,16,384]{2,1,0:T(8,128)(2,1)S(1)}, bf16[5,16,384]{2,1,0:T(8,128)(2,1)S(1)}, u32[]{:S(2)}, u32[]{:S(2)}) %collective-permute-start.9) | collective-permute-done | bytes 61472 | tf_op jit(solution)/shard_map/ppermute | solution.py:300
  40.4 0.0 collective-permute-done.3.refs_1_
  40.4 0.0 collective-permute-done.4.refs_2_
  40.4 0.0 collective-permute-done.5.refs_3_
  40.5 0.8 %join.1 = bf16[3,16,1024]{2,1,0:T(8,128)(2,1)} custom-call(bf16[5,16,640]{2,1,0:T(8,128)(2,1)S(1)} %get-tuple-element.33.refs_0_, bf16[5,16,640]{2,1,0:T(8,128)(2,1)S(1)} %collective-permute-done.3.refs_1_, bf16[5,16,640]{2,1,0:T(8,128)(2,1)S(1)} %collective-permute-done.4.refs_2_, bf16[5,16,640]{2,1,0:T(8,128)(2,1)S(1)} %collective-permute-done.5.refs_3_, ...), custom_call_target="tpu_custom_call" | custom-call | tf_op jit(solution)/shard_map/join/pallas_call | solution.py:290
Async XLA Ops:
  0.0 4.4 %copy-start = (bf16[3,256,768]{2,1,0:T(8,128)(2,1)S(1)}, bf16[3,256,768]{2,1,0:T(8,128)(2,1)}, u32[]{:S(2)}) copy-start(bf16[3,256,768]{2,1,0:T(8,128)(2,1)} %constant.5.clone.cols_ref) | copy-start | bytes 3538948
  0.0 4.5 %copy-start.1 = (bf16[3,768,192]{2,1,0:T(8,128)(2,1)S(1)}, bf16[3,768,192]{2,1,0:T(8,128)(2,1)}, u32[]{:S(2)}) copy-start(bf16[3,768,192]{2,1,0:T(8,128)(2,1)} %constant.4.clone.rows_ref) | copy-start | bytes 2654212
  1.7 5.0 %collective-permute-start = (bf16[4,32,1024]{2,1,0:T(8,128)(2,1)S(1)}, bf16[4,32,1024]{2,1,0:T(8,128)(2,1)S(1)}, u32[]{:S(2)}, u32[]{:S(2)}) collective-permute-start(bf16[4,32,1024]{2,1,0:T(8,128)(2,1)S(1)} %get-tuple-element.27), channel_id=1, source_target_pairs={{0,8},{8,0},{16,24},{24,16},{1,9},{9,1},{17,25},{25,17},{2,10},{10... | collective-permute-start | bytes 786440 | tf_op jit(solution)/shard_map/ppermute | solution.py:313
  1.8 7.7 %copy-start.2 = (f32[4]{0:T(128)S(1)}, f32[4]{0:T(128)}, u32[]{:S(2)}) copy-start(f32[4]{0:T(128)} %gain_ref.1) | copy-start | bytes 52
  1.8 7.7 %collective-permute-start.1 = (bf16[4,32,1024]{2,1,0:T(8,128)(2,1)S(1)}, bf16[4,32,1024]{2,1,0:T(8,128)(2,1)S(1)}, u32[]{:S(2)}, u32[]{:S(2)}) collective-permute-start(bf16[4,32,1024]{2,1,0:T(8,128)(2,1)S(1)} %get-tuple-element.28), channel_id=1, source_target_pairs={{8,16},{16,8},{9,17},{17,9},{10,18},{18,10},{11,19},{19,11},{12,20... | collective-permute-start | bytes 786440 | tf_op jit(solution)/shard_map/ppermute | solution.py:315
  17.4 8.0 %collective-permute-start.2 = (bf16[4,5,16,640]{3,2,1,0:T(8,128)(2,1)S(1)}, bf16[4,5,16,640]{3,2,1,0:T(8,128)(2,1)S(1)}, u32[]{:S(2)}, u32[]{:S(2)}) collective-permute-start(bf16[4,5,16,640]{3,2,1,0:T(8,128)(2,1)S(1)} %get-tuple-element.32), channel_id=1, source_target_pairs={{0,1},{1,0},{2,3},{3,2},{4,5},{5,4},{6,7},{7,6},{8,9},{9,8},{10,11... | collective-permute-start | bytes 1228808 | tf_op jit(solution)/shard_map/ppermute | solution.py:300
  19.0 9.8 %collective-permute-start.6 = (bf16[2,5,16,384]{3,2,1,0:T(8,128)(2,1)S(1)}, bf16[2,5,16,384]{3,2,1,0:T(8,128)(2,1)S(1)}, u32[]{:S(2)}, u32[]{:S(2)}) collective-permute-start(bf16[2,5,16,384]{3,2,1,0:T(8,128)(2,1)S(1)} %get-tuple-element.38), channel_id=1, source_target_pairs={{0,2},{1,3},{2,0},{3,1},{4,6},{5,7},{6,4},{7,5},{8,10},{9,11},{10,... | collective-permute-start | bytes 368648 | tf_op jit(solution)/shard_map/ppermute | solution.py:300
  19.5 11.0 %collective-permute-start.7 = (bf16[2,5,16,384]{3,2,1,0:T(8,128)(2,1)S(1)}, bf16[2,5,16,384]{3,2,1,0:T(8,128)(2,1)S(1)}, u32[]{:S(2)}, u32[]{:S(2)}) collective-permute-start(bf16[2,5,16,384]{3,2,1,0:T(8,128)(2,1)S(1)} %get-tuple-element.39), channel_id=1, source_target_pairs={{0,4},{1,5},{2,6},{3,7},{4,0},{5,1},{6,2},{7,3},{8,12},{9,13},{10,... | collective-permute-start | bytes 368648 | tf_op jit(solution)/shard_map/ppermute | solution.py:300
  22.1 13.9 %collective-permute-start.8 = (bf16[2,5,16,384]{3,2,1,0:T(8,128)(2,1)S(1)}, bf16[2,5,16,384]{3,2,1,0:T(8,128)(2,1)S(1)}, u32[]{:S(2)}, u32[]{:S(2)}) collective-permute-start(bf16[2,5,16,384]{3,2,1,0:T(8,128)(2,1)S(1)} %get-tuple-element.40), channel_id=1, source_target_pairs={{0,6},{1,7},{2,4},{3,5},{4,2},{5,3},{6,0},{7,1},{8,14},{9,15},{10,... | collective-permute-start | bytes 368648 | tf_op jit(solution)/shard_map/ppermute | solution.py:300
  25.7 14.7 %collective-permute-start.3 = (bf16[5,16,640]{2,1,0:T(8,128)(2,1)S(1)}, bf16[5,16,640]{2,1,0:T(8,128)(2,1)S(1)}, u32[]{:S(2)}, u32[]{:S(2)}) collective-permute-start(bf16[5,16,640]{2,1,0:T(8,128)(2,1)S(1)} %get-tuple-element.34), channel_id=1, source_target_pairs={{0,2},{1,3},{2,0},{3,1},{4,6},{5,7},{6,4},{7,5},{8,10},{9,11},{10,... | collective-permute-start | bytes 307208 | tf_op jit(solution)/shard_map/ppermute | solution.py:300
  26.2 14.2 %collective-permute-start.4 = (bf16[5,16,640]{2,1,0:T(8,128)(2,1)S(1)}, bf16[5,16,640]{2,1,0:T(8,128)(2,1)S(1)}, u32[]{:S(2)}, u32[]{:S(2)}) collective-permute-start(bf16[5,16,640]{2,1,0:T(8,128)(2,1)S(1)} %get-tuple-element.35), channel_id=1, source_target_pairs={{0,4},{1,5},{2,6},{3,7},{4,0},{5,1},{6,2},{7,3},{8,12},{9,13},{10,... | collective-permute-start | bytes 307208 | tf_op jit(solution)/shard_map/ppermute | solution.py:300
  28.8 11.6 %collective-permute-start.5 = (bf16[5,16,640]{2,1,0:T(8,128)(2,1)S(1)}, bf16[5,16,640]{2,1,0:T(8,128)(2,1)S(1)}, u32[]{:S(2)}, u32[]{:S(2)}) collective-permute-start(bf16[5,16,640]{2,1,0:T(8,128)(2,1)S(1)} %get-tuple-element.36), channel_id=1, source_target_pairs={{0,6},{1,7},{2,4},{3,5},{4,2},{5,3},{6,0},{7,1},{8,14},{9,15},{10,... | collective-permute-start | bytes 307208 | tf_op jit(solution)/shard_map/ppermute | solution.py:300
  36.2 4.3 %collective-permute-start.9 = (bf16[5,16,384]{2,1,0:T(8,128)(2,1)S(1)}, bf16[5,16,384]{2,1,0:T(8,128)(2,1)S(1)}, u32[]{:S(2)}, u32[]{:S(2)}) collective-permute-start(bf16[5,16,384]{2,1,0:T(8,128)(2,1)S(1)} %get-tuple-element.42), channel_id=1, source_target_pairs={{0,1},{1,0},{2,3},{3,2},{4,5},{5,4},{6,7},{7,6},{8,9},{9,8},{10,11... | collective-permute-start | bytes 184328 | tf_op jit(solution)/shard_map/ppermute | solution.py:300

commit v4 on v2

v4 whole, which is shorter than its diff:
```python
import functools

import jax
import jax.numpy as jnp
import numpy as np
from jax import lax
from jax.experimental import pallas as pl
from jax.experimental.pallas import tpu as pltpu
from jax.sharding import PartitionSpec as P

LEVELS = 4
TAPS = (1, 4, 6, 4, 1)
HALO = 32
LANES = 128
WINDOW = 256
STEP = 192


def band_products(count):
    made = []
    whole = np.eye(count)
    for level in range(LEVELS):
        step = sum(tap * np.eye(count, k=(place - 2) * 2**level) for place, tap in enumerate(TAPS))
        whole = step @ whole
        made.append(whole)
    return made


def split_exact(matrix):
    high = matrix.astype(jnp.bfloat16).astype(matrix.dtype)
    return high, matrix - high


def row_matrices(image_rows, rows):
    bands = band_products(image_rows)

    def taps(lines, first, last):
        parts = []
        for level, band in enumerate(bands):
            high, low = split_exact(np.pad(band, ((0, 0), (HALO, HALO)))[lines, first + HALO : last + HALO])
            scale = 1.0 / 16 ** (level + 1)
            parts.append(high * scale)
            if level >= 2:
                parts.append(low * scale)
        return np.concatenate(parts, axis=0)

    inner = np.arange(HALO, rows - HALO)
    edge = np.concatenate([np.arange(HALO), np.arange(rows - HALO, rows)])
    starts = [tile * rows for tile in (0, 1, image_rows // rows - 1)]
    return (
        taps(rows + inner, rows, 2 * rows).astype(jnp.bfloat16),
        np.stack([taps(start + edge, start - HALO, start + rows + HALO) for start in starts]).astype(jnp.bfloat16),
    )


def windows_of(columns):
    count = (columns - WINDOW) // STEP + 1
    assert (count - 1) * STEP + WINDOW == columns
    inside = [STEP * k + HALO for k in range(1, count)]
    return list(zip([0] + inside, inside + [columns]))


def column_matrices(columns):
    split = [split_exact(band) for band in band_products(columns)]
    parts = [high / 16 ** (level + 1) for level, (high, _) in enumerate(split)]
    parts += [low / 16 ** (level + 1) for level, (_, low) in enumerate(split) if level >= 2]
    made = np.zeros((len(windows_of(columns)), len(parts), WINDOW, WINDOW))
    for k, (first, last) in enumerate(windows_of(columns)):
        inputs, outputs = np.arange(STEP * k, STEP * k + WINDOW), np.arange(first, last)
        for j, part in enumerate(parts):
            made[k, j][np.ix_(inputs % WINDOW, outputs % WINDOW)] = part[np.ix_(outputs, inputs)].T
    return made.astype(jnp.bfloat16)


def filters(columns, rows, tiles):
    inner, edge = row_matrices(rows * tiles, rows)
    parts = [column_matrices(columns).reshape(-1, WINDOW)]
    for part in (inner, *edge):
        parts.append(np.pad(part, ((0, 0), (0, WINDOW - part.shape[1]))))
    return np.concatenate(parts, axis=0)


def dot(left, right):
    return jnp.dot(left, right, preferred_element_type=jnp.float32)


def luminance_of(colours):
    red, green, blue = (colours[channel].astype(jnp.float32) for channel in range(3))
    return (0.299 * red + 0.587 * green + 0.114 * blue).astype(jnp.bfloat16)


def combine(states):
    states = [[part.astype(jnp.float32) for part in state] for state in states]
    peak = functools.reduce(jnp.maximum, [state[0] for state in states])
    weights = [state[1] * jnp.exp(state[0] - peak) for state in states]
    total = sum(weights[1:], weights[0])
    inverse = 1.0 / total
    colours = []
    for channel in range(2, 5):
        terms = [weight * state[channel] for weight, state in zip(weights, states)]
        colours.append(sum(terms[1:], terms[0]) * inverse)
    return [peak, total] + colours


def fetch_kernel(planes_ref, stack_ref, core_ref, far_ref, arrived):
    depth, _, rows, _ = planes_ref.shape
    odd = lax.axis_index("tile") % 2
    copies = []
    for part, (start, count) in enumerate(((0, HALO), (rows - HALO, HALO), (HALO, rows - 2 * HALO))):
        at = pl.ds(start, count)
        copies.append(pltpu.make_async_copy(planes_ref.at[:, :, at], stack_ref.at[:, :, at], arrived.at[part]))
        copies[-1].start()
    copies[0].wait()
    copies[1].wait()
    tail, head = rows - HALO, 0
    for out, start in ((core_ref, jnp.where(odd == 0, tail, head)), (far_ref, jnp.where(odd == 0, head, tail))):
        at = pl.ds(pl.multiple_of(start, HALO), HALO)
        for plane in range(depth):
            out[plane] = luminance_of([stack_ref[plane, channel, at] for channel in range(3)])
    copies[2].wait()


def fetch(planes):
    depth, _, _, columns = planes.shape
    vmem = pl.BlockSpec(memory_space=pltpu.VMEM)
    shapes = [planes.shape] + [(depth, HALO, columns)] * 2
    return pl.pallas_call(
        fetch_kernel,
        out_shape=[jax.ShapeDtypeStruct(shape, jnp.bfloat16) for shape in shapes],
        in_specs=[pl.BlockSpec(memory_space=pl.ANY)],
        out_specs=[vmem] * 3,
        scratch_shapes=[pltpu.SemaphoreType.DMA((3,))],
        compiler_params=pltpu.CompilerParams(vmem_limit_bytes=50 * 2**20),
        name="fetch",
    )(planes)


def lane_below(limit, rows):
    return lax.broadcasted_iota(jnp.int32, (rows, LANES), 1) < limit


def filter_rows(row_ref, reach, window_of, depth, columns, high, low):
    count = row_ref.shape[0] // 6
    below = lane_below(LANES // 2, count)
    for plane in range(depth):
        here = pl.ds(plane * count, count)
        smooth = [dot(row_ref[:, :reach], window_of(plane, pl.ds(at, WINDOW))) for at in range(0, columns, WINDOW)]
        for level, parts in enumerate(((0,), (1,), (2, 3), (4, 5))):
            value = [sum(field[k * count : (k + 1) * count] for k in parts) for field in smooth]
            value = [half for field in value for half in (field[:, :LANES], field[:, LANES:])]
            for window in range(len(windows_of(columns))):
                first, mixed = divmod(STEP * window, LANES)
                for group in (first, first + 1):
                    line = value[group]
                    if mixed and group == first:
                        line = jnp.where(below, value[group + 2], line)
                    at = pl.ds(window * WINDOW + group % 2 * LANES, LANES)
                    top = line.astype(jnp.bfloat16)
                    high[level, here, at] = top
                    low[level, here, at] = (line - top.astype(jnp.float32)).astype(jnp.bfloat16)


def smooth_window(window, col_ref, high, low):
    at = pl.ds(window * WINDOW, WINDOW)
    made = []
    for level in range(LEVELS):
        top, rest = high[level, :, at], low[level, :, at]
        taps = [col_ref[pl.ds((window * 6 + k) * WINDOW, WINDOW)] for k in ((level,) if level < 2 else (level, level + 2))]
        value = dot(top, taps[0]) + dot(rest, taps[0])
        if level >= 2:
            value = value + dot(top, taps[1])
        made.append(value)
    return made


def scores(columns, luminance_at, gain_ref, col_ref, high, low):
    before = None
    ends = windows_of(columns)
    for window, (_, end) in enumerate(ends):
        after = smooth_window(window, col_ref, high, low)
        start = 0 if window == 0 else ends[window - 1][1] // LANES
        for group in range(start, end // LANES):
            at = pl.ds(group * LANES, LANES)
            half = slice(group % 2 * LANES, (group % 2 + 1) * LANES)
            approx = luminance_at(at).astype(jnp.float32)
            approx = approx.reshape(-1, LANES)
            score = jnp.zeros(approx.shape, jnp.float32)
            border = 0 if window == 0 else ends[window - 1][1] - group * LANES
            for level in range(LEVELS):
                smoother = after[level][:, half]
                if border > 0:
                    smoother = jnp.where(lane_below(border, smoother.shape[0]), before[level][:, half], smoother)
                detail = approx - smoother
                score = score + gain_ref[level] * detail * detail
                approx = smoother
            yield at, score
        before = after


def state_of(score, colours):
    peak = jnp.max(score, axis=0).astype(jnp.bfloat16)
    weight = jnp.exp(score - peak.astype(jnp.float32)[None])
    total = jnp.sum(weight, axis=0)
    inverse = 1.0 / total
    means = [jnp.sum(weight * colour.astype(jnp.float32), axis=0) * inverse for colour in colours]
    return [peak, total.astype(jnp.bfloat16)] + [mean.astype(jnp.bfloat16) for mean in means]


def inner_kernel(
    gain_ref, planes_ref, taps_ref, lum_ref, row_ref, col_ref, state_ref, spread_ref, gain, inner, high, low, arrived
):
    depth, _, rows, columns = planes_ref.shape
    bands, _, share, _ = state_ref.shape
    count = rows - 2 * HALO
    tile, tiles = lax.axis_index("tile"), lax.axis_size("tile")
    tile_case = jnp.where(tile == 0, 0, jnp.where(tile == tiles - 1, 2, 1))
    lines, first = inner.shape[0], col_ref.shape[0]
    edge = pl.multiple_of(first + lines + tile_case * row_ref.shape[0], LANES)
    copies = []
    copies.append(pltpu.make_async_copy(gain_ref, gain, arrived.at[0]))
    copies[0].start()
    for start, target in ((first, inner), (0, col_ref), (edge, row_ref)):
        source = taps_ref.at[pl.ds(start, target.shape[0])]
        copies.append(pltpu.make_async_copy(source, target, arrived.at[len(copies)]))
        copies[-1].start()
    for plane in range(depth):
        lum_ref[plane] = luminance_of([planes_ref[plane, channel] for channel in range(3)])
    copies[1].wait()
    filter_rows(inner, rows, lambda plane, at: lum_ref[plane, :, at], depth, columns, high, low)
    copies[0].wait()
    for level in range(LEVELS):
        spread_ref[level] = jnp.full((1, LANES), gain[level], jnp.float32)
    copies[2].wait()
    inside = pl.ds(HALO, count)
    for at, score in scores(columns, lambda at: lum_ref[:, inside, at], gain, col_ref, high, low):
        colours = [planes_ref[:, channel, inside, at] for channel in range(3)]
        for k, part in enumerate(state_of(score.reshape(depth, count, LANES), colours)):
            state_ref[:, k, :, at] = part.reshape(bands, share, LANES)
    copies[3].wait()


def inner_state(planes, level_gain, groups, tiles):
    depth, channels, rows, columns = planes.shape
    count, share = rows - 2 * HALO, rows // groups
    taps = jnp.asarray(filters(columns, rows, tiles))
    inner_lines, edge_lines = 6 * count, 12 * HALO
    vmem = pl.BlockSpec(memory_space=pltpu.VMEM)
    window_lines = taps.shape[0] - inner_lines - 3 * edge_lines
    shapes = [(depth, rows, columns), (edge_lines, WINDOW), (window_lines, WINDOW), (count // share, 5, share, columns)]
    wide = len(windows_of(columns)) * WINDOW
    return pl.pallas_call(
        inner_kernel,
        out_shape=[jax.ShapeDtypeStruct(shape, jnp.bfloat16) for shape in shapes]
        + [jax.ShapeDtypeStruct((LEVELS, 1, LANES), jnp.float32)],
        in_specs=[pl.BlockSpec(memory_space=pl.ANY), vmem, pl.BlockSpec(memory_space=pl.ANY)],
        out_specs=[vmem] * (len(shapes) + 1),
        scratch_shapes=[
            pltpu.SMEM((LEVELS,), jnp.float32),
            pltpu.VMEM((inner_lines, WINDOW), jnp.bfloat16),
            pltpu.VMEM((LEVELS, depth * count, wide), jnp.bfloat16),
            pltpu.VMEM((LEVELS, depth * count, wide), jnp.bfloat16),
            pltpu.SemaphoreType.DMA((4,)),
        ],
        compiler_params=pltpu.CompilerParams(vmem_limit_bytes=43 * 2**20),
        cost_estimate=pl.CostEstimate(flops=2**30, bytes_accessed=10 * 2**20, transcendentals=0),
        name="inner_state",
    )(level_gain, planes, taps)


def edge_state_kernel(slow, planes_ref, lum_ref, row_ref, col_ref, inner_ref, gain_ref, core_ref, far_ref, *refs):
    *outs, halo, high, low, held = refs
    depth, _, rows, columns = planes_ref.shape
    groups, _, share, _ = held.shape
    fast = groups // slow
    split = outs[0].shape[-1]
    odd = lax.axis_index("tile") % 2

    def place_halo(above_ref, below_ref):
        halo[0] = above_ref[...]
        halo[1] = below_ref[...]

    pl.when(odd == 0)(lambda: place_halo(far_ref, core_ref))
    pl.when(odd == 1)(lambda: place_halo(core_ref, far_ref))

    def window_of(plane, at):
        return jnp.concatenate([halo[0, plane, :, at], lum_ref[plane, :, at], halo[1, plane, :, at]], axis=0)

    def edges_of(ref, *index):
        return jnp.concatenate([ref[index[:-1] + (pl.ds(start, HALO), index[-1])] for start in (0, rows - HALO)], axis=-2)

    filter_rows(row_ref, rows + 2 * HALO, window_of, depth, columns, high, low)
    side = HALO // share
    held[side : groups - side] = inner_ref[...]
    for at, score in scores(columns, lambda at: edges_of(lum_ref, slice(None), at), gain_ref, col_ref, high, low):
        colours = [edges_of(planes_ref, slice(None), channel, at) for channel in range(3)]
        for k, part in enumerate(state_of(score.reshape(depth, 2 * HALO, LANES), colours)):
            held[:side, k, :, at] = part[:HALO].reshape(side, share, LANES)
            held[groups - side :, k, :, at] = part[HALO:].reshape(side, share, LANES)

    group = lax.axis_index("gz")
    mine_slow, mine_fast = group // fast, group % fast
    for other in range(fast):
        for place in range(slow):
            outs[other][place] = held[place * fast + (mine_fast ^ other), :, :, :split]
    for other in range(slow):
        for place in range(fast):
            outs[fast + other][place] = held[(mine_slow ^ other) * fast + place, :, :, split:]


def edge_state(planes, inner, core, far, slow, groups, split):
    depth, _, rows, columns = planes.shape
    fast, share = groups // slow, rows // groups
    vmem = pl.BlockSpec(memory_space=pltpu.VMEM)
    wide = len(windows_of(columns)) * WINDOW
    shapes = [(slow, 5, share, split)] * fast + [(fast, 5, share, columns - split)] * slow
    return pl.pallas_call(
        functools.partial(edge_state_kernel, slow),
        out_shape=[jax.ShapeDtypeStruct(shape, jnp.bfloat16) for shape in shapes],
        in_specs=[vmem] * 8,
        out_specs=[vmem] * len(shapes),
        scratch_shapes=[
            pltpu.VMEM((2, depth, HALO, columns), jnp.bfloat16),
            pltpu.VMEM((LEVELS, 2 * depth * HALO, wide), jnp.bfloat16),
            pltpu.VMEM((LEVELS, 2 * depth * HALO, wide), jnp.bfloat16),
            pltpu.VMEM((groups, 5, share, columns), jnp.bfloat16),
        ],
        compiler_params=pltpu.CompilerParams(vmem_limit_bytes=40 * 2**20),
        name="edge_state",
    )(planes, *inner, core, far)


def merge_kernel(count, pick, *refs):
    states, outs, held = refs[:count], refs[count:-1], refs[-1]
    for place in range(held.shape[0]):
        for k, part in enumerate(combine([[state[place, k] for k in range(5)] for state in states])):
            held[place, k] = part.astype(jnp.bfloat16)
    place = pick(lax.axis_index("gz"))
    for other, out in enumerate(outs):
        out[...] = held[place ^ other]


def merge(states, pick):
    bands, _, share, columns = states[0].shape
    return pl.pallas_call(
        functools.partial(merge_kernel, len(states), pick),
        out_shape=[jax.ShapeDtypeStruct((5, share, columns), jnp.bfloat16)] * bands,
        scratch_shapes=[pltpu.VMEM(states[0].shape, jnp.bfloat16)],
        compiler_params=pltpu.CompilerParams(vmem_limit_bytes=16 * 2**20),
        name="merge",
    )(*states)


def join_kernel(counts, *refs):
    *refs, out_ref = refs
    start = 0
    for count in counts:
        states, refs = refs[:count], refs[count:]
        width = states[0].shape[-1]
        merged = combine([[state[k] for k in range(5)] for state in states])
        for channel in range(3):
            out_ref[channel, :, start : start + width] = merged[2 + channel].astype(jnp.bfloat16)
        start += width


def join(*parts):
    share = parts[0][0].shape[1]
    columns = sum(part[0].shape[2] for part in parts)
    return pl.pallas_call(
        functools.partial(join_kernel, [len(part) for part in parts]),
        out_shape=jax.ShapeDtypeStruct((3, share, columns), jnp.bfloat16),
        compiler_params=pltpu.CompilerParams(vmem_limit_bytes=16 * 2**20),
        name="join",
    )(*[state for part in parts for state in part])


def swap(states, groups, step):
    moved = [
        lax.ppermute(state, "gz", [(i, i ^ (k * step)) for i in range(groups)]) for k, state in enumerate(states) if k
    ]
    return [states[0]] + moved


def per_device(planes, level_gain):
    columns = planes.shape[3]
    tiles = lax.axis_size("tile")
    groups = lax.axis_size("gz")
    slow = min(4, groups)
    fast = groups // slow
    split = 5 * columns // 8
    stack, to_core, to_far = fetch(planes)
    core = lax.ppermute(to_core, "tile", [(i, i ^ 1) for i in range(tiles)])
    between = range(1, tiles - 1, 2)
    far = lax.ppermute(to_far, "tile", [(i, i + 1) for i in between] + [(i + 1, i) for i in between])
    inner = inner_state(stack, level_gain, groups, tiles)
    states = edge_state(stack, inner, core, far, slow, groups, split)
    first = swap(states[:fast], groups, 1)
    second = swap(states[fast:], groups, fast)
    first = swap(merge(first, lambda group: group // fast), groups, fast)
    second = swap(merge(second, lambda group: group % fast), groups, 1)
    return join(first, second)


def solution(mesh):
    return jax.shard_map(
        per_device,
        mesh=mesh,
        in_specs=(P("gz", None, "tile", None), P()),
        out_specs=P(None, ("tile", "gz"), None),
        check_vma=False,
    )
```

time: 48.9 us -> 39.5 us (0.81)
  local copies, waits for them, and re-layouts: 5.08 us -> 0.65 us
  waiting for transfers between devices: 14.9 us -> 12 us
  starting transfers between devices: 16.8 us -> 14.9 us
  other arithmetic: 1.66 us -> 0 us
  Pallas kernels: 9.76 us -> 11.4 us
    unnamed x8 -> x2, local copies, waits for them, and re-layouts: 5.08 us -> 0.65 us
    ppermute x2, waiting for transfers between devices: 3.29 us -> 0.01 us  [the longest x1 0.01 us: per_device(): lax.ppermute(to_far, 'tile', [(i, i + 1) for i in between] + [(i + 1, i)...]
    ppermute x2, starting transfers between devices: 6.43 us -> 4.59 us  [the longest x1 4.47 us: per_device(): lax.ppermute(to_far, 'tile', [(i, i + 1) for i in between] + [(i + 1, i)...]
    pallas_call x1 -> x3, Pallas kernels: 8.57 us -> 10.2 us  [the longest x1 4.67 us: inner_state(): pl.pallas_call(inner_kernel, out_shape=[jax.ShapeDtypeStruct(shape, jnp.b...]
    add x1 -> x0, other arithmetic: 1.66 us -> none  [luminance_of(): return (0.299 * red + 0.587 * green + 0.114 * blue).astype(jnp.bfloat16)]
  transfers between devices with their start and end apart: 10 -> 10, of which waited for: 5 -> 3; matrix products, arithmetic and copies ran while one was open for 0% -> 0% of each run, Pallas kernels for 1% -> 13%
where the time goes in v4:
time: 39.5 us; the launch traced here: 39.1 us
  starting transfers between devices  14.9 us (38%)
  waiting for transfers between devices  12 us (30%)
  Pallas kernels  11.4 us (29%)
  local copies, waits for them, and re-layouts  0.65 us (2%)
    ppermute x8, waiting for transfers between devices, swap(): lax.ppermute(state, 'gz', [(i, i ^ k * step) for i in range(groups)])  12 us
    ppermute x8, starting transfers between devices, swap(): lax.ppermute(state, 'gz', [(i, i ^ k * step) for i in range(groups)])  10.3 us
    pallas_call x1, Pallas kernels, inner_state(): pl.pallas_call(inner_kernel, out_shape=[jax.ShapeDtypeStruct(shape, jnp.b...  4.67 us
    ppermute x1, starting transfers between devices, per_device(): lax.ppermute(to_far, 'tile', [(i, i + 1) for i in between] + [(i + 1, i)...  4.47 us
    pallas_call x1, Pallas kernels, edge_state(): pl.pallas_call(functools.partial(edge_state_kernel, slow), out_shape=[jax...  3.67 us
    pallas_call x1, Pallas kernels, fetch(): pl.pallas_call(fetch_kernel, out_shape=[jax.ShapeDtypeStruct(shape, jnp.b...  1.92 us
  transfers between devices with their start and end apart: 10, of which 3 were waited for; matrix products, arithmetic and copies ran while one was open for 0% of the time, Pallas kernels for 13%

profile of v4, /device:TPU:1, one launch (start us, length us, event | category | flops | bytes accessed | tf_op | source)
XLA Modules:
  0.0 39.1 jit_solution(10710408604672241222)
XLA Ops:
  0.0 1.9 %fetch.1 = (bf16[4,3,128,1024]{3,2,1,0:T(8,128)(2,1)S(1)}, bf16[4,32,1024]{2,1,0:T(8,128)(2,1)S(1)}, bf16[4,32,1024]{2,1,0:T(8,128)(2,1)S(1)}) custom-call(bf16[4,3,128,1024]{3,2,1,0:T(8,128)(2,1)} %planes_ref.1), custom_call_target="tpu_custom_call" | custom-call | tf_op jit(solution)/shard_map/fetch/pallas_call | solution.py:127
  1.9 0.1 collective-permute-start
  2.0 4.5 %collective-permute-start.1 = (bf16[4,32,1024]{2,1,0:T(8,128)(2,1)S(1)}, bf16[4,32,1024]{2,1,0:T(8,128)(2,1)S(1)}, u32[]{:S(2)}, u32[]{:S(2)}) collective-permute-start(bf16[4,32,1024]{2,1,0:T(8,128)(2,1)S(1)} %get-tuple-element.32), channel_id=1, source_target_pairs={{8,16},{16,8},{9,17},{17,9},{10,18},{18,10},{11,19},{19,11},{12,20... | collective-permute-start | bytes 786440 | tf_op jit(solution)/shard_map/ppermute | solution.py:393
  6.5 0.0 copy-start
  6.5 0.6 %copy-done = f32[4]{0:T(128)S(1)} copy-done((f32[4]{0:T(128)S(1)}, f32[4]{0:T(128)}, u32[]{:S(2)}) %copy-start) | copy-done | bytes 40
  7.2 4.7 %inner_state.1 = (bf16[4,128,1024]{2,1,0:T(8,128)(2,1)S(1)}, bf16[384,256]{1,0:T(8,128)(2,1)S(1)}, bf16[7680,256]{1,0:T(8,128)(2,1)S(1)}, bf16[4,5,16,1024]{3,2,1,0:T(8,128)(2,1)S(1)}, f32[4,1,128]{2,1,0:T(1,128)S(1)}) custom-call(f32[4]{0:T(128)S(1)} %copy-done, bf16[4,3,128,1024]{3,2,1,0:T(8,128)(2,1)S(1)} %get-tuple-element.25.planes_ref, ...), custom_call_target="tpu_custom_call" | custom-call | flops 1073741824 | bytes 10485760 | tf_op jit(solution)/shard_map/inner_state/pallas_call | solution.py:251
  11.9 0.0 collective-permute-done.core_ref
  11.9 0.0 collective-permute-done.1.far_ref
  11.9 3.7 %edge_state.1 = (bf16[4,5,16,640]{3,2,1,0:T(8,128)(2,1)S(1)}, bf16[4,5,16,640]{3,2,1,0:T(8,128)(2,1)S(1)}, bf16[2,5,16,384]{3,2,1,0:T(8,128)(2,1)S(1)}, bf16[2,5...) custom-call(bf16[4,3,128,1024]{3,2,1,0:T(8,128)(2,1)S(1)} %get-tuple-element.25, ...), custom_call_target="tpu_custom_call" | custom-call | tf_op jit(solution)/shard_map/edge_state/pallas_call | solution.py:316
  15.6 1.3 %collective-permute-start.2 = (bf16[4,5,16,640]{3,2,1,0:T(8,128)(2,1)S(1)}, bf16[4,5,16,640]{3,2,1,0:T(8,128)(2,1)S(1)}, u32[]{:S(2)}, u32[]{:S(2)}) collective-permute-start(bf16[4,5,16,640]{3,2,1,0:T(8,128)(2,1)S(1)} %get-tuple-element.34), channel_id=1, source_target_pairs={{0,1},{1,0},{2,3},{3,2},{4,5},{5,4},{6,7},{7,6},{8,9},{9,8},{10,11... | collective-permute-start | bytes 1228808 | tf_op jit(solution)/shard_map/ppermute | solution.py:378
  16.9 1.3 %collective-permute-start.6 = (bf16[2,5,16,384]{3,2,1,0:T(8,128)(2,1)S(1)}, bf16[2,5,16,384]{3,2,1,0:T(8,128)(2,1)S(1)}, u32[]{:S(2)}, u32[]{:S(2)}) collective-permute-start(bf16[2,5,16,384]{3,2,1,0:T(8,128)(2,1)S(1)} %get-tuple-element.40), channel_id=1, source_target_pairs={{0,2},{1,3},{2,0},{3,1},{4,6},{5,7},{6,4},{7,5},{8,10},{9,11},{10,... | collective-permute-start | bytes 368648 | tf_op jit(solution)/shard_map/ppermute | solution.py:378
  18.2 2.3 %collective-permute-start.7 = (bf16[2,5,16,384]{3,2,1,0:T(8,128)(2,1)S(1)}, bf16[2,5,16,384]{3,2,1,0:T(8,128)(2,1)S(1)}, u32[]{:S(2)}, u32[]{:S(2)}) collective-permute-start(bf16[2,5,16,384]{3,2,1,0:T(8,128)(2,1)S(1)} %get-tuple-element.41), channel_id=1, source_target_pairs={{0,4},{1,5},{2,6},{3,7},{4,0},{5,1},{6,2},{7,3},{8,12},{9,13},{10,... | collective-permute-start | bytes 368648 | tf_op jit(solution)/shard_map/ppermute | solution.py:378
  20.5 0.0 collective-permute-start.8
  20.5 4.3 %collective-permute-done.2.refs_1_ = bf16[4,5,16,640]{3,2,1,0:T(8,128)(2,1)S(1)} collective-permute-done((bf16[4,5,16,640]{3,2,1,0:T(8,128)(2,1)S(1)}, bf16[4,5,16,640]{3,2,1,0:T(8,128)(2,1)S(1)}, u32[]{:S(2)}, u32[]{:S(2)}) %collective-permute-start.2) | collective-permute-done | bytes 409632 | tf_op jit(solution)/shard_map/ppermute | solution.py:378
  24.8 0.3 merge.2
  25.0 1.9 %collective-permute-start.3 = (bf16[5,16,640]{2,1,0:T(8,128)(2,1)S(1)}, bf16[5,16,640]{2,1,0:T(8,128)(2,1)S(1)}, u32[]{:S(2)}, u32[]{:S(2)}) collective-permute-start(bf16[5,16,640]{2,1,0:T(8,128)(2,1)S(1)} %get-tuple-element.36), channel_id=1, source_target_pairs={{0,2},{1,3},{2,0},{3,1},{4,6},{5,7},{6,4},{7,5},{8,10},{9,11},{10,... | collective-permute-start | bytes 307208 | tf_op jit(solution)/shard_map/ppermute | solution.py:378
  26.9 2.3 %collective-permute-start.4 = (bf16[5,16,640]{2,1,0:T(8,128)(2,1)S(1)}, bf16[5,16,640]{2,1,0:T(8,128)(2,1)S(1)}, u32[]{:S(2)}, u32[]{:S(2)}) collective-permute-start(bf16[5,16,640]{2,1,0:T(8,128)(2,1)S(1)} %get-tuple-element.37), channel_id=1, source_target_pairs={{0,4},{1,5},{2,6},{3,7},{4,0},{5,1},{6,2},{7,3},{8,12},{9,13},{10,... | collective-permute-start | bytes 307208 | tf_op jit(solution)/shard_map/ppermute | solution.py:378
  29.2 0.0 collective-permute-done.6.refs_1_
  29.2 0.0 collective-permute-start.5
  29.2 0.0 collective-permute-done.7.refs_2_
  29.2 0.0 collective-permute-done.8.refs_3_
  29.2 0.2 merge.3
  29.3 1.3 %collective-permute-start.9 = (bf16[5,16,384]{2,1,0:T(8,128)(2,1)S(1)}, bf16[5,16,384]{2,1,0:T(8,128)(2,1)S(1)}, u32[]{:S(2)}, u32[]{:S(2)}) collective-permute-start(bf16[5,16,384]{2,1,0:T(8,128)(2,1)S(1)} %get-tuple-element.44), channel_id=1, source_target_pairs={{0,1},{1,0},{2,3},{3,2},{4,5},{5,4},{6,7},{7,6},{8,9},{9,8},{10,11... | collective-permute-start | bytes 184328 | tf_op jit(solution)/shard_map/ppermute | solution.py:378
  30.6 2.3 %collective-permute-done.9.refs_5_ = bf16[5,16,384]{2,1,0:T(8,128)(2,1)S(1)} collective-permute-done((bf16[5,16,384]{2,1,0:T(8,128)(2,1)S(1)}, bf16[5,16,384]{2,1,0:T(8,128)(2,1)S(1)}, u32[]{:S(2)}, u32[]{:S(2)}) %collective-permute-start.9) | collective-permute-done | bytes 61472 | tf_op jit(solution)/shard_map/ppermute | solution.py:378
  32.9 0.0 collective-permute-done.3.refs_1_
  32.9 5.4 %collective-permute-done.4.refs_2_ = bf16[5,16,640]{2,1,0:T(8,128)(2,1)S(1)} collective-permute-done((bf16[5,16,640]{2,1,0:T(8,128)(2,1)S(1)}, bf16[5,16,640]{2,1,0:T(8,128)(2,1)S(1)}, u32[]{:S(2)}, u32[]{:S(2)}) %collective-permute-start.4) | collective-permute-done | bytes 102432 | tf_op jit(solution)/shard_map/ppermute | solution.py:378
  38.3 0.0 collective-permute-done.5.refs_3_
  38.3 0.8 %join.1 = bf16[3,16,1024]{2,1,0:T(8,128)(2,1)} custom-call(bf16[5,16,640]{2,1,0:T(8,128)(2,1)S(1)} %get-tuple-element.35.refs_0_, bf16[5,16,640]{2,1,0:T(8,128)(2,1)S(1)} %collective-permute-done.3.refs_1_, bf16[5,16,640]{2,1,0:T(8,128)(2,1)S(1)} %collective-permute-done.4.refs_2_, bf16[5,16,640]{2,1,0:T(8,128)(2,1)S(1)} %collective-permute-done.5.refs_3_, ...), custom_call_target="tpu_custom_call" | custom-call | tf_op jit(solution)/shard_map/join/pallas_call | solution.py:368
Async XLA Ops:
  1.9 9.9 %collective-permute-start = (bf16[4,32,1024]{2,1,0:T(8,128)(2,1)S(1)}, bf16[4,32,1024]{2,1,0:T(8,128)(2,1)S(1)}, u32[]{:S(2)}, u32[]{:S(2)}) collective-permute-start(bf16[4,32,1024]{2,1,0:T(8,128)(2,1)S(1)} %get-tuple-element.31), channel_id=1, source_target_pairs={{0,8},{8,0},{16,24},{24,16},{1,9},{9,1},{17,25},{25,17},{2,10},{10... | collective-permute-start | bytes 786440 | tf_op jit(solution)/shard_map/ppermute | solution.py:391
  2.0 9.8 %collective-permute-start.1 = (bf16[4,32,1024]{2,1,0:T(8,128)(2,1)S(1)}, bf16[4,32,1024]{2,1,0:T(8,128)(2,1)S(1)}, u32[]{:S(2)}, u32[]{:S(2)}) collective-permute-start(bf16[4,32,1024]{2,1,0:T(8,128)(2,1)S(1)} %get-tuple-element.32), channel_id=1, source_target_pairs={{8,16},{16,8},{9,17},{17,9},{10,18},{18,10},{11,19},{19,11},{12,20... | collective-permute-start | bytes 786440 | tf_op jit(solution)/shard_map/ppermute | solution.py:393
  6.5 0.7 %copy-start = (f32[4]{0:T(128)S(1)}, f32[4]{0:T(128)}, u32[]{:S(2)}) copy-start(f32[4]{0:T(128)} %gain_ref.1) | copy-start | bytes 52
  15.6 9.2 %collective-permute-start.2 = (bf16[4,5,16,640]{3,2,1,0:T(8,128)(2,1)S(1)}, bf16[4,5,16,640]{3,2,1,0:T(8,128)(2,1)S(1)}, u32[]{:S(2)}, u32[]{:S(2)}) collective-permute-start(bf16[4,5,16,640]{3,2,1,0:T(8,128)(2,1)S(1)} %get-tuple-element.34), channel_id=1, source_target_pairs={{0,1},{1,0},{2,3},{3,2},{4,5},{5,4},{6,7},{7,6},{8,9},{9,8},{10,11... | collective-permute-start | bytes 1228808 | tf_op jit(solution)/shard_map/ppermute | solution.py:378
  16.9 12.3 %collective-permute-start.6 = (bf16[2,5,16,384]{3,2,1,0:T(8,128)(2,1)S(1)}, bf16[2,5,16,384]{3,2,1,0:T(8,128)(2,1)S(1)}, u32[]{:S(2)}, u32[]{:S(2)}) collective-permute-start(bf16[2,5,16,384]{3,2,1,0:T(8,128)(2,1)S(1)} %get-tuple-element.40), channel_id=1, source_target_pairs={{0,2},{1,3},{2,0},{3,1},{4,6},{5,7},{6,4},{7,5},{8,10},{9,11},{10,... | collective-permute-start | bytes 368648 | tf_op jit(solution)/shard_map/ppermute | solution.py:378
  18.2 11.0 %collective-permute-start.7 = (bf16[2,5,16,384]{3,2,1,0:T(8,128)(2,1)S(1)}, bf16[2,5,16,384]{3,2,1,0:T(8,128)(2,1)S(1)}, u32[]{:S(2)}, u32[]{:S(2)}) collective-permute-start(bf16[2,5,16,384]{3,2,1,0:T(8,128)(2,1)S(1)} %get-tuple-element.41), channel_id=1, source_target_pairs={{0,4},{1,5},{2,6},{3,7},{4,0},{5,1},{6,2},{7,3},{8,12},{9,13},{10,... | collective-permute-start | bytes 368648 | tf_op jit(solution)/shard_map/ppermute | solution.py:378
  20.5 8.7 %collective-permute-start.8 = (bf16[2,5,16,384]{3,2,1,0:T(8,128)(2,1)S(1)}, bf16[2,5,16,384]{3,2,1,0:T(8,128)(2,1)S(1)}, u32[]{:S(2)}, u32[]{:S(2)}) collective-permute-start(bf16[2,5,16,384]{3,2,1,0:T(8,128)(2,1)S(1)} %get-tuple-element.42), channel_id=1, source_target_pairs={{0,6},{1,7},{2,4},{3,5},{4,2},{5,3},{6,0},{7,1},{8,14},{9,15},{10,... | collective-permute-start | bytes 368648 | tf_op jit(solution)/shard_map/ppermute | solution.py:378
  25.0 7.9 %collective-permute-start.3 = (bf16[5,16,640]{2,1,0:T(8,128)(2,1)S(1)}, bf16[5,16,640]{2,1,0:T(8,128)(2,1)S(1)}, u32[]{:S(2)}, u32[]{:S(2)}) collective-permute-start(bf16[5,16,640]{2,1,0:T(8,128)(2,1)S(1)} %get-tuple-element.36), channel_id=1, source_target_pairs={{0,2},{1,3},{2,0},{3,1},{4,6},{5,7},{6,4},{7,5},{8,10},{9,11},{10,... | collective-permute-start | bytes 307208 | tf_op jit(solution)/shard_map/ppermute | solution.py:378
  26.9 11.4 %collective-permute-start.4 = (bf16[5,16,640]{2,1,0:T(8,128)(2,1)S(1)}, bf16[5,16,640]{2,1,0:T(8,128)(2,1)S(1)}, u32[]{:S(2)}, u32[]{:S(2)}) collective-permute-start(bf16[5,16,640]{2,1,0:T(8,128)(2,1)S(1)} %get-tuple-element.37), channel_id=1, source_target_pairs={{0,4},{1,5},{2,6},{3,7},{4,0},{5,1},{6,2},{7,3},{8,12},{9,13},{10,... | collective-permute-start | bytes 307208 | tf_op jit(solution)/shard_map/ppermute | solution.py:378
  29.2 9.1 %collective-permute-start.5 = (bf16[5,16,640]{2,1,0:T(8,128)(2,1)S(1)}, bf16[5,16,640]{2,1,0:T(8,128)(2,1)S(1)}, u32[]{:S(2)}, u32[]{:S(2)}) collective-permute-start(bf16[5,16,640]{2,1,0:T(8,128)(2,1)S(1)} %get-tuple-element.38), channel_id=1, source_target_pairs={{0,6},{1,7},{2,4},{3,5},{4,2},{5,3},{6,0},{7,1},{8,14},{9,15},{10,... | collective-permute-start | bytes 307208 | tf_op jit(solution)/shard_map/ppermute | solution.py:378
  29.3 3.6 %collective-permute-start.9 = (bf16[5,16,384]{2,1,0:T(8,128)(2,1)S(1)}, bf16[5,16,384]{2,1,0:T(8,128)(2,1)S(1)}, u32[]{:S(2)}, u32[]{:S(2)}) collective-permute-start(bf16[5,16,384]{2,1,0:T(8,128)(2,1)S(1)} %get-tuple-element.44), channel_id=1, source_target_pairs={{0,1},{1,0},{2,3},{3,2},{4,5},{5,4},{6,7},{7,6},{8,9},{9,8},{10,11... | collective-permute-start | bytes 184328 | tf_op jit(solution)/shard_map/ppermute | solution.py:378

commit v5 on v4

--- a/solution.py
+++ b/solution.py
@@ -131,6 +131,7 @@
         out_specs=[vmem] * 3,
         scratch_shapes=[pltpu.SemaphoreType.DMA((3,))],
         compiler_params=pltpu.CompilerParams(vmem_limit_bytes=50 * 2**20),
+        cost_estimate=pl.CostEstimate(flops=2**32, bytes_accessed=64 * 2**20, transcendentals=0),
         name="fetch",
     )(planes)
 

time: 39.5 us -> 39 us (0.987)
  local copies, waits for them, and re-layouts: 0.65 us -> 0.01 us
    unnamed x2, local copies, waits for them, and re-layouts: 0.65 us -> 0.01 us
where the time goes in v5:
time: 39 us; the launch traced here: 38.5 us
  starting transfers between devices  14.9 us (38%)
  waiting for transfers between devices  12 us (31%)
  Pallas kernels  11.5 us (29%)
    ppermute x8, waiting for transfers between devices, swap(): lax.ppermute(state, 'gz', [(i, i ^ k * step) for i in range(groups)])  12 us
    ppermute x8, starting transfers between devices, swap(): lax.ppermute(state, 'gz', [(i, i ^ k * step) for i in range(groups)])  10.3 us
    pallas_call x1, Pallas kernels, inner_state(): pl.pallas_call(inner_kernel, out_shape=[jax.ShapeDtypeStruct(shape, jnp.b...  4.67 us
    ppermute x1, starting transfers between devices, per_device(): lax.ppermute(to_far, 'tile', [(i, i + 1) for i in between] + [(i + 1, i)...  4.47 us
    pallas_call x1, Pallas kernels, edge_state(): pl.pallas_call(functools.partial(edge_state_kernel, slow), out_shape=[jax...  3.67 us
    pallas_call x1, Pallas kernels, fetch(): pl.pallas_call(fetch_kernel, out_shape=[jax.ShapeDtypeStruct(shape, jnp.b...  1.93 us
  transfers between devices with their start and end apart: 10, of which 3 were waited for; matrix products, arithmetic and copies ran while one was open for 0% of the time, Pallas kernels for 13%

profile of v5, /device:TPU:1, one launch (start us, length us, event | category | flops | bytes accessed | tf_op | source)
XLA Modules:
  0.0 38.5 jit_solution(5307078286080726591)
XLA Ops:
  0.0 0.0 copy-start
  0.0 1.9 %fetch.1 = (bf16[4,3,128,1024]{3,2,1,0:T(8,128)(2,1)S(1)}, bf16[4,32,1024]{2,1,0:T(8,128)(2,1)S(1)}, bf16[4,32,1024]{2,1,0:T(8,128)(2,1)S(1)}) custom-call(bf16[4,3,128,1024]{3,2,1,0:T(8,128)(2,1)} %planes_ref.1), custom_call_target="tpu_custom_call" | custom-call | flops 4294967296 | bytes 67108864 | tf_op jit(solution)/shard_map/fetch/pallas_call | solution.py:127
  1.9 0.1 collective-permute-start
  2.1 4.5 %collective-permute-start.1 = (bf16[4,32,1024]{2,1,0:T(8,128)(2,1)S(1)}, bf16[4,32,1024]{2,1,0:T(8,128)(2,1)S(1)}, u32[]{:S(2)}, u32[]{:S(2)}) collective-permute-start(bf16[4,32,1024]{2,1,0:T(8,128)(2,1)S(1)} %get-tuple-element.32), channel_id=1, source_target_pairs={{8,16},{16,8},{9,17},{17,9},{10,18},{18,10},{11,19},{19,11},{12,20... | collective-permute-start | bytes 786440 | tf_op jit(solution)/shard_map/ppermute | solution.py:394
  6.5 0.0 copy-done
  6.5 4.7 %inner_state.1 = (bf16[4,128,1024]{2,1,0:T(8,128)(2,1)S(1)}, bf16[384,256]{1,0:T(8,128)(2,1)S(1)}, bf16[7680,256]{1,0:T(8,128)(2,1)S(1)}, bf16[4,5,16,1024]{3,2,1,0:T(8,128)(2,1)S(1)}, f32[4,1,128]{2,1,0:T(1,128)S(1)}) custom-call(f32[4]{0:T(128)S(1)} %copy-done, bf16[4,3,128,1024]{3,2,1,0:T(8,128)(2,1)S(1)} %get-tuple-element.25.planes_ref, ...), custom_call_target="tpu_custom_call" | custom-call | flops 1073741824 | bytes 10485760 | tf_op jit(solution)/shard_map/inner_state/pallas_call | solution.py:252
  11.2 0.0 collective-permute-done.core_ref
  11.2 0.0 collective-permute-done.1.far_ref
  11.2 3.7 %edge_state.1 = (bf16[4,5,16,640]{3,2,1,0:T(8,128)(2,1)S(1)}, bf16[4,5,16,640]{3,2,1,0:T(8,128)(2,1)S(1)}, bf16[2,5,16,384]{3,2,1,0:T(8,128)(2,1)S(1)}, bf16[2,5...) custom-call(bf16[4,3,128,1024]{3,2,1,0:T(8,128)(2,1)S(1)} %get-tuple-element.25, ...), custom_call_target="tpu_custom_call" | custom-call | tf_op jit(solution)/shard_map/edge_state/pallas_call | solution.py:317
  14.9 1.3 %collective-permute-start.2 = (bf16[4,5,16,640]{3,2,1,0:T(8,128)(2,1)S(1)}, bf16[4,5,16,640]{3,2,1,0:T(8,128)(2,1)S(1)}, u32[]{:S(2)}, u32[]{:S(2)}) collective-permute-start(bf16[4,5,16,640]{3,2,1,0:T(8,128)(2,1)S(1)} %get-tuple-element.34), channel_id=1, source_target_pairs={{0,1},{1,0},{2,3},{3,2},{4,5},{5,4},{6,7},{7,6},{8,9},{9,8},{10,11... | collective-permute-start | bytes 1228808 | tf_op jit(solution)/shard_map/ppermute | solution.py:379
  16.2 1.3 %collective-permute-start.6 = (bf16[2,5,16,384]{3,2,1,0:T(8,128)(2,1)S(1)}, bf16[2,5,16,384]{3,2,1,0:T(8,128)(2,1)S(1)}, u32[]{:S(2)}, u32[]{:S(2)}) collective-permute-start(bf16[2,5,16,384]{3,2,1,0:T(8,128)(2,1)S(1)} %get-tuple-element.40), channel_id=1, source_target_pairs={{0,2},{1,3},{2,0},{3,1},{4,6},{5,7},{6,4},{7,5},{8,10},{9,11},{10,... | collective-permute-start | bytes 368648 | tf_op jit(solution)/shard_map/ppermute | solution.py:379
  17.5 2.3 %collective-permute-start.7 = (bf16[2,5,16,384]{3,2,1,0:T(8,128)(2,1)S(1)}, bf16[2,5,16,384]{3,2,1,0:T(8,128)(2,1)S(1)}, u32[]{:S(2)}, u32[]{:S(2)}) collective-permute-start(bf16[2,5,16,384]{3,2,1,0:T(8,128)(2,1)S(1)} %get-tuple-element.41), channel_id=1, source_target_pairs={{0,4},{1,5},{2,6},{3,7},{4,0},{5,1},{6,2},{7,3},{8,12},{9,13},{10,... | collective-permute-start | bytes 368648 | tf_op jit(solution)/shard_map/ppermute | solution.py:379
  19.9 0.0 collective-permute-start.8
  19.9 4.3 %collective-permute-done.2.refs_1_ = bf16[4,5,16,640]{3,2,1,0:T(8,128)(2,1)S(1)} collective-permute-done((bf16[4,5,16,640]{3,2,1,0:T(8,128)(2,1)S(1)}, bf16[4,5,16,640]{3,2,1,0:T(8,128)(2,1)S(1)}, u32[]{:S(2)}, u32[]{:S(2)}) %collective-permute-start.2) | collective-permute-done | bytes 409632 | tf_op jit(solution)/shard_map/ppermute | solution.py:379
  24.1 0.3 merge.2
  24.4 1.9 %collective-permute-start.3 = (bf16[5,16,640]{2,1,0:T(8,128)(2,1)S(1)}, bf16[5,16,640]{2,1,0:T(8,128)(2,1)S(1)}, u32[]{:S(2)}, u32[]{:S(2)}) collective-permute-start(bf16[5,16,640]{2,1,0:T(8,128)(2,1)S(1)} %get-tuple-element.36), channel_id=1, source_target_pairs={{0,2},{1,3},{2,0},{3,1},{4,6},{5,7},{6,4},{7,5},{8,10},{9,11},{10,... | collective-permute-start | bytes 307208 | tf_op jit(solution)/shard_map/ppermute | solution.py:379
  26.2 2.3 %collective-permute-start.4 = (bf16[5,16,640]{2,1,0:T(8,128)(2,1)S(1)}, bf16[5,16,640]{2,1,0:T(8,128)(2,1)S(1)}, u32[]{:S(2)}, u32[]{:S(2)}) collective-permute-start(bf16[5,16,640]{2,1,0:T(8,128)(2,1)S(1)} %get-tuple-element.37), channel_id=1, source_target_pairs={{0,4},{1,5},{2,6},{3,7},{4,0},{5,1},{6,2},{7,3},{8,12},{9,13},{10,... | collective-permute-start | bytes 307208 | tf_op jit(solution)/shard_map/ppermute | solution.py:379
  28.5 0.0 collective-permute-done.6.refs_1_
  28.5 0.0 collective-permute-start.5
  28.6 0.0 collective-permute-done.7.refs_2_
  28.6 0.0 collective-permute-done.8.refs_3_
  28.6 0.2 merge.3
  28.7 1.3 %collective-permute-start.9 = (bf16[5,16,384]{2,1,0:T(8,128)(2,1)S(1)}, bf16[5,16,384]{2,1,0:T(8,128)(2,1)S(1)}, u32[]{:S(2)}, u32[]{:S(2)}) collective-permute-start(bf16[5,16,384]{2,1,0:T(8,128)(2,1)S(1)} %get-tuple-element.44), channel_id=1, source_target_pairs={{0,1},{1,0},{2,3},{3,2},{4,5},{5,4},{6,7},{7,6},{8,9},{9,8},{10,11... | collective-permute-start | bytes 184328 | tf_op jit(solution)/shard_map/ppermute | solution.py:379
  30.0 2.3 %collective-permute-done.9.refs_5_ = bf16[5,16,384]{2,1,0:T(8,128)(2,1)S(1)} collective-permute-done((bf16[5,16,384]{2,1,0:T(8,128)(2,1)S(1)}, bf16[5,16,384]{2,1,0:T(8,128)(2,1)S(1)}, u32[]{:S(2)}, u32[]{:S(2)}) %collective-permute-start.9) | collective-permute-done | bytes 61472 | tf_op jit(solution)/shard_map/ppermute | solution.py:379
  32.3 0.0 collective-permute-done.3.refs_1_
  32.3 5.4 %collective-permute-done.4.refs_2_ = bf16[5,16,640]{2,1,0:T(8,128)(2,1)S(1)} collective-permute-done((bf16[5,16,640]{2,1,0:T(8,128)(2,1)S(1)}, bf16[5,16,640]{2,1,0:T(8,128)(2,1)S(1)}, u32[]{:S(2)}, u32[]{:S(2)}) %collective-permute-start.4) | collective-permute-done | bytes 102432 | tf_op jit(solution)/shard_map/ppermute | solution.py:379
  37.7 0.0 collective-permute-done.5.refs_3_
  37.7 0.8 %join.1 = bf16[3,16,1024]{2,1,0:T(8,128)(2,1)} custom-call(bf16[5,16,640]{2,1,0:T(8,128)(2,1)S(1)} %get-tuple-element.35.refs_0_, bf16[5,16,640]{2,1,0:T(8,128)(2,1)S(1)} %collective-permute-done.3.refs_1_, bf16[5,16,640]{2,1,0:T(8,128)(2,1)S(1)} %collective-permute-done.4.refs_2_, bf16[5,16,640]{2,1,0:T(8,128)(2,1)S(1)} %collective-permute-done.5.refs_3_, ...), custom_call_target="tpu_custom_call" | custom-call | tf_op jit(solution)/shard_map/join/pallas_call | solution.py:369
Async XLA Ops:
  0.0 6.5 %copy-start = (f32[4]{0:T(128)S(1)}, f32[4]{0:T(128)}, u32[]{:S(2)}) copy-start(f32[4]{0:T(128)} %gain_ref.1) | copy-start | bytes 52
  1.9 9.3 %collective-permute-start = (bf16[4,32,1024]{2,1,0:T(8,128)(2,1)S(1)}, bf16[4,32,1024]{2,1,0:T(8,128)(2,1)S(1)}, u32[]{:S(2)}, u32[]{:S(2)}) collective-permute-start(bf16[4,32,1024]{2,1,0:T(8,128)(2,1)S(1)} %get-tuple-element.31), channel_id=1, source_target_pairs={{0,8},{8,0},{16,24},{24,16},{1,9},{9,1},{17,25},{25,17},{2,10},{10... | collective-permute-start | bytes 786440 | tf_op jit(solution)/shard_map/ppermute | solution.py:392
  2.1 9.2 %collective-permute-start.1 = (bf16[4,32,1024]{2,1,0:T(8,128)(2,1)S(1)}, bf16[4,32,1024]{2,1,0:T(8,128)(2,1)S(1)}, u32[]{:S(2)}, u32[]{:S(2)}) collective-permute-start(bf16[4,32,1024]{2,1,0:T(8,128)(2,1)S(1)} %get-tuple-element.32), channel_id=1, source_target_pairs={{8,16},{16,8},{9,17},{17,9},{10,18},{18,10},{11,19},{19,11},{12,20... | collective-permute-start | bytes 786440 | tf_op jit(solution)/shard_map/ppermute | solution.py:394
  14.9 9.2 %collective-permute-start.2 = (bf16[4,5,16,640]{3,2,1,0:T(8,128)(2,1)S(1)}, bf16[4,5,16,640]{3,2,1,0:T(8,128)(2,1)S(1)}, u32[]{:S(2)}, u32[]{:S(2)}) collective-permute-start(bf16[4,5,16,640]{3,2,1,0:T(8,128)(2,1)S(1)} %get-tuple-element.34), channel_id=1, source_target_pairs={{0,1},{1,0},{2,3},{3,2},{4,5},{5,4},{6,7},{7,6},{8,9},{9,8},{10,11... | collective-permute-start | bytes 1228808 | tf_op jit(solution)/shard_map/ppermute | solution.py:379
  16.2 12.3 %collective-permute-start.6 = (bf16[2,5,16,384]{3,2,1,0:T(8,128)(2,1)S(1)}, bf16[2,5,16,384]{3,2,1,0:T(8,128)(2,1)S(1)}, u32[]{:S(2)}, u32[]{:S(2)}) collective-permute-start(bf16[2,5,16,384]{3,2,1,0:T(8,128)(2,1)S(1)} %get-tuple-element.40), channel_id=1, source_target_pairs={{0,2},{1,3},{2,0},{3,1},{4,6},{5,7},{6,4},{7,5},{8,10},{9,11},{10,... | collective-permute-start | bytes 368648 | tf_op jit(solution)/shard_map/ppermute | solution.py:379
  17.5 11.0 %collective-permute-start.7 = (bf16[2,5,16,384]{3,2,1,0:T(8,128)(2,1)S(1)}, bf16[2,5,16,384]{3,2,1,0:T(8,128)(2,1)S(1)}, u32[]{:S(2)}, u32[]{:S(2)}) collective-permute-start(bf16[2,5,16,384]{3,2,1,0:T(8,128)(2,1)S(1)} %get-tuple-element.41), channel_id=1, source_target_pairs={{0,4},{1,5},{2,6},{3,7},{4,0},{5,1},{6,2},{7,3},{8,12},{9,13},{10,... | collective-permute-start | bytes 368648 | tf_op jit(solution)/shard_map/ppermute | solution.py:379
  19.9 8.7 %collective-permute-start.8 = (bf16[2,5,16,384]{3,2,1,0:T(8,128)(2,1)S(1)}, bf16[2,5,16,384]{3,2,1,0:T(8,128)(2,1)S(1)}, u32[]{:S(2)}, u32[]{:S(2)}) collective-permute-start(bf16[2,5,16,384]{3,2,1,0:T(8,128)(2,1)S(1)} %get-tuple-element.42), channel_id=1, source_target_pairs={{0,6},{1,7},{2,4},{3,5},{4,2},{5,3},{6,0},{7,1},{8,14},{9,15},{10,... | collective-permute-start | bytes 368648 | tf_op jit(solution)/shard_map/ppermute | solution.py:379
  24.4 7.9 %collective-permute-start.3 = (bf16[5,16,640]{2,1,0:T(8,128)(2,1)S(1)}, bf16[5,16,640]{2,1,0:T(8,128)(2,1)S(1)}, u32[]{:S(2)}, u32[]{:S(2)}) collective-permute-start(bf16[5,16,640]{2,1,0:T(8,128)(2,1)S(1)} %get-tuple-element.36), channel_id=1, source_target_pairs={{0,2},{1,3},{2,0},{3,1},{4,6},{5,7},{6,4},{7,5},{8,10},{9,11},{10,... | collective-permute-start | bytes 307208 | tf_op jit(solution)/shard_map/ppermute | solution.py:379
  26.2 11.4 %collective-permute-start.4 = (bf16[5,16,640]{2,1,0:T(8,128)(2,1)S(1)}, bf16[5,16,640]{2,1,0:T(8,128)(2,1)S(1)}, u32[]{:S(2)}, u32[]{:S(2)}) collective-permute-start(bf16[5,16,640]{2,1,0:T(8,128)(2,1)S(1)} %get-tuple-element.37), channel_id=1, source_target_pairs={{0,4},{1,5},{2,6},{3,7},{4,0},{5,1},{6,2},{7,3},{8,12},{9,13},{10,... | collective-permute-start | bytes 307208 | tf_op jit(solution)/shard_map/ppermute | solution.py:379
  28.5 9.1 %collective-permute-start.5 = (bf16[5,16,640]{2,1,0:T(8,128)(2,1)S(1)}, bf16[5,16,640]{2,1,0:T(8,128)(2,1)S(1)}, u32[]{:S(2)}, u32[]{:S(2)}) collective-permute-start(bf16[5,16,640]{2,1,0:T(8,128)(2,1)S(1)} %get-tuple-element.38), channel_id=1, source_target_pairs={{0,6},{1,7},{2,4},{3,5},{4,2},{5,3},{6,0},{7,1},{8,14},{9,15},{10,... | collective-permute-start | bytes 307208 | tf_op jit(solution)/shard_map/ppermute | solution.py:379
  28.7 3.6 %collective-permute-start.9 = (bf16[5,16,384]{2,1,0:T(8,128)(2,1)S(1)}, bf16[5,16,384]{2,1,0:T(8,128)(2,1)S(1)}, u32[]{:S(2)}, u32[]{:S(2)}) collective-permute-start(bf16[5,16,384]{2,1,0:T(8,128)(2,1)S(1)} %get-tuple-element.44), channel_id=1, source_target_pairs={{0,1},{1,0},{2,3},{3,2},{4,5},{5,4},{6,7},{7,6},{8,9},{9,8},{10,11... | collective-permute-start | bytes 184328 | tf_op jit(solution)/shard_map/ppermute | solution.py:379

commit v6 on v5

--- a/solution.py
+++ b/solution.py
@@ -14,6 +14,7 @@
 LANES = 128
 WINDOW = 256
 STEP = 192
+FAR_FIRST = (3, 1, 2)
 
 
 def band_products(count):
@@ -374,10 +375,8 @@
     )(*[state for part in parts for state in part])
 
 
-def swap(states, groups, step):
-    moved = [
-        lax.ppermute(state, "gz", [(i, i ^ (k * step)) for i in range(groups)]) for k, state in enumerate(states) if k
-    ]
+def swap(states, groups, step, order):
+    moved = [lax.ppermute(states[k], "gz", [(i, i ^ (k * step)) for i in range(groups)]) for k in order]
     return [states[0]] + moved
 
 
@@ -394,10 +393,11 @@
     far = lax.ppermute(to_far, "tile", [(i, i + 1) for i in between] + [(i + 1, i) for i in between])
     inner = inner_state(stack, level_gain, groups, tiles)
     states = edge_state(stack, inner, core, far, slow, groups, split)
-    first = swap(states[:fast], groups, 1)
-    second = swap(states[fast:], groups, fast)
-    first = swap(merge(first, lambda group: group // fast), groups, fast)
-    second = swap(merge(second, lambda group: group % fast), groups, 1)
+    near = range(1, fast)
+    first = swap(states[:fast], groups, 1, near)
+    second = swap(states[fast:], groups, fast, FAR_FIRST)
+    first = swap(merge(first, lambda group: group // fast), groups, fast, range(1, slow))
+    second = swap(merge(second, lambda group: group % fast), groups, 1, near)
     return join(first, second)
 
 

time: 39 us -> 36.9 us (0.946); the launches traced: 38.5 us -> 36.8 us
  waiting for transfers between devices: 12 us -> 10.4 us
    ppermute x8, waiting for transfers between devices: 12 us -> 10.4 us  [swap(): lax.ppermute(states[k], 'gz', [(i, i ^ k * step) for i in range(groups)])]
  transfers between devices with their start and end apart: 10 -> 10, of which waited for: 3 -> 4; matrix products, arithmetic and copies ran while one was open for 0% -> 0% of each run, Pallas kernels for 13% -> 14%
where the time goes in v6:
time: 36.9 us; the launch traced here: 36.8 us
  starting transfers between devices  14.8 us (40%)
  Pallas kernels  11.5 us (31%)
  waiting for transfers between devices  10.4 us (28%)
    ppermute x8, waiting for transfers between devices, swap(): lax.ppermute(states[k], 'gz', [(i, i ^ k * step) for i in range(groups)])  10.4 us
    ppermute x8, starting transfers between devices, swap(): lax.ppermute(states[k], 'gz', [(i, i ^ k * step) for i in range(groups)])  10.2 us
    pallas_call x1, Pallas kernels, inner_state(): pl.pallas_call(inner_kernel, out_shape=[jax.ShapeDtypeStruct(shape, jnp.b...  4.67 us
    ppermute x1, starting transfers between devices, per_device(): lax.ppermute(to_far, 'tile', [(i, i + 1) for i in between] + [(i + 1, i)...  4.47 us
    pallas_call x1, Pallas kernels, edge_state(): pl.pallas_call(functools.partial(edge_state_kernel, slow), out_shape=[jax...  3.67 us
    pallas_call x1, Pallas kernels, fetch(): pl.pallas_call(fetch_kernel, out_shape=[jax.ShapeDtypeStruct(shape, jnp.b...  1.93 us
    pallas_call x1, Pallas kernels, join(): pl.pallas_call(functools.partial(join_kernel, [len(part) for part in part...  0.78 us
  transfers between devices with their start and end apart: 10, of which 4 were waited for; matrix products, arithmetic and copies ran while one was open for 0% of the time, Pallas kernels for 14%

profile of v6, /device:TPU:1, one launch (start us, length us, event | category | flops | bytes accessed | tf_op | source)
XLA Modules:
  0.0 36.8 jit_solution(1448185654602872962)
XLA Ops:
  0.0 0.0 copy-start
  0.0 1.9 %fetch.1 = (bf16[4,3,128,1024]{3,2,1,0:T(8,128)(2,1)S(1)}, bf16[4,32,1024]{2,1,0:T(8,128)(2,1)S(1)}, bf16[4,32,1024]{2,1,0:T(8,128)(2,1)S(1)}) custom-call(bf16[4,3,128,1024]{3,2,1,0:T(8,128)(2,1)} %planes_ref.1), custom_call_target="tpu_custom_call" | custom-call | flops 4294967296 | bytes 67108864 | tf_op jit(solution)/shard_map/fetch/pallas_call | solution.py:128
  1.9 0.1 collective-permute-start
  2.1 4.5 %collective-permute-start.1 = (bf16[4,32,1024]{2,1,0:T(8,128)(2,1)S(1)}, bf16[4,32,1024]{2,1,0:T(8,128)(2,1)S(1)}, u32[]{:S(2)}, u32[]{:S(2)}) collective-permute-start(bf16[4,32,1024]{2,1,0:T(8,128)(2,1)S(1)} %get-tuple-element.32), channel_id=1, source_target_pairs={{8,16},{16,8},{9,17},{17,9},{10,18},{18,10},{11,19},{19,11},{12,20... | collective-permute-start | bytes 786440 | tf_op jit(solution)/shard_map/ppermute | solution.py:393
  6.5 0.0 copy-done
  6.5 4.7 %inner_state.1 = (bf16[4,128,1024]{2,1,0:T(8,128)(2,1)S(1)}, bf16[384,256]{1,0:T(8,128)(2,1)S(1)}, bf16[7680,256]{1,0:T(8,128)(2,1)S(1)}, bf16[4,5,16,1024]{3,2,1,0:T(8,128)(2,1)S(1)}, f32[4,1,128]{2,1,0:T(1,128)S(1)}) custom-call(f32[4]{0:T(128)S(1)} %copy-done, bf16[4,3,128,1024]{3,2,1,0:T(8,128)(2,1)S(1)} %get-tuple-element.25.planes_ref, ...), custom_call_target="tpu_custom_call" | custom-call | flops 1073741824 | bytes 10485760 | tf_op jit(solution)/shard_map/inner_state/pallas_call | solution.py:253
  11.2 0.0 collective-permute-done.core_ref
  11.2 0.0 collective-permute-done.1.far_ref
  11.2 3.7 %edge_state.1 = (bf16[4,5,16,640]{3,2,1,0:T(8,128)(2,1)S(1)}, bf16[4,5,16,640]{3,2,1,0:T(8,128)(2,1)S(1)}, bf16[2,5,16,384]{3,2,1,0:T(8,128)(2,1)S(1)}, bf16[2,5...) custom-call(bf16[4,3,128,1024]{3,2,1,0:T(8,128)(2,1)S(1)} %get-tuple-element.25, ...), custom_call_target="tpu_custom_call" | custom-call | tf_op jit(solution)/shard_map/edge_state/pallas_call | solution.py:318
  14.9 1.3 %collective-permute-start.2 = (bf16[4,5,16,640]{3,2,1,0:T(8,128)(2,1)S(1)}, bf16[4,5,16,640]{3,2,1,0:T(8,128)(2,1)S(1)}, u32[]{:S(2)}, u32[]{:S(2)}) collective-permute-start(bf16[4,5,16,640]{3,2,1,0:T(8,128)(2,1)S(1)} %get-tuple-element.34), channel_id=1, source_target_pairs={{0,1},{1,0},{2,3},{3,2},{4,5},{5,4},{6,7},{7,6},{8,9},{9,8},{10,11... | collective-permute-start | bytes 1228808 | tf_op jit(solution)/shard_map/ppermute | solution.py:379
  16.2 3.3 %collective-permute-start.6 = (bf16[2,5,16,384]{3,2,1,0:T(8,128)(2,1)S(1)}, bf16[2,5,16,384]{3,2,1,0:T(8,128)(2,1)S(1)}, u32[]{:S(2)}, u32[]{:S(2)}) collective-permute-start(bf16[2,5,16,384]{3,2,1,0:T(8,128)(2,1)S(1)} %get-tuple-element.40), channel_id=1, source_target_pairs={{0,6},{1,7},{2,4},{3,5},{4,2},{5,3},{6,0},{7,1},{8,14},{9,15},{10,... | collective-permute-start | bytes 368648 | tf_op jit(solution)/shard_map/ppermute | solution.py:379
  19.6 0.0 collective-permute-start.7
  19.6 0.3 collective-permute-start.8
  19.9 4.3 %collective-permute-done.2.refs_1_ = bf16[4,5,16,640]{3,2,1,0:T(8,128)(2,1)S(1)} collective-permute-done((bf16[4,5,16,640]{3,2,1,0:T(8,128)(2,1)S(1)}, bf16[4,5,16,640]{3,2,1,0:T(8,128)(2,1)S(1)}, u32[]{:S(2)}, u32[]{:S(2)}) %collective-permute-start.2) | collective-permute-done | bytes 409632 | tf_op jit(solution)/shard_map/ppermute | solution.py:379
  24.1 0.3 merge.2
  24.4 1.9 %collective-permute-start.3 = (bf16[5,16,640]{2,1,0:T(8,128)(2,1)S(1)}, bf16[5,16,640]{2,1,0:T(8,128)(2,1)S(1)}, u32[]{:S(2)}, u32[]{:S(2)}) collective-permute-start(bf16[5,16,640]{2,1,0:T(8,128)(2,1)S(1)} %get-tuple-element.36), channel_id=1, source_target_pairs={{0,2},{1,3},{2,0},{3,1},{4,6},{5,7},{6,4},{7,5},{8,10},{9,11},{10,... | collective-permute-start | bytes 307208 | tf_op jit(solution)/shard_map/ppermute | solution.py:379
  26.2 2.3 %collective-permute-start.4 = (bf16[5,16,640]{2,1,0:T(8,128)(2,1)S(1)}, bf16[5,16,640]{2,1,0:T(8,128)(2,1)S(1)}, u32[]{:S(2)}, u32[]{:S(2)}) collective-permute-start(bf16[5,16,640]{2,1,0:T(8,128)(2,1)S(1)} %get-tuple-element.37), channel_id=1, source_target_pairs={{0,4},{1,5},{2,6},{3,7},{4,0},{5,1},{6,2},{7,3},{8,12},{9,13},{10,... | collective-permute-start | bytes 307208 | tf_op jit(solution)/shard_map/ppermute | solution.py:379
  28.5 0.0 collective-permute-done.6.refs_1_
  28.5 0.0 collective-permute-start.5
  28.6 0.0 collective-permute-done.7.refs_2_
  28.6 0.2 collective-permute-done.8.refs_3_
  28.7 0.2 merge.3
  28.9 1.2 %collective-permute-start.9 = (bf16[5,16,384]{2,1,0:T(8,128)(2,1)S(1)}, bf16[5,16,384]{2,1,0:T(8,128)(2,1)S(1)}, u32[]{:S(2)}, u32[]{:S(2)}) collective-permute-start(bf16[5,16,384]{2,1,0:T(8,128)(2,1)S(1)} %get-tuple-element.44), channel_id=1, source_target_pairs={{0,1},{1,0},{2,3},{3,2},{4,5},{5,4},{6,7},{7,6},{8,9},{9,8},{10,11... | collective-permute-start | bytes 184328 | tf_op jit(solution)/shard_map/ppermute | solution.py:379
  30.0 2.7 %collective-permute-done.9.refs_5_ = bf16[5,16,384]{2,1,0:T(8,128)(2,1)S(1)} collective-permute-done((bf16[5,16,384]{2,1,0:T(8,128)(2,1)S(1)}, bf16[5,16,384]{2,1,0:T(8,128)(2,1)S(1)}, u32[]{:S(2)}, u32[]{:S(2)}) %collective-permute-start.9) | collective-permute-done | bytes 61472 | tf_op jit(solution)/shard_map/ppermute | solution.py:379
  32.8 0.0 collective-permute-done.3.refs_1_
  32.8 3.2 %collective-permute-done.4.refs_2_ = bf16[5,16,640]{2,1,0:T(8,128)(2,1)S(1)} collective-permute-done((bf16[5,16,640]{2,1,0:T(8,128)(2,1)S(1)}, bf16[5,16,640]{2,1,0:T(8,128)(2,1)S(1)}, u32[]{:S(2)}, u32[]{:S(2)}) %collective-permute-start.4) | collective-permute-done | bytes 102432 | tf_op jit(solution)/shard_map/ppermute | solution.py:379
  36.0 0.0 collective-permute-done.5.refs_3_
  36.0 0.8 %join.1 = bf16[3,16,1024]{2,1,0:T(8,128)(2,1)} custom-call(bf16[5,16,640]{2,1,0:T(8,128)(2,1)S(1)} %get-tuple-element.35.refs_0_, bf16[5,16,640]{2,1,0:T(8,128)(2,1)S(1)} %collective-permute-done.3.refs_1_, bf16[5,16,640]{2,1,0:T(8,128)(2,1)S(1)} %collective-permute-done.4.refs_2_, bf16[5,16,640]{2,1,0:T(8,128)(2,1)S(1)} %collective-permute-done.5.refs_3_, ...), custom_call_target="tpu_custom_call" | custom-call | tf_op jit(solution)/shard_map/join/pallas_call | solution.py:370
Async XLA Ops:
  0.0 6.5 %copy-start = (f32[4]{0:T(128)S(1)}, f32[4]{0:T(128)}, u32[]{:S(2)}) copy-start(f32[4]{0:T(128)} %gain_ref.1) | copy-start | bytes 52
  1.9 9.3 %collective-permute-start = (bf16[4,32,1024]{2,1,0:T(8,128)(2,1)S(1)}, bf16[4,32,1024]{2,1,0:T(8,128)(2,1)S(1)}, u32[]{:S(2)}, u32[]{:S(2)}) collective-permute-start(bf16[4,32,1024]{2,1,0:T(8,128)(2,1)S(1)} %get-tuple-element.31), channel_id=1, source_target_pairs={{0,8},{8,0},{16,24},{24,16},{1,9},{9,1},{17,25},{25,17},{2,10},{10... | collective-permute-start | bytes 786440 | tf_op jit(solution)/shard_map/ppermute | solution.py:391
  2.1 9.2 %collective-permute-start.1 = (bf16[4,32,1024]{2,1,0:T(8,128)(2,1)S(1)}, bf16[4,32,1024]{2,1,0:T(8,128)(2,1)S(1)}, u32[]{:S(2)}, u32[]{:S(2)}) collective-permute-start(bf16[4,32,1024]{2,1,0:T(8,128)(2,1)S(1)} %get-tuple-element.32), channel_id=1, source_target_pairs={{8,16},{16,8},{9,17},{17,9},{10,18},{18,10},{11,19},{19,11},{12,20... | collective-permute-start | bytes 786440 | tf_op jit(solution)/shard_map/ppermute | solution.py:393
  14.9 9.2 %collective-permute-start.2 = (bf16[4,5,16,640]{3,2,1,0:T(8,128)(2,1)S(1)}, bf16[4,5,16,640]{3,2,1,0:T(8,128)(2,1)S(1)}, u32[]{:S(2)}, u32[]{:S(2)}) collective-permute-start(bf16[4,5,16,640]{3,2,1,0:T(8,128)(2,1)S(1)} %get-tuple-element.34), channel_id=1, source_target_pairs={{0,1},{1,0},{2,3},{3,2},{4,5},{5,4},{6,7},{7,6},{8,9},{9,8},{10,11... | collective-permute-start | bytes 1228808 | tf_op jit(solution)/shard_map/ppermute | solution.py:379
  16.2 12.3 %collective-permute-start.6 = (bf16[2,5,16,384]{3,2,1,0:T(8,128)(2,1)S(1)}, bf16[2,5,16,384]{3,2,1,0:T(8,128)(2,1)S(1)}, u32[]{:S(2)}, u32[]{:S(2)}) collective-permute-start(bf16[2,5,16,384]{3,2,1,0:T(8,128)(2,1)S(1)} %get-tuple-element.40), channel_id=1, source_target_pairs={{0,6},{1,7},{2,4},{3,5},{4,2},{5,3},{6,0},{7,1},{8,14},{9,15},{10,... | collective-permute-start | bytes 368648 | tf_op jit(solution)/shard_map/ppermute | solution.py:379
  19.6 9.0 %collective-permute-start.7 = (bf16[2,5,16,384]{3,2,1,0:T(8,128)(2,1)S(1)}, bf16[2,5,16,384]{3,2,1,0:T(8,128)(2,1)S(1)}, u32[]{:S(2)}, u32[]{:S(2)}) collective-permute-start(bf16[2,5,16,384]{3,2,1,0:T(8,128)(2,1)S(1)} %get-tuple-element.41), channel_id=1, source_target_pairs={{0,2},{1,3},{2,0},{3,1},{4,6},{5,7},{6,4},{7,5},{8,10},{9,11},{10,... | collective-permute-start | bytes 368648 | tf_op jit(solution)/shard_map/ppermute | solution.py:379
  19.6 9.2 %collective-permute-start.8 = (bf16[2,5,16,384]{3,2,1,0:T(8,128)(2,1)S(1)}, bf16[2,5,16,384]{3,2,1,0:T(8,128)(2,1)S(1)}, u32[]{:S(2)}, u32[]{:S(2)}) collective-permute-start(bf16[2,5,16,384]{3,2,1,0:T(8,128)(2,1)S(1)} %get-tuple-element.42), channel_id=1, source_target_pairs={{0,4},{1,5},{2,6},{3,7},{4,0},{5,1},{6,2},{7,3},{8,12},{9,13},{10,... | collective-permute-start | bytes 368648 | tf_op jit(solution)/shard_map/ppermute | solution.py:379
  24.4 8.4 %collective-permute-start.3 = (bf16[5,16,640]{2,1,0:T(8,128)(2,1)S(1)}, bf16[5,16,640]{2,1,0:T(8,128)(2,1)S(1)}, u32[]{:S(2)}, u32[]{:S(2)}) collective-permute-start(bf16[5,16,640]{2,1,0:T(8,128)(2,1)S(1)} %get-tuple-element.36), channel_id=1, source_target_pairs={{0,2},{1,3},{2,0},{3,1},{4,6},{5,7},{6,4},{7,5},{8,10},{9,11},{10,... | collective-permute-start | bytes 307208 | tf_op jit(solution)/shard_map/ppermute | solution.py:379
  26.2 9.8 %collective-permute-start.4 = (bf16[5,16,640]{2,1,0:T(8,128)(2,1)S(1)}, bf16[5,16,640]{2,1,0:T(8,128)(2,1)S(1)}, u32[]{:S(2)}, u32[]{:S(2)}) collective-permute-start(bf16[5,16,640]{2,1,0:T(8,128)(2,1)S(1)} %get-tuple-element.37), channel_id=1, source_target_pairs={{0,4},{1,5},{2,6},{3,7},{4,0},{5,1},{6,2},{7,3},{8,12},{9,13},{10,... | collective-permute-start | bytes 307208 | tf_op jit(solution)/shard_map/ppermute | solution.py:379
  28.5 7.5 %collective-permute-start.5 = (bf16[5,16,640]{2,1,0:T(8,128)(2,1)S(1)}, bf16[5,16,640]{2,1,0:T(8,128)(2,1)S(1)}, u32[]{:S(2)}, u32[]{:S(2)}) collective-permute-start(bf16[5,16,640]{2,1,0:T(8,128)(2,1)S(1)} %get-tuple-element.38), channel_id=1, source_target_pairs={{0,6},{1,7},{2,4},{3,5},{4,2},{5,3},{6,0},{7,1},{8,14},{9,15},{10,... | collective-permute-start | bytes 307208 | tf_op jit(solution)/shard_map/ppermute | solution.py:379
  28.9 3.9 %collective-permute-start.9 = (bf16[5,16,384]{2,1,0:T(8,128)(2,1)S(1)}, bf16[5,16,384]{2,1,0:T(8,128)(2,1)S(1)}, u32[]{:S(2)}, u32[]{:S(2)}) collective-permute-start(bf16[5,16,384]{2,1,0:T(8,128)(2,1)S(1)} %get-tuple-element.44), channel_id=1, source_target_pairs={{0,1},{1,0},{2,3},{3,2},{4,5},{5,4},{6,7},{7,6},{8,9},{9,8},{10,11... | collective-permute-start | bytes 184328 | tf_op jit(solution)/shard_map/ppermute | solution.py:379

commit v7 on v6

--- a/solution.py
+++ b/solution.py
@@ -168,9 +168,8 @@
     for level in range(LEVELS):
         top, rest = high[level, :, at], low[level, :, at]
         taps = [col_ref[pl.ds((window * 6 + k) * WINDOW, WINDOW)] for k in ((level,) if level < 2 else (level, level + 2))]
-        value = dot(top, taps[0]) + dot(rest, taps[0])
-        if level >= 2:
-            value = value + dot(top, taps[1])
+        lines, factors = [top, rest] + [top] * (level >= 2), [taps[0]] + taps
+        value = dot(jnp.concatenate(lines, axis=1), jnp.concatenate(factors, axis=0))
         made.append(value)
     return made
 

time: 36.9 us -> 37 us (level)
  no operation moved by 1% of the time
where the time goes in v7:
time: 37 us; the launch traced here: 36.8 us
  starting transfers between devices  14.8 us (40%)
  Pallas kernels  11.4 us (31%)
  waiting for transfers between devices  10.4 us (28%)
    ppermute x8, waiting for transfers between devices, swap(): lax.ppermute(states[k], 'gz', [(i, i ^ k * step) for i in range(groups)])  10.4 us
    ppermute x8, starting transfers between devices, swap(): lax.ppermute(states[k], 'gz', [(i, i ^ k * step) for i in range(groups)])  10.3 us
    pallas_call x1, Pallas kernels, inner_state(): pl.pallas_call(inner_kernel, out_shape=[jax.ShapeDtypeStruct(shape, jnp.b...  4.67 us
    ppermute x1, starting transfers between devices, per_device(): lax.ppermute(to_far, 'tile', [(i, i + 1) for i in between] + [(i + 1, i)...  4.47 us
    pallas_call x1, Pallas kernels, edge_state(): pl.pallas_call(functools.partial(edge_state_kernel, slow), out_shape=[jax...  3.66 us
    pallas_call x1, Pallas kernels, fetch(): pl.pallas_call(fetch_kernel, out_shape=[jax.ShapeDtypeStruct(shape, jnp.b...  1.93 us
    pallas_call x1, Pallas kernels, join(): pl.pallas_call(functools.partial(join_kernel, [len(part) for part in part...  0.78 us
  transfers between devices with their start and end apart: 10, of which 4 were waited for; matrix products, arithmetic and copies ran while one was open for 0% of the time, Pallas kernels for 14%

profile of v7, /device:TPU:1, one launch (start us, length us, event | category | flops | bytes accessed | tf_op | source)
XLA Modules:
  0.0 36.8 jit_solution(1034549066161610003)
XLA Ops:
  0.0 0.0 copy-start
  0.0 1.9 %fetch.1 = (bf16[4,3,128,1024]{3,2,1,0:T(8,128)(2,1)S(1)}, bf16[4,32,1024]{2,1,0:T(8,128)(2,1)S(1)}, bf16[4,32,1024]{2,1,0:T(8,128)(2,1)S(1)}) custom-call(bf16[4,3,128,1024]{3,2,1,0:T(8,128)(2,1)} %planes_ref.1), custom_call_target="tpu_custom_call" | custom-call | flops 4294967296 | bytes 67108864 | tf_op jit(solution)/shard_map/fetch/pallas_call | solution.py:128
  1.9 0.1 collective-permute-start
  2.1 4.5 %collective-permute-start.1 = (bf16[4,32,1024]{2,1,0:T(8,128)(2,1)S(1)}, bf16[4,32,1024]{2,1,0:T(8,128)(2,1)S(1)}, u32[]{:S(2)}, u32[]{:S(2)}) collective-permute-start(bf16[4,32,1024]{2,1,0:T(8,128)(2,1)S(1)} %get-tuple-element.32), channel_id=1, source_target_pairs={{8,16},{16,8},{9,17},{17,9},{10,18},{18,10},{11,19},{19,11},{12,20... | collective-permute-start | bytes 786440 | tf_op jit(solution)/shard_map/ppermute | solution.py:392
  6.5 0.0 copy-done
  6.5 4.7 %inner_state.1 = (bf16[4,128,1024]{2,1,0:T(8,128)(2,1)S(1)}, bf16[384,256]{1,0:T(8,128)(2,1)S(1)}, bf16[7680,256]{1,0:T(8,128)(2,1)S(1)}, bf16[4,5,16,1024]{3,2,1,0:T(8,128)(2,1)S(1)}, f32[4,1,128]{2,1,0:T(1,128)S(1)}) custom-call(f32[4]{0:T(128)S(1)} %copy-done, bf16[4,3,128,1024]{3,2,1,0:T(8,128)(2,1)S(1)} %get-tuple-element.25.planes_ref, ...), custom_call_target="tpu_custom_call" | custom-call | flops 1073741824 | bytes 10485760 | tf_op jit(solution)/shard_map/inner_state/pallas_call | solution.py:252
  11.2 0.0 collective-permute-done.core_ref
  11.2 0.0 collective-permute-done.1.far_ref
  11.2 3.7 %edge_state.1 = (bf16[4,5,16,640]{3,2,1,0:T(8,128)(2,1)S(1)}, bf16[4,5,16,640]{3,2,1,0:T(8,128)(2,1)S(1)}, bf16[2,5,16,384]{3,2,1,0:T(8,128)(2,1)S(1)}, bf16[2,5...) custom-call(bf16[4,3,128,1024]{3,2,1,0:T(8,128)(2,1)S(1)} %get-tuple-element.25, ...), custom_call_target="tpu_custom_call" | custom-call | tf_op jit(solution)/shard_map/edge_state/pallas_call | solution.py:317
  14.9 1.3 %collective-permute-start.2 = (bf16[4,5,16,640]{3,2,1,0:T(8,128)(2,1)S(1)}, bf16[4,5,16,640]{3,2,1,0:T(8,128)(2,1)S(1)}, u32[]{:S(2)}, u32[]{:S(2)}) collective-permute-start(bf16[4,5,16,640]{3,2,1,0:T(8,128)(2,1)S(1)} %get-tuple-element.34), channel_id=1, source_target_pairs={{0,1},{1,0},{2,3},{3,2},{4,5},{5,4},{6,7},{7,6},{8,9},{9,8},{10,11... | collective-permute-start | bytes 1228808 | tf_op jit(solution)/shard_map/ppermute | solution.py:378
  16.2 3.3 %collective-permute-start.6 = (bf16[2,5,16,384]{3,2,1,0:T(8,128)(2,1)S(1)}, bf16[2,5,16,384]{3,2,1,0:T(8,128)(2,1)S(1)}, u32[]{:S(2)}, u32[]{:S(2)}) collective-permute-start(bf16[2,5,16,384]{3,2,1,0:T(8,128)(2,1)S(1)} %get-tuple-element.40), channel_id=1, source_target_pairs={{0,6},{1,7},{2,4},{3,5},{4,2},{5,3},{6,0},{7,1},{8,14},{9,15},{10,... | collective-permute-start | bytes 368648 | tf_op jit(solution)/shard_map/ppermute | solution.py:378
  19.6 0.0 collective-permute-start.7
  19.6 0.3 collective-permute-start.8
  19.8 4.3 %collective-permute-done.2.refs_1_ = bf16[4,5,16,640]{3,2,1,0:T(8,128)(2,1)S(1)} collective-permute-done((bf16[4,5,16,640]{3,2,1,0:T(8,128)(2,1)S(1)}, bf16[4,5,16,640]{3,2,1,0:T(8,128)(2,1)S(1)}, u32[]{:S(2)}, u32[]{:S(2)}) %collective-permute-start.2) | collective-permute-done | bytes 409632 | tf_op jit(solution)/shard_map/ppermute | solution.py:378
  24.1 0.3 merge.2
  24.4 1.9 %collective-permute-start.3 = (bf16[5,16,640]{2,1,0:T(8,128)(2,1)S(1)}, bf16[5,16,640]{2,1,0:T(8,128)(2,1)S(1)}, u32[]{:S(2)}, u32[]{:S(2)}) collective-permute-start(bf16[5,16,640]{2,1,0:T(8,128)(2,1)S(1)} %get-tuple-element.36), channel_id=1, source_target_pairs={{0,2},{1,3},{2,0},{3,1},{4,6},{5,7},{6,4},{7,5},{8,10},{9,11},{10,... | collective-permute-start | bytes 307208 | tf_op jit(solution)/shard_map/ppermute | solution.py:378
  26.2 2.3 %collective-permute-start.4 = (bf16[5,16,640]{2,1,0:T(8,128)(2,1)S(1)}, bf16[5,16,640]{2,1,0:T(8,128)(2,1)S(1)}, u32[]{:S(2)}, u32[]{:S(2)}) collective-permute-start(bf16[5,16,640]{2,1,0:T(8,128)(2,1)S(1)} %get-tuple-element.37), channel_id=1, source_target_pairs={{0,4},{1,5},{2,6},{3,7},{4,0},{5,1},{6,2},{7,3},{8,12},{9,13},{10,... | collective-permute-start | bytes 307208 | tf_op jit(solution)/shard_map/ppermute | solution.py:378
  28.5 0.0 collective-permute-done.6.refs_1_
  28.5 0.0 collective-permute-start.5
  28.5 0.0 collective-permute-done.7.refs_2_
  28.5 0.2 collective-permute-done.8.refs_3_
  28.7 0.2 merge.3
  28.9 1.2 %collective-permute-start.9 = (bf16[5,16,384]{2,1,0:T(8,128)(2,1)S(1)}, bf16[5,16,384]{2,1,0:T(8,128)(2,1)S(1)}, u32[]{:S(2)}, u32[]{:S(2)}) collective-permute-start(bf16[5,16,384]{2,1,0:T(8,128)(2,1)S(1)} %get-tuple-element.44), channel_id=1, source_target_pairs={{0,1},{1,0},{2,3},{3,2},{4,5},{5,4},{6,7},{7,6},{8,9},{9,8},{10,11... | collective-permute-start | bytes 184328 | tf_op jit(solution)/shard_map/ppermute | solution.py:378
  30.0 2.7 %collective-permute-done.9.refs_5_ = bf16[5,16,384]{2,1,0:T(8,128)(2,1)S(1)} collective-permute-done((bf16[5,16,384]{2,1,0:T(8,128)(2,1)S(1)}, bf16[5,16,384]{2,1,0:T(8,128)(2,1)S(1)}, u32[]{:S(2)}, u32[]{:S(2)}) %collective-permute-start.9) | collective-permute-done | bytes 61472 | tf_op jit(solution)/shard_map/ppermute | solution.py:378
  32.8 0.0 collective-permute-done.3.refs_1_
  32.8 3.3 %collective-permute-done.4.refs_2_ = bf16[5,16,640]{2,1,0:T(8,128)(2,1)S(1)} collective-permute-done((bf16[5,16,640]{2,1,0:T(8,128)(2,1)S(1)}, bf16[5,16,640]{2,1,0:T(8,128)(2,1)S(1)}, u32[]{:S(2)}, u32[]{:S(2)}) %collective-permute-start.4) | collective-permute-done | bytes 102432 | tf_op jit(solution)/shard_map/ppermute | solution.py:378
  36.0 0.0 collective-permute-done.5.refs_3_
  36.0 0.8 %join.1 = bf16[3,16,1024]{2,1,0:T(8,128)(2,1)} custom-call(bf16[5,16,640]{2,1,0:T(8,128)(2,1)S(1)} %get-tuple-element.35.refs_0_, bf16[5,16,640]{2,1,0:T(8,128)(2,1)S(1)} %collective-permute-done.3.refs_1_, bf16[5,16,640]{2,1,0:T(8,128)(2,1)S(1)} %collective-permute-done.4.refs_2_, bf16[5,16,640]{2,1,0:T(8,128)(2,1)S(1)} %collective-permute-done.5.refs_3_, ...), custom_call_target="tpu_custom_call" | custom-call | tf_op jit(solution)/shard_map/join/pallas_call | solution.py:369
Async XLA Ops:
  0.0 6.5 %copy-start = (f32[4]{0:T(128)S(1)}, f32[4]{0:T(128)}, u32[]{:S(2)}) copy-start(f32[4]{0:T(128)} %gain_ref.1) | copy-start | bytes 52
  1.9 9.3 %collective-permute-start = (bf16[4,32,1024]{2,1,0:T(8,128)(2,1)S(1)}, bf16[4,32,1024]{2,1,0:T(8,128)(2,1)S(1)}, u32[]{:S(2)}, u32[]{:S(2)}) collective-permute-start(bf16[4,32,1024]{2,1,0:T(8,128)(2,1)S(1)} %get-tuple-element.31), channel_id=1, source_target_pairs={{0,8},{8,0},{16,24},{24,16},{1,9},{9,1},{17,25},{25,17},{2,10},{10... | collective-permute-start | bytes 786440 | tf_op jit(solution)/shard_map/ppermute | solution.py:390
  2.1 9.2 %collective-permute-start.1 = (bf16[4,32,1024]{2,1,0:T(8,128)(2,1)S(1)}, bf16[4,32,1024]{2,1,0:T(8,128)(2,1)S(1)}, u32[]{:S(2)}, u32[]{:S(2)}) collective-permute-start(bf16[4,32,1024]{2,1,0:T(8,128)(2,1)S(1)} %get-tuple-element.32), channel_id=1, source_target_pairs={{8,16},{16,8},{9,17},{17,9},{10,18},{18,10},{11,19},{19,11},{12,20... | collective-permute-start | bytes 786440 | tf_op jit(solution)/shard_map/ppermute | solution.py:392
  14.9 9.2 %collective-permute-start.2 = (bf16[4,5,16,640]{3,2,1,0:T(8,128)(2,1)S(1)}, bf16[4,5,16,640]{3,2,1,0:T(8,128)(2,1)S(1)}, u32[]{:S(2)}, u32[]{:S(2)}) collective-permute-start(bf16[4,5,16,640]{3,2,1,0:T(8,128)(2,1)S(1)} %get-tuple-element.34), channel_id=1, source_target_pairs={{0,1},{1,0},{2,3},{3,2},{4,5},{5,4},{6,7},{7,6},{8,9},{9,8},{10,11... | collective-permute-start | bytes 1228808 | tf_op jit(solution)/shard_map/ppermute | solution.py:378
  16.2 12.3 %collective-permute-start.6 = (bf16[2,5,16,384]{3,2,1,0:T(8,128)(2,1)S(1)}, bf16[2,5,16,384]{3,2,1,0:T(8,128)(2,1)S(1)}, u32[]{:S(2)}, u32[]{:S(2)}) collective-permute-start(bf16[2,5,16,384]{3,2,1,0:T(8,128)(2,1)S(1)} %get-tuple-element.40), channel_id=1, source_target_pairs={{0,6},{1,7},{2,4},{3,5},{4,2},{5,3},{6,0},{7,1},{8,14},{9,15},{10,... | collective-permute-start | bytes 368648 | tf_op jit(solution)/shard_map/ppermute | solution.py:378
  19.6 9.0 %collective-permute-start.7 = (bf16[2,5,16,384]{3,2,1,0:T(8,128)(2,1)S(1)}, bf16[2,5,16,384]{3,2,1,0:T(8,128)(2,1)S(1)}, u32[]{:S(2)}, u32[]{:S(2)}) collective-permute-start(bf16[2,5,16,384]{3,2,1,0:T(8,128)(2,1)S(1)} %get-tuple-element.41), channel_id=1, source_target_pairs={{0,2},{1,3},{2,0},{3,1},{4,6},{5,7},{6,4},{7,5},{8,10},{9,11},{10,... | collective-permute-start | bytes 368648 | tf_op jit(solution)/shard_map/ppermute | solution.py:378
  19.6 9.2 %collective-permute-start.8 = (bf16[2,5,16,384]{3,2,1,0:T(8,128)(2,1)S(1)}, bf16[2,5,16,384]{3,2,1,0:T(8,128)(2,1)S(1)}, u32[]{:S(2)}, u32[]{:S(2)}) collective-permute-start(bf16[2,5,16,384]{3,2,1,0:T(8,128)(2,1)S(1)} %get-tuple-element.42), channel_id=1, source_target_pairs={{0,4},{1,5},{2,6},{3,7},{4,0},{5,1},{6,2},{7,3},{8,12},{9,13},{10,... | collective-permute-start | bytes 368648 | tf_op jit(solution)/shard_map/ppermute | solution.py:378
  24.4 8.4 %collective-permute-start.3 = (bf16[5,16,640]{2,1,0:T(8,128)(2,1)S(1)}, bf16[5,16,640]{2,1,0:T(8,128)(2,1)S(1)}, u32[]{:S(2)}, u32[]{:S(2)}) collective-permute-start(bf16[5,16,640]{2,1,0:T(8,128)(2,1)S(1)} %get-tuple-element.36), channel_id=1, source_target_pairs={{0,2},{1,3},{2,0},{3,1},{4,6},{5,7},{6,4},{7,5},{8,10},{9,11},{10,... | collective-permute-start | bytes 307208 | tf_op jit(solution)/shard_map/ppermute | solution.py:378
  26.2 9.8 %collective-permute-start.4 = (bf16[5,16,640]{2,1,0:T(8,128)(2,1)S(1)}, bf16[5,16,640]{2,1,0:T(8,128)(2,1)S(1)}, u32[]{:S(2)}, u32[]{:S(2)}) collective-permute-start(bf16[5,16,640]{2,1,0:T(8,128)(2,1)S(1)} %get-tuple-element.37), channel_id=1, source_target_pairs={{0,4},{1,5},{2,6},{3,7},{4,0},{5,1},{6,2},{7,3},{8,12},{9,13},{10,... | collective-permute-start | bytes 307208 | tf_op jit(solution)/shard_map/ppermute | solution.py:378
  28.5 7.5 %collective-permute-start.5 = (bf16[5,16,640]{2,1,0:T(8,128)(2,1)S(1)}, bf16[5,16,640]{2,1,0:T(8,128)(2,1)S(1)}, u32[]{:S(2)}, u32[]{:S(2)}) collective-permute-start(bf16[5,16,640]{2,1,0:T(8,128)(2,1)S(1)} %get-tuple-element.38), channel_id=1, source_target_pairs={{0,6},{1,7},{2,4},{3,5},{4,2},{5,3},{6,0},{7,1},{8,14},{9,15},{10,... | collective-permute-start | bytes 307208 | tf_op jit(solution)/shard_map/ppermute | solution.py:378
  28.9 3.9 %collective-permute-start.9 = (bf16[5,16,384]{2,1,0:T(8,128)(2,1)S(1)}, bf16[5,16,384]{2,1,0:T(8,128)(2,1)S(1)}, u32[]{:S(2)}, u32[]{:S(2)}) collective-permute-start(bf16[5,16,384]{2,1,0:T(8,128)(2,1)S(1)} %get-tuple-element.44), channel_id=1, source_target_pairs={{0,1},{1,0},{2,3},{3,2},{4,5},{5,4},{6,7},{7,6},{8,9},{9,8},{10,11... | collective-permute-start | bytes 184328 | tf_op jit(solution)/shard_map/ppermute | solution.py:378

commit v8 on v7

--- a/solution.py
+++ b/solution.py
@@ -14,7 +14,7 @@
 LANES = 128
 WINDOW = 256
 STEP = 192
-FAR_FIRST = (3, 1, 2)
+FAR_FIRST = (3, 2, 1)
 
 
 def band_products(count):

time: 37 us -> 37 us (level)
  no operation moved by 1% of the time
where the time goes in v8:
time: 37 us; the launch traced here: 36.9 us
  starting transfers between devices  14.8 us (40%)
  Pallas kernels  11.4 us (31%)
  waiting for transfers between devices  10.5 us (28%)
    ppermute x8, waiting for transfers between devices, swap(): lax.ppermute(states[k], 'gz', [(i, i ^ k * step) for i in range(groups)])  10.5 us
    ppermute x8, starting transfers between devices, swap(): lax.ppermute(states[k], 'gz', [(i, i ^ k * step) for i in range(groups)])  10.3 us
    pallas_call x1, Pallas kernels, inner_state(): pl.pallas_call(inner_kernel, out_shape=[jax.ShapeDtypeStruct(shape, jnp.b...  4.67 us
    ppermute x1, starting transfers between devices, per_device(): lax.ppermute(to_far, 'tile', [(i, i + 1) for i in between] + [(i + 1, i)...  4.47 us
    pallas_call x1, Pallas kernels, edge_state(): pl.pallas_call(functools.partial(edge_state_kernel, slow), out_shape=[jax...  3.66 us
    pallas_call x1, Pallas kernels, fetch(): pl.pallas_call(fetch_kernel, out_shape=[jax.ShapeDtypeStruct(shape, jnp.b...  1.93 us
    pallas_call x1, Pallas kernels, join(): pl.pallas_call(functools.partial(join_kernel, [len(part) for part in part...  0.78 us
  transfers between devices with their start and end apart: 10, of which 4 were waited for; matrix products, arithmetic and copies ran while one was open for 0% of the time, Pallas kernels for 14%

profile of v8, /device:TPU:1, one launch (start us, length us, event | category | flops | bytes accessed | tf_op | source)
XLA Modules:
  0.0 36.9 jit_solution(2043188184608310503)
XLA Ops:
  0.0 0.0 copy-start
  0.0 1.9 %fetch.1 = (bf16[4,3,128,1024]{3,2,1,0:T(8,128)(2,1)S(1)}, bf16[4,32,1024]{2,1,0:T(8,128)(2,1)S(1)}, bf16[4,32,1024]{2,1,0:T(8,128)(2,1)S(1)}) custom-call(bf16[4,3,128,1024]{3,2,1,0:T(8,128)(2,1)} %planes_ref.1), custom_call_target="tpu_custom_call" | custom-call | flops 4294967296 | bytes 67108864 | tf_op jit(solution)/shard_map/fetch/pallas_call | solution.py:128
  1.9 0.1 collective-permute-start
  2.1 4.5 %collective-permute-start.1 = (bf16[4,32,1024]{2,1,0:T(8,128)(2,1)S(1)}, bf16[4,32,1024]{2,1,0:T(8,128)(2,1)S(1)}, u32[]{:S(2)}, u32[]{:S(2)}) collective-permute-start(bf16[4,32,1024]{2,1,0:T(8,128)(2,1)S(1)} %get-tuple-element.32), channel_id=1, source_target_pairs={{8,16},{16,8},{9,17},{17,9},{10,18},{18,10},{11,19},{19,11},{12,20... | collective-permute-start | bytes 786440 | tf_op jit(solution)/shard_map/ppermute | solution.py:392
  6.5 0.0 copy-done
  6.5 4.7 %inner_state.1 = (bf16[4,128,1024]{2,1,0:T(8,128)(2,1)S(1)}, bf16[384,256]{1,0:T(8,128)(2,1)S(1)}, bf16[7680,256]{1,0:T(8,128)(2,1)S(1)}, bf16[4,5,16,1024]{3,2,1,0:T(8,128)(2,1)S(1)}, f32[4,1,128]{2,1,0:T(1,128)S(1)}) custom-call(f32[4]{0:T(128)S(1)} %copy-done, bf16[4,3,128,1024]{3,2,1,0:T(8,128)(2,1)S(1)} %get-tuple-element.25.planes_ref, ...), custom_call_target="tpu_custom_call" | custom-call | flops 1073741824 | bytes 10485760 | tf_op jit(solution)/shard_map/inner_state/pallas_call | solution.py:252
  11.2 0.0 collective-permute-done.core_ref
  11.2 0.0 collective-permute-done.1.far_ref
  11.2 3.7 %edge_state.1 = (bf16[4,5,16,640]{3,2,1,0:T(8,128)(2,1)S(1)}, bf16[4,5,16,640]{3,2,1,0:T(8,128)(2,1)S(1)}, bf16[2,5,16,384]{3,2,1,0:T(8,128)(2,1)S(1)}, bf16[2,5...) custom-call(bf16[4,3,128,1024]{3,2,1,0:T(8,128)(2,1)S(1)} %get-tuple-element.25, ...), custom_call_target="tpu_custom_call" | custom-call | tf_op jit(solution)/shard_map/edge_state/pallas_call | solution.py:317
  14.9 1.3 %collective-permute-start.2 = (bf16[4,5,16,640]{3,2,1,0:T(8,128)(2,1)S(1)}, bf16[4,5,16,640]{3,2,1,0:T(8,128)(2,1)S(1)}, u32[]{:S(2)}, u32[]{:S(2)}) collective-permute-start(bf16[4,5,16,640]{3,2,1,0:T(8,128)(2,1)S(1)} %get-tuple-element.34), channel_id=1, source_target_pairs={{0,1},{1,0},{2,3},{3,2},{4,5},{5,4},{6,7},{7,6},{8,9},{9,8},{10,11... | collective-permute-start | bytes 1228808 | tf_op jit(solution)/shard_map/ppermute | solution.py:378
  16.2 3.3 %collective-permute-start.6 = (bf16[2,5,16,384]{3,2,1,0:T(8,128)(2,1)S(1)}, bf16[2,5,16,384]{3,2,1,0:T(8,128)(2,1)S(1)}, u32[]{:S(2)}, u32[]{:S(2)}) collective-permute-start(bf16[2,5,16,384]{3,2,1,0:T(8,128)(2,1)S(1)} %get-tuple-element.40), channel_id=1, source_target_pairs={{0,6},{1,7},{2,4},{3,5},{4,2},{5,3},{6,0},{7,1},{8,14},{9,15},{10,... | collective-permute-start | bytes 368648 | tf_op jit(solution)/shard_map/ppermute | solution.py:378
  19.6 0.0 collective-permute-start.7
  19.6 0.3 collective-permute-start.8
  19.8 4.3 %collective-permute-done.2.refs_1_ = bf16[4,5,16,640]{3,2,1,0:T(8,128)(2,1)S(1)} collective-permute-done((bf16[4,5,16,640]{3,2,1,0:T(8,128)(2,1)S(1)}, bf16[4,5,16,640]{3,2,1,0:T(8,128)(2,1)S(1)}, u32[]{:S(2)}, u32[]{:S(2)}) %collective-permute-start.2) | collective-permute-done | bytes 409632 | tf_op jit(solution)/shard_map/ppermute | solution.py:378
  24.1 0.3 merge.2
  24.4 1.9 %collective-permute-start.3 = (bf16[5,16,640]{2,1,0:T(8,128)(2,1)S(1)}, bf16[5,16,640]{2,1,0:T(8,128)(2,1)S(1)}, u32[]{:S(2)}, u32[]{:S(2)}) collective-permute-start(bf16[5,16,640]{2,1,0:T(8,128)(2,1)S(1)} %get-tuple-element.36), channel_id=1, source_target_pairs={{0,2},{1,3},{2,0},{3,1},{4,6},{5,7},{6,4},{7,5},{8,10},{9,11},{10,... | collective-permute-start | bytes 307208 | tf_op jit(solution)/shard_map/ppermute | solution.py:378
  26.2 2.3 %collective-permute-start.4 = (bf16[5,16,640]{2,1,0:T(8,128)(2,1)S(1)}, bf16[5,16,640]{2,1,0:T(8,128)(2,1)S(1)}, u32[]{:S(2)}, u32[]{:S(2)}) collective-permute-start(bf16[5,16,640]{2,1,0:T(8,128)(2,1)S(1)} %get-tuple-element.37), channel_id=1, source_target_pairs={{0,4},{1,5},{2,6},{3,7},{4,0},{5,1},{6,2},{7,3},{8,12},{9,13},{10,... | collective-permute-start | bytes 307208 | tf_op jit(solution)/shard_map/ppermute | solution.py:378
  28.5 0.0 collective-permute-done.6.refs_1_
  28.5 0.0 collective-permute-start.5
  28.5 0.2 collective-permute-done.7.refs_2_
  28.7 0.0 collective-permute-done.8.refs_3_
  28.7 0.2 merge.3
  28.9 1.2 %collective-permute-start.9 = (bf16[5,16,384]{2,1,0:T(8,128)(2,1)S(1)}, bf16[5,16,384]{2,1,0:T(8,128)(2,1)S(1)}, u32[]{:S(2)}, u32[]{:S(2)}) collective-permute-start(bf16[5,16,384]{2,1,0:T(8,128)(2,1)S(1)} %get-tuple-element.44), channel_id=1, source_target_pairs={{0,1},{1,0},{2,3},{3,2},{4,5},{5,4},{6,7},{7,6},{8,9},{9,8},{10,11... | collective-permute-start | bytes 184328 | tf_op jit(solution)/shard_map/ppermute | solution.py:378
  30.0 2.7 %collective-permute-done.9.refs_5_ = bf16[5,16,384]{2,1,0:T(8,128)(2,1)S(1)} collective-permute-done((bf16[5,16,384]{2,1,0:T(8,128)(2,1)S(1)}, bf16[5,16,384]{2,1,0:T(8,128)(2,1)S(1)}, u32[]{:S(2)}, u32[]{:S(2)}) %collective-permute-start.9) | collective-permute-done | bytes 61472 | tf_op jit(solution)/shard_map/ppermute | solution.py:378
  32.8 0.0 collective-permute-done.3.refs_1_
  32.8 3.3 %collective-permute-done.4.refs_2_ = bf16[5,16,640]{2,1,0:T(8,128)(2,1)S(1)} collective-permute-done((bf16[5,16,640]{2,1,0:T(8,128)(2,1)S(1)}, bf16[5,16,640]{2,1,0:T(8,128)(2,1)S(1)}, u32[]{:S(2)}, u32[]{:S(2)}) %collective-permute-start.4) | collective-permute-done | bytes 102432 | tf_op jit(solution)/shard_map/ppermute | solution.py:378
  36.1 0.0 collective-permute-done.5.refs_3_
  36.1 0.8 %join.1 = bf16[3,16,1024]{2,1,0:T(8,128)(2,1)} custom-call(bf16[5,16,640]{2,1,0:T(8,128)(2,1)S(1)} %get-tuple-element.35.refs_0_, bf16[5,16,640]{2,1,0:T(8,128)(2,1)S(1)} %collective-permute-done.3.refs_1_, bf16[5,16,640]{2,1,0:T(8,128)(2,1)S(1)} %collective-permute-done.4.refs_2_, bf16[5,16,640]{2,1,0:T(8,128)(2,1)S(1)} %collective-permute-done.5.refs_3_, ...), custom_call_target="tpu_custom_call" | custom-call | tf_op jit(solution)/shard_map/join/pallas_call | solution.py:369
Async XLA Ops:
  0.0 6.5 %copy-start = (f32[4]{0:T(128)S(1)}, f32[4]{0:T(128)}, u32[]{:S(2)}) copy-start(f32[4]{0:T(128)} %gain_ref.1) | copy-start | bytes 52
  1.9 9.3 %collective-permute-start = (bf16[4,32,1024]{2,1,0:T(8,128)(2,1)S(1)}, bf16[4,32,1024]{2,1,0:T(8,128)(2,1)S(1)}, u32[]{:S(2)}, u32[]{:S(2)}) collective-permute-start(bf16[4,32,1024]{2,1,0:T(8,128)(2,1)S(1)} %get-tuple-element.31), channel_id=1, source_target_pairs={{0,8},{8,0},{16,24},{24,16},{1,9},{9,1},{17,25},{25,17},{2,10},{10... | collective-permute-start | bytes 786440 | tf_op jit(solution)/shard_map/ppermute | solution.py:390
  2.1 9.2 %collective-permute-start.1 = (bf16[4,32,1024]{2,1,0:T(8,128)(2,1)S(1)}, bf16[4,32,1024]{2,1,0:T(8,128)(2,1)S(1)}, u32[]{:S(2)}, u32[]{:S(2)}) collective-permute-start(bf16[4,32,1024]{2,1,0:T(8,128)(2,1)S(1)} %get-tuple-element.32), channel_id=1, source_target_pairs={{8,16},{16,8},{9,17},{17,9},{10,18},{18,10},{11,19},{19,11},{12,20... | collective-permute-start | bytes 786440 | tf_op jit(solution)/shard_map/ppermute | solution.py:392
  14.9 9.2 %collective-permute-start.2 = (bf16[4,5,16,640]{3,2,1,0:T(8,128)(2,1)S(1)}, bf16[4,5,16,640]{3,2,1,0:T(8,128)(2,1)S(1)}, u32[]{:S(2)}, u32[]{:S(2)}) collective-permute-start(bf16[4,5,16,640]{3,2,1,0:T(8,128)(2,1)S(1)} %get-tuple-element.34), channel_id=1, source_target_pairs={{0,1},{1,0},{2,3},{3,2},{4,5},{5,4},{6,7},{7,6},{8,9},{9,8},{10,11... | collective-permute-start | bytes 1228808 | tf_op jit(solution)/shard_map/ppermute | solution.py:378
  16.2 12.3 %collective-permute-start.6 = (bf16[2,5,16,384]{3,2,1,0:T(8,128)(2,1)S(1)}, bf16[2,5,16,384]{3,2,1,0:T(8,128)(2,1)S(1)}, u32[]{:S(2)}, u32[]{:S(2)}) collective-permute-start(bf16[2,5,16,384]{3,2,1,0:T(8,128)(2,1)S(1)} %get-tuple-element.40), channel_id=1, source_target_pairs={{0,6},{1,7},{2,4},{3,5},{4,2},{5,3},{6,0},{7,1},{8,14},{9,15},{10,... | collective-permute-start | bytes 368648 | tf_op jit(solution)/shard_map/ppermute | solution.py:378
  19.6 9.2 %collective-permute-start.7 = (bf16[2,5,16,384]{3,2,1,0:T(8,128)(2,1)S(1)}, bf16[2,5,16,384]{3,2,1,0:T(8,128)(2,1)S(1)}, u32[]{:S(2)}, u32[]{:S(2)}) collective-permute-start(bf16[2,5,16,384]{3,2,1,0:T(8,128)(2,1)S(1)} %get-tuple-element.41), channel_id=1, source_target_pairs={{0,4},{1,5},{2,6},{3,7},{4,0},{5,1},{6,2},{7,3},{8,12},{9,13},{10,... | collective-permute-start | bytes 368648 | tf_op jit(solution)/shard_map/ppermute | solution.py:378
  19.6 9.2 %collective-permute-start.8 = (bf16[2,5,16,384]{3,2,1,0:T(8,128)(2,1)S(1)}, bf16[2,5,16,384]{3,2,1,0:T(8,128)(2,1)S(1)}, u32[]{:S(2)}, u32[]{:S(2)}) collective-permute-start(bf16[2,5,16,384]{3,2,1,0:T(8,128)(2,1)S(1)} %get-tuple-element.42), channel_id=1, source_target_pairs={{0,2},{1,3},{2,0},{3,1},{4,6},{5,7},{6,4},{7,5},{8,10},{9,11},{10,... | collective-permute-start | bytes 368648 | tf_op jit(solution)/shard_map/ppermute | solution.py:378
  24.4 8.4 %collective-permute-start.3 = (bf16[5,16,640]{2,1,0:T(8,128)(2,1)S(1)}, bf16[5,16,640]{2,1,0:T(8,128)(2,1)S(1)}, u32[]{:S(2)}, u32[]{:S(2)}) collective-permute-start(bf16[5,16,640]{2,1,0:T(8,128)(2,1)S(1)} %get-tuple-element.36), channel_id=1, source_target_pairs={{0,2},{1,3},{2,0},{3,1},{4,6},{5,7},{6,4},{7,5},{8,10},{9,11},{10,... | collective-permute-start | bytes 307208 | tf_op jit(solution)/shard_map/ppermute | solution.py:378
  26.2 9.9 %collective-permute-start.4 = (bf16[5,16,640]{2,1,0:T(8,128)(2,1)S(1)}, bf16[5,16,640]{2,1,0:T(8,128)(2,1)S(1)}, u32[]{:S(2)}, u32[]{:S(2)}) collective-permute-start(bf16[5,16,640]{2,1,0:T(8,128)(2,1)S(1)} %get-tuple-element.37), channel_id=1, source_target_pairs={{0,4},{1,5},{2,6},{3,7},{4,0},{5,1},{6,2},{7,3},{8,12},{9,13},{10,... | collective-permute-start | bytes 307208 | tf_op jit(solution)/shard_map/ppermute | solution.py:378
  28.5 7.6 %collective-permute-start.5 = (bf16[5,16,640]{2,1,0:T(8,128)(2,1)S(1)}, bf16[5,16,640]{2,1,0:T(8,128)(2,1)S(1)}, u32[]{:S(2)}, u32[]{:S(2)}) collective-permute-start(bf16[5,16,640]{2,1,0:T(8,128)(2,1)S(1)} %get-tuple-element.38), channel_id=1, source_target_pairs={{0,6},{1,7},{2,4},{3,5},{4,2},{5,3},{6,0},{7,1},{8,14},{9,15},{10,... | collective-permute-start | bytes 307208 | tf_op jit(solution)/shard_map/ppermute | solution.py:378
  28.9 3.9 %collective-permute-start.9 = (bf16[5,16,384]{2,1,0:T(8,128)(2,1)S(1)}, bf16[5,16,384]{2,1,0:T(8,128)(2,1)S(1)}, u32[]{:S(2)}, u32[]{:S(2)}) collective-permute-start(bf16[5,16,384]{2,1,0:T(8,128)(2,1)S(1)} %get-tuple-element.44), channel_id=1, source_target_pairs={{0,1},{1,0},{2,3},{3,2},{4,5},{5,4},{6,7},{7,6},{8,9},{9,8},{10,11... | collective-permute-start | bytes 184328 | tf_op jit(solution)/shard_map/ppermute | solution.py:378
